TPU v7x, 32 devices: a whole 2x2x4 slice. The times are simulated.
32 devices in a mesh: req: 8 (over y, x, core), head: 4 (over z).
Axes of the slice: x: 2, y: 2, z: 4, core: 2. Of those that a mesh axis runs over, the one named last changes fastest.
Arguments:
- hidden_in: bfloat16 [2048, 4096], P('req', 'head'), may hold values from -6 to 6
- norm_gain: float32 [4096], replicated, may hold values from 0.25 to 1.75
- norm_shift: float32 [4096], replicated, may hold values from -3 to 3
- attend_weight: bfloat16 [4096, 3, 2048], P(None, None, 'head'), may hold values from -0.09375 to 0.09375
- output_weight: bfloat16 [2048, 4096], P('head'), may hold values from -0.125 to 0.125
- up_weight: bfloat16 [4096, 8192], P('req', 'head'), may hold values from -0.09375 to 0.09375
- up_bias: float32 [8192], P('head'), may hold values from -3 to 3
- down_weight: bfloat16 [8192, 4096], P('head', 'req'), may hold values from -0.0625 to 0.0625
- down_bias: float32 [4096], P('head'), may hold values from -3 to 3
- key_cache: bfloat16 [16, 1536, 2048], P('req', None, 'head'), may hold values from -160 to 160
- value_cache: bfloat16 [16, 1536, 2048], P('req', None, 'head'), may hold values from -5 to 5
- cached_len: int32 [16], P('req'), may hold values from 1 to 1536, as said below
Outputs:
- hidden_out: bfloat16 [2048, 4096], P('req', 'head')
- new_keys: bfloat16 [16, 128, 2048], P('req', None, 'head')
- new_values: bfloat16 [16, 128, 2048], P('req', None, 'head')
Inputs may be any that keep to these rules, and one draw needn't show every extreme that they name: `cached_len`: each cached length is under 64 or between 768 and 1536; some request has exactly 1536.
All inputs are finite; a program needn't handle non-finite values.
Results may differ from a plain program's by a relative error of at most 0.012.
Values may be sent and summed in bfloat16 or wider, within the bound.
No kernel may reach another device: no remote copies, remote signals or barrier semaphores. Data moves between devices by JAX's collectives and lax.ppermute only.
A program may use at most 128 MiB of HBM per device.

v0:
```python
import jax
import jax.numpy as jnp
from jax import lax
from jax.sharding import PartitionSpec as P

HD = 256
ROT = 64
GROUP = 128
BLOCK = 128


epsilon = 1e-05
very_low = -1e30


def layer_norm(values, gain_vec, shift_vec):
    floats = values.astype(jnp.float32)
    center = floats - jnp.mean(floats, axis=-1, keepdims=True)
    spread = jnp.mean(center * center, axis=-1, keepdims=True)
    return center * lax.rsqrt(spread + epsilon) * gain_vec + shift_vec


def rotate_pairs(tensor, positions):
    halves = ROT // 2
    frequency = 10000.0 ** (-(jnp.arange(halves, dtype=jnp.float32) * 2.0) / ROT)
    angles = positions.astype(jnp.float32)[:, :, None] * frequency
    cosine = jnp.cos(angles)[:, :, None, :]
    sine_part = jnp.sin(angles)[:, :, None, :]
    rotary = tensor[..., :ROT]
    even_part = rotary[..., 0::2]
    odd_part = rotary[..., 1::2]
    rotated = jnp.stack(
        [even_part * cosine - odd_part * sine_part, odd_part * cosine + even_part * sine_part],
        axis=-1,
    )
    return jnp.concatenate([rotated.reshape(rotary.shape), tensor[..., ROT:]], axis=-1)


def block_part(query_rows, key_rows, value_rows, lengths, offset):
    batch_size, group_len, head_count, head_size = query_rows.shape
    span_len = key_rows.shape[1]
    keys_four = key_rows.reshape(batch_size, span_len, head_count, head_size)
    values_four = value_rows.reshape(batch_size, span_len, head_count, head_size)
    score_scale = head_size ** (-0.5)
    live_len = jnp.clip(jnp.max(lengths) - offset, 0, span_len)
    steps_count = (live_len + BLOCK - 1) // BLOCK
    start_state = (
        jnp.full((batch_size, head_count, group_len), very_low, jnp.float32),
        jnp.zeros((batch_size, head_count, group_len), jnp.float32),
        jnp.zeros((batch_size, head_count, group_len, head_size), jnp.float32),
    )

    def visit(block_index, carry_state):
        top_score, weight_sum, weighted = carry_state
        block_start = block_index * BLOCK
        key_block = lax.dynamic_slice_in_dim(keys_four, block_start, BLOCK, 1)
        value_block = lax.dynamic_slice_in_dim(values_four, block_start, BLOCK, 1)
        scores = (
            jnp.einsum("rchd,rkhd->rhck", query_rows, key_block, preferred_element_type=jnp.float32)
            * score_scale
        )
        slot_place = offset + block_start + jnp.arange(BLOCK, dtype=jnp.int32)
        visible = (slot_place[None, :] < lengths[:, None])[:, None, None, :]
        scores = jnp.where(visible, scores, very_low)
        new_top = jnp.maximum(top_score, jnp.max(scores, axis=-1))
        rescale = jnp.exp(top_score - new_top)
        weights = jnp.where(visible, jnp.exp(scores - new_top[..., None]), 0.0)
        weight_sum = weight_sum * rescale + jnp.sum(weights, axis=-1)
        weighted = weighted * rescale[..., None] + jnp.einsum(
            "rhck,rkhd->rhcd",
            weights.astype(jnp.bfloat16),
            value_block,
            preferred_element_type=jnp.float32,
        )
        return (new_top, weight_sum, weighted)

    return lax.fori_loop(0, steps_count, visit, start_state)


def group_part(query_rows, key_rows, value_rows):
    group_len = query_rows.shape[1]
    score_scale = query_rows.shape[3] ** (-0.5)
    scores = (
        jnp.einsum("rchd,rkhd->rhck", query_rows, key_rows, preferred_element_type=jnp.float32)
        * score_scale
    )
    causal = jnp.arange(group_len)[:, None] >= jnp.arange(group_len)[None, :]
    scores = jnp.where(causal, scores, very_low)
    top_score = jnp.max(scores, axis=-1)
    weights = jnp.exp(scores - top_score[..., None])
    weighted = jnp.einsum(
        "rhck,rkhd->rhcd",
        weights.astype(jnp.bfloat16),
        value_rows,
        preferred_element_type=jnp.float32,
    )
    return (top_score, jnp.sum(weights, axis=-1), weighted)


def merge_parts(first_part, second_part):
    top_score = jnp.maximum(first_part[0], second_part[0])
    first_scale = jnp.exp(first_part[0] - top_score)
    second_scale = jnp.exp(second_part[0] - top_score)
    weight_sum = first_part[1] * first_scale + second_part[1] * second_scale
    weighted = first_part[2] * first_scale[..., None] + second_part[2] * second_scale[..., None]
    return (top_score, weight_sum, weighted)


def body(
    hidden_in,
    norm_gain,
    norm_shift,
    attend_weight,
    output_weight,
    up_weight,
    up_bias,
    down_weight,
    down_bias,
    key_cache,
    value_cache,
    cached_len,
):
    gathered = lax.all_gather(hidden_in, "head", axis=1, tiled=True)
    normed = layer_norm(gathered, norm_gain, norm_shift).astype(jnp.bfloat16)
    model_width = gathered.shape[1]
    batch_size = key_cache.shape[0]
    local_width = output_weight.shape[0]
    head_count = local_width // HD
    projected = jnp.dot(
        normed,
        attend_weight.reshape(model_width, 3 * local_width),
        preferred_element_type=jnp.float32,
    )
    projected = projected.reshape(batch_size, GROUP, 3, head_count, HD)
    positions = cached_len[:, None] + jnp.arange(GROUP, dtype=jnp.int32)[None, :]
    query_rows = rotate_pairs(projected[:, :, 0], positions).astype(jnp.bfloat16)
    key_rows = rotate_pairs(projected[:, :, 1], positions).astype(jnp.bfloat16)
    value_rows = projected[:, :, 2].astype(jnp.bfloat16)
    group_state = group_part(query_rows, key_rows, value_rows)
    cached = block_part(query_rows, key_cache, value_cache, cached_len, 0)
    top_score, weight_sum, weighted = merge_parts(group_state, cached)
    context = (
        (weighted / weight_sum[..., None])
        .transpose(0, 2, 1, 3)
        .reshape(batch_size * GROUP, local_width)
        .astype(jnp.bfloat16)
    )
    attended = jnp.dot(context, output_weight, preferred_element_type=jnp.float32)
    upward = jnp.dot(
        normed,
        lax.all_gather(up_weight, "req", axis=0, tiled=True),
        preferred_element_type=jnp.float32,
    )
    active = jax.nn.gelu(upward + up_bias, approximate=True).astype(jnp.bfloat16)
    downward = jnp.dot(
        active,
        lax.all_gather(down_weight, "req", axis=1, tiled=True),
        preferred_element_type=jnp.float32,
    )
    summed = lax.psum_scatter(
        (attended + downward).astype(jnp.bfloat16), "head", scatter_dimension=1, tiled=True
    ).astype(jnp.float32)
    hidden_out = (hidden_in.astype(jnp.float32) + summed + down_bias).astype(jnp.bfloat16)
    new_keys = key_rows.reshape(batch_size, GROUP, local_width)
    new_values = value_rows.reshape(batch_size, GROUP, local_width)
    return (hidden_out, new_keys, new_values)


def solution(mesh):
    placed = (
        P("req", "head"),
        P(),
        P(),
        P(None, None, "head"),
        P("head", None),
        P("req", "head"),
        P("head"),
        P("head", "req"),
        P("head"),
        P("req", None, "head"),
        P("req", None, "head"),
        P("req"),
    )
    return jax.shard_map(
        body,
        mesh=mesh,
        in_specs=placed,
        out_specs=(P("req", "head"), P("req", None, "head"), P("req", None, "head")),
        check_vma=False,
    )
```

profile of v0, /device:TPU:0, one launch (start us, length us, event | category | flops | bytes accessed | tf_op | source)
XLA Modules:
  0.0 319.9 jit_solution(5650358955540083121)
XLA Ops:
  10.8 2.8 copy.65
  13.6 17.2 %copy.58 = bf16[4096,3,512]{0,2,1:T(8,128)(2,1)} copy(bf16[4096,3,512]{2,0,1:T(8,128)(2,1)} %param.17) | data formatting | bytes 25165824 | tf_op args[3]
  30.8 2.9 copy.66
  34.3 24.0 %all-gather.4.cloned.1.call-done = bf16[256,4096]{1,0:T(8,128)(2,1)} async-done(((bf16[256,1024]{1,0:T(8,128)(2,1)}), bf16[256,4096]{1,0:T(8,128)(2,1)}) %all-gather.4.cloned.1.call-update) | async-done | bytes 2097168 | tf_op jit(solution)/shard_map/all_gather | solution.py:123
  58.3 2.1 convert_reduce_fusion
  62.2 7.4 %fusion.52 = f32[2,128,3,2,256]{4,1,3,2,0:T(8,128)S(1)} fusion(bf16[2,128,4096,1,1]{2,1,4,3,0:T(8,128)(2,1)S(1)} %bitcast.57, bf16[3,2,256,4096,1]{3,2,1,0,4:T(8,128)(2,1)} %bitcast.54), kind=kOutput, calls=%fused_computation.86 | convolution fusion | flops 3221225472 | bytes 16252928 | tf_op jit(solution)/shard_map/dot_general | solution.py:129
  71.0 3.0 slice.42
  74.0 2.9 slice.41
  77.8 2.4 slice.37
  80.2 2.9 slice.36
  88.0 32.1 %while.14 = (s32[]{:T(128)}, f32[2,2,128]{2,1,0:T(2,128)S(1)}, f32[2,2,128]{2,1,0:T(2,128)S(1)}, f32[2,2,128,256]{3,2,1,0:T(8,128)S(1)}, s32[]{:T(128)}, /*index...) while((s32[]{:T(128)}, f32[2,2,128]{2,1,0:T(2,128)S(1)}, ...), condition=%wide.region_7.8_spmd, body=%wide.region_4.7_spmd.sunk | while | flops 67962240 | bytes 2656455 | solution.py:77
  90.2 1.4 convolution_add_fusion.4
  93.7 1.4 convolution_add_fusion.4
  100.9 1.4 convolution_add_fusion.4
  104.4 1.4 convolution_add_fusion.4
  108.0 1.4 convolution_add_fusion.4
  115.1 1.4 convolution_add_fusion.4
  120.2 1.4 fusion.32
  121.9 30.1 %all-gather.8.cloned.1.call-done = bf16[2048,4096]{1,0:T(8,128)(2,1)} async-done(((bf16[2048,512]{1,0:T(8,128)(2,1)}), bf16[2048,4096]{1,0:T(8,128)(2,1)}) %all-gather.8.cloned.1.call-update) | async-done | bytes 16777232 | tf_op jit(solution)/shard_map/all_gather | solution.py:157
  152.0 91.8 %all-gather.6.cloned.1.call-done = bf16[4096,2048]{1,0:T(8,128)(2,1)} async-done(((bf16[512,2048]{1,0:T(8,128)(2,1)}), bf16[4096,2048]{1,0:T(8,128)(2,1)}) %all-gather.6.cloned.1.call-update) | async-done | bytes 16777232 | tf_op jit(solution)/shard_map/all_gather | solution.py:151
  243.8 17.4 %fusion.33 = f32[256,4096]{1,0:T(8,128)} fusion(bf16[2048,4096]{1,0:T(8,128)(2,1)} %all-gather.8.cloned.1.call-done, bf16[256,4096]{1,0:T(8,128)(2,1)S(1)} %fusion.19, bf16[4096,2048]{1,0:T(8,128)(2,1)} %all-gather.6.cloned.1.call-done, f32[2048]{0:T(1024)S(1)} %copy-done.9), kind=kOutput, calls=%fused_computation.47 | convolution fusion | flops 8595177472 | bytes 39854080 | tf_op jit(solution)/shard_map/dot_general | solution.py:155
  261.2 6.1 %fusion.13 = bf16[256,4096]{1,0:T(8,128)(2,1)} fusion(f32[256,4096]{1,0:T(8,128)} %fusion.33, bf16[256,512]{1,0:T(8,128)(2,1)S(1)} %bitcast.61, bf16[512,4096]{1,0:T(8,128)(2,1)} %param.18), kind=kOutput, calls=%fused_computation.22 | convolution fusion | flops 1075838976 | bytes 10747904 | tf_op jit(solution)/shard_map/dot_general | solution.py:148
  270.4 40.9 %reduce-scatter.2.cloned.1.call-done = bf16[256,1024]{1,0:T(8,128)(2,1)} async-done(((bf16[256,4096]{1,0:T(8,128)(2,1)}), bf16[256,1024]{1,0:T(8,128)(2,1)}) %reduce-scatter.2.cloned.1.call-update) | async-done | bytes 524304 | tf_op jit(solution)/shard_map/reduce_scatter | solution.py:160
  311.3 2.0 add_convert_fusion
  (132 shorter events, 39.1 us)
Async XLA Ops:
  7.2 2.3 copy-start.10
  7.2 3.6 %copy-start.1 = (bf16[2,1536,512]{2,1,0:T(8,128)(2,1)S(1)}, bf16[2,1536,512]{2,1,0:T(8,128)(2,1)}, u32[]{:S(2)}) copy-start(bf16[2,1536,512]{2,1,0:T(8,128)(2,1)} %param.23) | copy-start | bytes 9437188
  7.2 51.1 %all-gather.4.cloned.1.call-start = ((), (), s32[]{:S(2)}) async-start(), calls=%async_computation.1 | async-start | bytes 2621440 | tf_op jit(solution)/shard_map/all_gather | solution.py:123
  7.9 144.1 %all-gather.8.cloned.1.call-start = ((), (), s32[]{:S(2)}) async-start(), calls=%async_computation.3 | async-start | bytes 18874368 | tf_op jit(solution)/shard_map/all_gather | solution.py:157
  8.7 235.1 %all-gather.6.cloned.1.call-start = ((), (), s32[]{:S(2)}) async-start(), calls=%async_computation.2 | async-start | bytes 18874368 | tf_op jit(solution)/shard_map/all_gather | solution.py:151
  9.4 301.9 %reduce-scatter.2.cloned.1.call-start = ((), (), s32[]{:S(2)}) async-start(), calls=%async_computation.4 | async-start | bytes 2621440 | tf_op jit(solution)/shard_map/reduce_scatter | solution.py:160
  13.6 17.2 %copy-start.2 = (bf16[2,1536,512]{2,1,0:T(8,128)(2,1)S(1)}, bf16[2,1536,512]{2,1,0:T(8,128)(2,1)}, u32[]{:S(2)}) copy-start(bf16[2,1536,512]{2,1,0:T(8,128)(2,1)} %param.24) | copy-start | bytes 9437188
  33.6 27.5 %copy-start.6 = (f32[4096]{0:T(1024)S(1)}, f32[4096]{0:T(1024)}, u32[]{:S(2)}) copy-start(f32[4096]{0:T(1024)} %param.16) | copy-start | bytes 49156
  33.6 27.5 %copy-start.7 = (f32[4096]{0:T(1024)S(1)}, f32[4096]{0:T(1024)}, u32[]{:S(2)}) copy-start(f32[4096]{0:T(1024)} %param.15) | copy-start | bytes 49156
  58.3 2.2 copy-start
  69.7 1.1 copy-start.4
  77.8 9.6 %copy-start.5 = (bf16[2,128,2,192]{3,1,2,0:T(8,128)(2,1)S(1)}, bf16[2,128,2,192]{3,1,2,0:T(8,128)(2,1)}, u32[]{:S(2)}) copy-start(bf16[2,128,2,192]{3,1,2,0:T(8,128)(2,1)} %slice.57) | copy-start | bytes 589828
  120.2 123.6 %copy-start.9 = (f32[2048]{0:T(1024)S(1)}, f32[2048]{0:T(1024)}, u32[]{:S(2)}) copy-start(f32[2048]{0:T(1024)} %param.20) | copy-start | bytes 24580
  267.3 44.0 %copy-start.3 = (bf16[256,1024]{1,0:T(8,128)(2,1)S(1)}, bf16[256,1024]{1,0:T(8,128)(2,1)}, u32[]{:S(2)}) copy-start(bf16[256,1024]{1,0:T(8,128)(2,1)} %param.14) | copy-start | bytes 1572868
  267.3 44.0 %copy-start.8 = (f32[1024]{0:T(1024)S(1)}, f32[1024]{0:T(1024)}, u32[]{:S(2)}) copy-start(f32[1024]{0:T(1024)} %param.22) | copy-start | bytes 12292
Sparse Core Ops, SparseCore 0:
  9.6 48.6 all-gather.3
  60.1 91.8 all-gather.7
  153.9 89.8 all-gather.5
  267.4 43.8 reduce-scatter.1
where the time goes:
time: 321 us; the launch traced here: 320 us
  waiting for transfers between devices  189 us (59%)
  matrix products  56.2 us (18%)
  local copies, waits for them, and re-layouts  41.8 us (13%)
  other arithmetic  17.6 us (5%)
  between operations  14.7 us (5%)
    all_gather x1, waiting for transfers between devices, body(): lax.all_gather(up_weight, 'req', axis=0, tiled=True)  91.8 us
    reduce_scatter x1, waiting for transfers between devices, body(): lax.psum_scatter((attended + downward).astype(jnp.bfloat16), 'head', scat...  40.9 us
    all_gather x1, waiting for transfers between devices, body(): lax.all_gather(down_weight, 'req', axis=1, tiled=True)  30.1 us
    unnamed x28, local copies, waits for them, and re-layouts  25.8 us
    all_gather x1, waiting for transfers between devices, body(): gathered = lax.all_gather(hidden_in, 'head', axis=1, tiled=True)  24 us
    dot_general x1, matrix products, body(): jnp.dot(active, lax.all_gather(down_weight, 'req', axis=1, tiled=True), p...  17.4 us
    dot_general x9, matrix products, visit(): jnp.einsum('rhck,rkhd->rhcd', weights.astype(jnp.bfloat16), value_block,...  12.4 us
    dot_general x9, matrix products, visit(): jnp.einsum('rchd,rkhd->rhck', query_rows, key_block, preferred_element_ty...  11.3 us
  transfers between devices with their start and end apart: 4, of which 4 were waited for; matrix products, arithmetic and copies ran while one was open for 28% of the time, Pallas kernels for 0%

commit v1 on v0

v1 whole, which is shorter than its diff:
```python
import functools

import jax
import jax.numpy as jnp
from jax import lax
from jax.experimental import pallas as pl
from jax.experimental.pallas import tpu as pltpu
from jax.sharding import PartitionSpec as P

HD = 256
ROT = 64
GROUP = 128
BLOCK = 128
LANES = 128


epsilon = 1e-05
very_low = -1e30
f32 = jnp.float32
bf16 = jnp.bfloat16


def params(mib):
    return pltpu.CompilerParams(vmem_limit_bytes=mib * 1024 * 1024)


def cost():
    return pl.CostEstimate(flops=1024, bytes_accessed=1024, transcendentals=0)


def norm_kernel(count, split, order_ref, *refs):
    *pieces, affine_ref, out_ref = refs[: len(refs) - split]
    sent = refs[len(refs) - split :]
    total = out_ref.shape[1]
    width = total // count
    floats = [
        piece[:, start : start + width].astype(f32)
        for piece in pieces
        for start in range(0, piece.shape[1], width)
    ]
    mean = sum(jnp.sum(part, axis=-1, keepdims=True) for part in floats) / total
    floats = [part - mean for part in floats]
    spread = sum(jnp.sum(part * part, axis=-1, keepdims=True) for part in floats) / total
    inverse = lax.rsqrt(spread + epsilon)
    for k, part in enumerate(floats):
        columns = pl.ds(pl.multiple_of(order_ref[k] * width, width), width)
        out_ref[:, columns] = (
            part * inverse * affine_ref[:1, columns] + affine_ref[1:, columns]
        ).astype(bf16)
    if split:
        half = total // 2
        sent[0][...] = out_ref[:, pl.ds(pl.multiple_of(order_ref[count] * half, half), half)]


def norm_call(order, count, pieces, affine, split=False):
    rows = pieces[0].shape[0]
    total = affine.shape[1]
    block = 64
    widths = [total] + [total // 2] * split
    return pl.pallas_call(
        functools.partial(norm_kernel, count, split),
        grid_spec=pltpu.PrefetchScalarGridSpec(
            num_scalar_prefetch=1,
            grid=(rows // block,),
            in_specs=[pl.BlockSpec((block, p.shape[1]), lambda i, order: (i, 0)) for p in pieces]
            + [pl.BlockSpec((2, total), lambda i, order: (0, 0))],
            out_specs=[pl.BlockSpec((block, each), lambda i, order: (i, 0)) for each in widths],
        ),
        out_shape=[jax.ShapeDtypeStruct((rows, each), bf16) for each in widths],
        compiler_params=params(24),
        cost_estimate=cost(),
        name="layer_norm",
    )(order, *pieces, affine)


def project_kernel(heads, x_ref, w_ref, a_ref, b_ref, c_ref, q_ref, k_ref, v_ref):
    step = pl.program_id(0)
    found = jnp.dot(x_ref[...], w_ref[0], preferred_element_type=f32)

    def rotate(out_ref):
        first = found[:, :LANES]
        after = pltpu.roll(first, LANES - 1, 1)
        before = pltpu.roll(first, 1, 1)
        turned = first * a_ref[...] + after * b_ref[...] + before * c_ref[...]
        out_ref[:, :LANES] = turned.astype(bf16)
        out_ref[:, LANES:] = found[:, LANES:].astype(bf16)

    @pl.when(step < heads)
    def _():
        rotate(q_ref)

    @pl.when((step >= heads) & (step < 2 * heads))
    def _():
        rotate(k_ref)

    @pl.when(step >= 2 * heads)
    def _():
        v_ref[...] = found.astype(bf16)


def project_call(normed, weight, positions):
    rows, depth = normed.shape
    local = weight.shape[2]
    heads = local // HD
    lane = jnp.arange(LANES)
    rate = 10000.0 ** (-((lane // 2).astype(f32) * 2.0) / ROT)
    angles = positions.astype(f32)[:, None] * rate
    turns = lane < ROT
    cosine = jnp.where(turns, jnp.cos(angles), 1.0)
    sine = jnp.where(turns, jnp.sin(angles), 0.0)
    even = lane % 2 == 0
    table = pl.BlockSpec((rows, LANES), lambda j: (0, 0))
    out = jax.ShapeDtypeStruct((rows, local), bf16)
    return pl.pallas_call(
        functools.partial(project_kernel, heads),
        grid=(3 * heads,),
        in_specs=[
            pl.BlockSpec((rows, depth), lambda j: (0, 0)),
            pl.BlockSpec((1, depth, HD), lambda j: (j // heads, 0, j % heads)),
            table,
            table,
            table,
        ],
        out_specs=[
            pl.BlockSpec((rows, HD), lambda j: (0, jnp.clip(j, 0, heads - 1))),
            pl.BlockSpec((rows, HD), lambda j: (0, jnp.clip(j - heads, 0, heads - 1))),
            pl.BlockSpec((rows, HD), lambda j: (0, jnp.clip(j - 2 * heads, 0, heads - 1))),
        ],
        out_shape=[out, out, out],
        compiler_params=params(45),
        cost_estimate=cost(),
        name="projections",
    )(normed, weight, cosine, jnp.where(even, -sine, 0.0), jnp.where(even, 0.0, sine))


def attend_kernel(heads, len_ref, q_ref, kn_ref, vn_ref, kc_ref, vc_ref, out_ref):
    length = len_ref[pl.program_id(0)]
    slots = kc_ref.shape[1]
    contract = (((1,), (1,)), ((), ()))
    scale = HD ** (-0.5)
    filled = lax.broadcasted_iota(jnp.int32, (GROUP, slots), 1) < length
    causal = lax.broadcasted_iota(jnp.int32, (GROUP, GROUP), 0) >= lax.broadcasted_iota(
        jnp.int32, (GROUP, GROUP), 1
    )
    for head in range(heads):
        columns = slice(head * HD, (head + 1) * HD)
        query = q_ref[:, columns]
        old = lax.dot_general(query, kc_ref[0, :, columns], contract, preferred_element_type=f32)
        new = lax.dot_general(query, kn_ref[:, columns], contract, preferred_element_type=f32)
        old = jnp.where(filled, old * scale, very_low)
        new = jnp.where(causal, new * scale, very_low)
        top = jnp.maximum(
            jnp.max(old, axis=-1, keepdims=True), jnp.max(new, axis=-1, keepdims=True)
        )
        old = jnp.exp(old - top)
        new = jnp.exp(new - top)
        total = jnp.sum(old, axis=-1, keepdims=True) + jnp.sum(new, axis=-1, keepdims=True)
        weighted = jnp.dot(
            old.astype(bf16), vc_ref[0, :, columns], preferred_element_type=f32
        ) + jnp.dot(new.astype(bf16), vn_ref[:, columns], preferred_element_type=f32)
        out_ref[:, columns] = (weighted / total).astype(bf16)


def attend_call(lengths, query, new_key, new_value, key_cache, value_cache):
    requests, slots, local = key_cache.shape
    fresh = pl.BlockSpec((GROUP, local), lambda r, lengths: (r, 0))
    cached = pl.BlockSpec((1, slots, local), lambda r, lengths: (r, 0, 0))
    return pl.pallas_call(
        functools.partial(attend_kernel, local // HD),
        grid_spec=pltpu.PrefetchScalarGridSpec(
            num_scalar_prefetch=1,
            grid=(requests,),
            in_specs=[fresh, fresh, fresh, cached, cached],
            out_specs=fresh,
        ),
        out_shape=jax.ShapeDtypeStruct((requests * GROUP, local), bf16),
        compiler_params=params(28),
        cost_estimate=cost(),
        name="attention",
    )(lengths, query, new_key, new_value, key_cache, value_cache)


def up_kernel(depths, spots_ref, x_ref, *refs):
    weights, (bias_ref, out_ref) = refs[: len(depths)], refs[len(depths) :]
    total = bias_ref[...] + jnp.zeros(out_ref.shape, f32)
    for k, depth in enumerate(depths):
        columns = pl.ds(pl.multiple_of(spots_ref[k] * LANES, LANES), depth)
        total += jnp.dot(x_ref[:, columns], weights[k][...], preferred_element_type=f32)
    out_ref[...] = jax.nn.gelu(total, approximate=True).astype(bf16)


def up_call(spots, normed, weights, bias):
    rows, depth = normed.shape
    width = weights[0].shape[1]
    depths = [weight.shape[0] for weight in weights]
    block = 256
    return pl.pallas_call(
        functools.partial(up_kernel, depths),
        grid_spec=pltpu.PrefetchScalarGridSpec(
            num_scalar_prefetch=1,
            grid=(width // block,),
            in_specs=[pl.BlockSpec((rows, depth), lambda n, spots: (0, 0))]
            + [pl.BlockSpec((part, block), lambda n, spots: (0, n)) for part in depths]
            + [pl.BlockSpec((1, block), lambda n, spots: (0, n))],
            out_specs=pl.BlockSpec((rows, block), lambda n, spots: (0, n)),
        ),
        out_shape=jax.ShapeDtypeStruct((rows, width), bf16),
        compiler_params=params(40),
        cost_estimate=cost(),
        name="up_and_gelu",
    )(spots, normed, *weights, bias[None])


def up_half_kernel(spots_ref, rows_ref, w0, w1, w2, w3, out_ref, x_ref):
    depth = w0.shape[0]

    @pl.when(pl.program_id(0) == 0)
    def _():
        for k in range(4):
            columns = pl.ds(pl.multiple_of(spots_ref[k] * depth, depth), depth)
            x_ref[:, k * depth : (k + 1) * depth] = rows_ref[:, columns]

    weight = jnp.concatenate([w0[...], w1[...], w2[...], w3[...]], axis=0)
    out_ref[...] = jnp.dot(x_ref[...], weight, preferred_element_type=f32).astype(out_ref.dtype)


def up_half_call(spots, x, weights, start, stop, dtype):
    rows = x.shape[0]
    width = stop - start
    depth = 4 * weights[0].shape[0]
    block = 256
    steps = width // block
    first = start // block
    in_specs = [pl.BlockSpec(x.shape, lambda n, spots: (0, 0))] + [
        pl.BlockSpec((w.shape[0], block), lambda n, spots: (0, first + n)) for w in weights
    ]
    return pl.pallas_call(
        up_half_kernel,
        grid_spec=pltpu.PrefetchScalarGridSpec(
            num_scalar_prefetch=1,
            grid=(steps,),
            in_specs=in_specs,
            out_specs=pl.BlockSpec((rows, block), lambda n, spots: (0, n)),
            scratch_shapes=[pltpu.VMEM((rows, depth), bf16)],
        ),
        out_shape=jax.ShapeDtypeStruct((rows, width), dtype),
        compiler_params=params(28),
        cost_estimate=cost(),
        name="up_half",
    )(spots, x, *weights)


def gelu_kernel(keep_ref, bias_ref, *refs):
    came, out_ref = refs[:-1], refs[-1]
    start = 0
    for ref in came:
        columns = slice(start, start + ref.shape[1])
        start += ref.shape[1]
        upward = keep_ref[:, columns] + ref[...].astype(f32) + bias_ref[:, columns]
        out_ref[:, columns] = jax.nn.gelu(upward, approximate=True).astype(bf16)


def gelu_call(keep, came, bias):
    rows, width = keep.shape
    block = 64
    whole = pl.BlockSpec((block, width), lambda i: (i, 0))
    return pl.pallas_call(
        gelu_kernel,
        grid=(rows // block,),
        in_specs=[whole, pl.BlockSpec((1, width), lambda i: (0, 0))]
        + [pl.BlockSpec((block, part.shape[1]), lambda i: (i, 0)) for part in came],
        out_specs=whole,
        out_shape=jax.ShapeDtypeStruct((rows, width), bf16),
        compiler_params=params(12),
        cost_estimate=cost(),
        name="gelu",
    )(keep, bias[None], *came)


def down_kernel(place_ref, a0, a1, c0, c1, v0, v1, v2, v3, o0, o1, o2, o3, own_ref, hold_ref, send_ref, total):
    step = pl.program_id(0)
    steps = pl.num_programs(0)
    rows, width = a0.shape[0], v0.shape[1]

    @pl.when(step == 0)
    def _():
        weight = jnp.concatenate([o0[...], o1[...], o2[...], o3[...]], axis=1)
        total[:rows] = jnp.dot(c0[...], weight, preferred_element_type=f32)
        total[rows:] = jnp.dot(c1[...], weight, preferred_element_type=f32)

    weight = jnp.concatenate([v0[...], v1[...], v2[...], v3[...]], axis=1)
    total[:rows] += jnp.dot(a0[...], weight, preferred_element_type=f32)
    total[rows:] += jnp.dot(a1[...], weight, preferred_element_type=f32)

    @pl.when(step == steps - 1)
    def _():
        for k in range(4):
            columns = slice(k * width, (k + 1) * width)

            @pl.when(place_ref[4 + k] == 0)
            def _():
                own_ref[...] = total[:, columns]

            @pl.when(place_ref[4 + k] == 1)
            def _():
                send_ref[: 2 * rows] = total[:, columns].astype(bf16)

            @pl.when(place_ref[4 + k] == 2)
            def _():
                hold_ref[...] = total[:, columns]

            @pl.when(place_ref[4 + k] == 3)
            def _():
                send_ref[2 * rows :] = total[:, columns].astype(bf16)


def down_call(place, active, context, weights, out_weight, start, width):
    rows, depth = active[0].shape
    local = context[0].shape[1]
    steps = 4
    part = depth // steps
    per = out_weight.shape[1] // 8 // width
    in_specs = [pl.BlockSpec((rows, part), lambda s, place: (0, s))] * 2
    in_specs += [pl.BlockSpec((rows, local), lambda s, place: (0, 0))] * 2
    for _, column in weights:
        in_specs.append(pl.BlockSpec((part, width), lambda s, place, column=column: (s, column)))
    for k in range(4):
        in_specs.append(
            pl.BlockSpec(
                (local, width), lambda s, place, k=k: (0, place[k] * per + start // width)
            )
        )
    result = pl.BlockSpec((2 * rows, width), lambda s, place: (0, 0))
    double = pl.BlockSpec((4 * rows, width), lambda s, place: (0, 0))
    return pl.pallas_call(
        down_kernel,
        grid_spec=pltpu.PrefetchScalarGridSpec(
            num_scalar_prefetch=1,
            grid=(steps,),
            in_specs=in_specs,
            out_specs=[result, result, double],
            scratch_shapes=[pltpu.VMEM((2 * rows, 4 * width), f32)],
        ),
        out_shape=[jax.ShapeDtypeStruct((2 * rows, width), f32)] * 2
        + [jax.ShapeDtypeStruct((4 * rows, width), bf16)],
        compiler_params=params(24),
        cost_estimate=cost(),
        name="down_and_output",
    )(place, *active, *context, *[w for w, _ in weights], *[out_weight] * 4)


def sum_kernel(own_ref, hold_ref, came_ref, kept_ref, send_ref):
    rows = own_ref.shape[0]
    kept_ref[...] = own_ref[...] + came_ref[:rows].astype(f32)
    send_ref[...] = (hold_ref[...] + came_ref[rows:].astype(f32)).astype(bf16)


def sum_call(own, hold, came):
    return pl.pallas_call(
        sum_kernel,
        out_shape=[
            jax.ShapeDtypeStruct(own.shape, f32),
            jax.ShapeDtypeStruct(own.shape, bf16),
        ],
        compiler_params=params(12),
        cost_estimate=cost(),
        name="sum_near",
    )(own, hold, came)


def join_kernel(widths, *refs):
    keep_ref, send_ref = refs[-2:]
    rows = keep_ref.shape[0]
    start = 0
    for piece, width in enumerate(widths):
        summed = refs[2 * piece][...] + refs[2 * piece + 1][...].astype(f32)
        keep_ref[:, start : start + width] = summed[:rows]
        send_ref[:, start : start + width] = summed[rows:]
        start += width


def join_call(pieces):
    widths = [piece[0].shape[1] for piece in pieces]
    rows = pieces[0][0].shape[0] // 2
    out = jax.ShapeDtypeStruct((rows, sum(widths)), f32)
    return pl.pallas_call(
        functools.partial(join_kernel, widths),
        out_shape=[out, out],
        compiler_params=params(12),
        cost_estimate=cost(),
        name="sum_far",
    )(*[array for piece in pieces for array in piece])


def close_kernel(side_ref, hidden_ref, bias_ref, own_ref, other_ref, out_ref):
    width = own_ref.shape[1]
    for source, side in ((own_ref, side_ref[0]), (other_ref, 1 - side_ref[0])):
        columns = pl.ds(pl.multiple_of(side * width, width), width)
        out_ref[:, columns] = (
            hidden_ref[:, columns].astype(f32) + source[...] + bias_ref[:, columns]
        ).astype(bf16)


def close_call(side, hidden, bias, own, other):
    return pl.pallas_call(
        close_kernel,
        in_specs=[pl.BlockSpec(memory_space=pltpu.SMEM)]
        + [pl.BlockSpec(memory_space=pltpu.VMEM)] * 4,
        out_shape=jax.ShapeDtypeStruct(hidden.shape, bf16),
        compiler_params=params(12),
        cost_estimate=cost(),
        name="final_sum",
    )(side, hidden, bias[None], own, other)


CORE, X, Y = 1, 2, 4


def swap(value, axis, size, mask):
    return lax.ppermute(value, axis, [(i, i ^ mask) for i in range(size)])


def after(value, earlier):
    return lax.optimization_barrier((value, earlier))[0]


def body_small(
    hidden_in,
    norm_gain,
    norm_shift,
    attend_weight,
    output_weight,
    up_weight,
    up_bias,
    down_weight,
    down_bias,
    key_cache,
    value_cache,
    cached_len,
):
    over_req = functools.partial(swap, axis="req", size=8)
    over_head = functools.partial(swap, axis="head", size=4)
    me = lax.axis_index("req").astype(jnp.int32)
    line = lax.axis_index("head").astype(jnp.int32)
    side = me & 1
    chips = jnp.arange(4, dtype=jnp.int32)
    batch_size = key_cache.shape[0]
    local_width = output_weight.shape[0]

    far = over_head(hidden_in, mask=2)
    near = over_head(hidden_in, mask=1)
    up_x = over_req(up_weight, mask=X)
    down_y = over_req(down_weight, mask=Y)
    up_core = over_req(up_weight, mask=CORE)
    last = over_head(far, mask=1)
    pair = jnp.concatenate([hidden_in, near], axis=1)
    affine = jnp.stack([norm_gain, norm_shift])
    last, pair, affine = lax.optimization_barrier((last, pair, affine))

    order = jnp.concatenate([line ^ chips, (1 - (me >> 2))[None]])
    normed, for_other = norm_call(order, 4, [pair, far, last], affine, split=True)
    normed_other = over_req(for_other, mask=Y)
    up_x, up_core, down_y, normed_next = lax.optimization_barrier((up_x, up_core, down_y, normed))
    up_x_core = over_req(up_x, mask=CORE)
    down_x = over_req(after(down_weight, up_x), mask=X)

    half = down_weight.shape[1] // 2
    quarter = half // 2
    forward_y = [down_y[:, k * quarter : (k + 1) * quarter] for k in range(2)]
    diagonal = [over_req(forward_y[0], mask=X)]
    normed_next, forward_y = lax.optimization_barrier((normed_next, forward_y))

    positions = (cached_len[:, None] + jnp.arange(GROUP, dtype=jnp.int32)[None, :]).reshape(-1)
    query, new_key, new_value = project_call(
        normed_next, attend_weight.transpose(1, 0, 2), positions
    )

    blocks = me ^ jnp.array([0, X, CORE, X | CORE], jnp.int32)
    weights = [up_weight, up_x, up_core, up_x_core]
    units = up_weight.shape[1]
    keep = up_half_call(blocks, after(normed, query), weights, 0, units, f32)
    other = after(normed_other, keep)
    came = []
    cut = units * 5 // 8
    for start, stop in ((0, cut), (cut, units)):
        send = up_half_call(blocks & 3, other, weights, start, stop, bf16)
        came.append(over_req(send, mask=Y))
        other = after(other, send)

    query = after(query, other)
    context = attend_call(cached_len, query, new_key, new_value, key_cache, value_cache)
    context_other = over_req(context, mask=CORE)

    came, context_other, diagonal[0] = lax.optimization_barrier((came, context_other, diagonal[0]))
    diagonal.append(over_req(after(forward_y[1], diagonal[0]), mask=X))
    forward_x = [down_x[:, half + k * quarter : half + (k + 1) * quarter] for k in range(2)]
    forward_x = after(forward_x, came)
    diagonal += [over_req(part, mask=Y) for part in forward_x]

    active = gelu_call(keep, came, up_bias)
    active_other = over_req(active, mask=CORE)

    blocks = me ^ (2 * chips)
    place = jnp.concatenate([blocks, line ^ (blocks >> 1)])
    results, behind = {}, []
    previous = None
    rows = active, active_other
    for k in (0, 2, 1, 3):
        if len(behind) == 2:
            rows = after(rows, behind.pop(0))
        own, hold, send = down_call(
            place,
            rows,
            (context, context_other),
            [(down_weight, k), (down_x, k), (down_y, k), (diagonal[k], 0)],
            output_weight,
            k * quarter,
            quarter,
        )
        came = over_head(send, mask=1)
        if previous is not None:
            came = after(came, previous)
        own, second = sum_call(own, hold, came)
        behind.append(second)
        previous = over_head(second, mask=2)
        results[k] = own, previous
    results = [results[k] for k in range(4)]
    own, send = join_call(results)
    other = over_req(send, mask=CORE)
    hidden_out = close_call(side[None], hidden_in, down_bias, own, other)
    shape = (batch_size, GROUP, local_width)
    return hidden_out, new_key.reshape(shape), new_value.reshape(shape)


def body_any(
    hidden_in,
    norm_gain,
    norm_shift,
    attend_weight,
    output_weight,
    up_weight,
    up_bias,
    down_weight,
    down_bias,
    key_cache,
    value_cache,
    cached_len,
):
    batch_size = key_cache.shape[0]
    local_width = output_weight.shape[0]
    gathered = lax.all_gather(hidden_in, "head", axis=1, tiled=True)
    affine = jnp.stack([norm_gain, norm_shift])
    (normed,) = norm_call(jnp.zeros((1,), jnp.int32), 1, [gathered], affine)
    positions = (cached_len[:, None] + jnp.arange(GROUP, dtype=jnp.int32)[None, :]).reshape(-1)
    query, new_key, new_value = project_call(
        normed, attend_weight.transpose(1, 0, 2), positions
    )
    context = attend_call(cached_len, query, new_key, new_value, key_cache, value_cache)
    attended = jnp.dot(context, output_weight, preferred_element_type=f32)
    up_whole = lax.all_gather(up_weight, "req", axis=0, tiled=True)
    active = up_call(jnp.zeros((1,), jnp.int32), normed, [up_whole], up_bias)
    downward = jnp.dot(
        active,
        lax.all_gather(down_weight, "req", axis=1, tiled=True),
        preferred_element_type=f32,
    )
    summed = lax.psum_scatter(
        (attended + downward).astype(bf16), "head", scatter_dimension=1, tiled=True
    ).astype(f32)
    hidden_out = (hidden_in.astype(f32) + summed + down_bias).astype(bf16)
    shape = (batch_size, GROUP, local_width)
    return hidden_out, new_key.reshape(shape), new_value.reshape(shape)


def solution(mesh):
    small = mesh.shape["req"] == 8 and mesh.shape["head"] == 4
    placed = (
        P("req", "head"),
        P(),
        P(),
        P(None, None, "head"),
        P("head", None),
        P("req", "head"),
        P("head"),
        P("head", "req"),
        P("head"),
        P("req", None, "head"),
        P("req", None, "head"),
        P("req"),
    )
    return jax.shard_map(
        body_small if small else body_any,
        mesh=mesh,
        in_specs=placed,
        out_specs=(P("req", "head"), P("req", None, "head"), P("req", None, "head")),
        check_vma=False,
    )
```

time: 321 us -> 170 us (0.53)
  waiting for transfers between devices: 189 us -> 78.7 us
  matrix products: 56.2 us -> 0 us
  Pallas kernels: 0 us -> 50 us
  local copies, waits for them, and re-layouts: 41.8 us -> 1 us
  starting transfers between devices: 0.15 us -> 34 us
  other arithmetic: 17.6 us -> 3.02 us
  between operations: 14.7 us -> 0.92 us
    all_gather x3 -> x0, waiting for transfers between devices: 146 us -> none  [the longest x1 91.8 us: body(): lax.all_gather(up_weight, 'req', axis=0, tiled=True)]
    ppermute x0 -> x26, waiting for transfers between devices: none -> 78.7 us  [swap(): return lax.ppermute(value, axis, [(i, i ^ mask) for i in range(size)])]
    dot_general x23 -> x0, matrix products: 56.2 us -> none  [the longest x1 17.4 us: body(): jnp.dot(active, lax.all_gather(down_weight, 'req', axis=1, tiled=True), p...]
    pallas_call x0 -> x17, Pallas kernels: none -> 50 us  [the longest x3 16.7 us: up_half_call(): pl.pallas_call(up_half_kernel, grid_spec=pltpu.PrefetchScalarGridSpec(num...]
    reduce_scatter x1 -> x0, waiting for transfers between devices: 40.9 us -> none  [body(): lax.psum_scatter((attended + downward).astype(jnp.bfloat16), 'head', scat...]
    ppermute x0 -> x26, starting transfers between devices: none -> 34 us  [swap(): return lax.ppermute(value, axis, [(i, i ^ mask) for i in range(size)])]
    unnamed x28 -> x24, local copies, waits for them, and re-layouts: 25.8 us -> 0.06 us
    slice x9 -> x2, local copies, waits for them, and re-layouts: 13.3 us -> 0.94 us  [the longest x1 0.87 us: body_small(): forward_y = [down_y[:, k * quarter:(k + 1) * quarter] for k in range(2)]]
  transfers between devices with their start and end apart: 4 -> 26, of which waited for: 4 -> 14; matrix products, arithmetic and copies ran while one was open for 28% -> 2% of each run, Pallas kernels for 0% -> 29%
where the time goes in v1:
time: 170 us; the launch traced here: 168 us
  waiting for transfers between devices  78.7 us (46%)
  Pallas kernels  50 us (29%)
  starting transfers between devices  34 us (20%)
  other arithmetic  3.02 us (2%)
    ppermute x26, waiting for transfers between devices, swap(): return lax.ppermute(value, axis, [(i, i ^ mask) for i in range(size)])  78.7 us
    ppermute x26, starting transfers between devices, swap(): return lax.ppermute(value, axis, [(i, i ^ mask) for i in range(size)])  34 us
    pallas_call x3, Pallas kernels, up_half_call(): pl.pallas_call(up_half_kernel, grid_spec=pltpu.PrefetchScalarGridSpec(num...  16.7 us
    pallas_call x4, Pallas kernels, down_call(): pl.pallas_call(down_kernel, grid_spec=pltpu.PrefetchScalarGridSpec(num_sc...  15.2 us
    pallas_call x1, Pallas kernels, project_call(): pl.pallas_call(functools.partial(project_kernel, heads), grid=(3 * heads,...  9.42 us
    pallas_call x1, Pallas kernels, attend_call(): pl.pallas_call(functools.partial(attend_kernel, local // HD), grid_spec=p...  3.72 us
  transfers between devices with their start and end apart: 26, of which 14 were waited for; matrix products, arithmetic and copies ran while one was open for 2% of the time, Pallas kernels for 29%

profile of v1, /device:TPU:0, one launch (start us, length us, event | category | flops | bytes accessed | tf_op | source)
XLA Modules:
  0.0 167.7 jit_solution(9892232586845202877)
XLA Ops:
  0.6 3.0 %collective-permute-start.3 = (bf16[512,2048]{1,0:T(8,128)(2,1)}, bf16[512,2048]{1,0:T(8,128)(2,1)}, u32[]{:S(2)}, u32[]{:S(2)}) collective-permute-start(bf16[512,2048]{1,0:T(8,128)(2,1)} %w0.5), channel_id=1, source_target_pairs={{0,8},{4,12},{8,0},{12,4},{16,24},{20,28},{24,16},{28,20},{1,9},{5... | collective-permute-start | bytes 6291464 | tf_op jit(solution)/shard_map/ppermute | solution.py:420
  5.2 2.6 %collective-permute-start = (bf16[256,1024]{1,0:T(8,128)(2,1)}, bf16[256,1024]{1,0:T(8,128)(2,1)S(1)}, u32[]{:S(2)}, u32[]{:S(2)}) collective-permute-start(bf16[256,1024]{1,0:T(8,128)(2,1)} %hidden_ref.1), channel_id=1, source_target_pairs={{0,2},{1,3},{2,0},{3,1},{4,6},{5,7},{6,4},{7,5},{8,10},{9,11},{10,... | collective-permute-start | bytes 1572872 | tf_op jit(solution)/shard_map/ppermute | solution.py:420
  9.3 22.3 %collective-permute-done.refs_1_ = bf16[256,1024]{1,0:T(8,128)(2,1)S(1)} collective-permute-done((bf16[256,1024]{1,0:T(8,128)(2,1)}, bf16[256,1024]{1,0:T(8,128)(2,1)S(1)}, u32[]{:S(2)}, u32[]{:S(2)}) %collective-permute-start) | collective-permute-done | bytes 524320 | tf_op jit(solution)/shard_map/ppermute | solution.py:420
  34.7 10.2 %collective-permute-done.1.refs_2_ = bf16[256,1024]{1,0:T(8,128)(2,1)S(1)} collective-permute-done((bf16[256,1024]{1,0:T(8,128)(2,1)S(1)}, bf16[256,1024]{1,0:T(8,128)(2,1)S(1)}, u32[]{:S(2)}, u32[]{:S(2)}) %collective-permute-start.1) | collective-permute-done | bytes 524320 | tf_op jit(solution)/shard_map/ppermute | solution.py:420
  44.8 2.7 %layer_norm.1 = (bf16[256,4096]{1,0:T(8,128)(2,1)S(1)}, bf16[256,2048]{1,0:T(8,128)(2,1)S(1)}) custom-call(s32[5]{0:T(128)S(1)} %pad_add_fusion.1.order_ref, bf16[256,2048]{1,0:T(8,128)(2,1)S(1)} %pad_maximum_fusion.refs_0_, bf16[256,1024]{1,0:T(8,128)(2,1)S(1)} %collective-permute-done.refs_1_, bf16[256,1024]{1,0:T(8,128)(2,1)S(1)} %collective-permute-done.1.refs_2_, ...), custom_call_target="tpu_custom_call" | custom-call | flops 1024 | bytes 1024 | tf_op jit(solution)/shard_map/layer_norm/pallas_call | solution.py:60
  49.6 2.3 %collective-permute-done.5.v2 = bf16[2048,512]{1,0:T(8,128)(2,1)S(1)} collective-permute-done((bf16[2048,512]{1,0:T(8,128)(2,1)}, bf16[2048,512]{1,0:T(8,128)(2,1)S(1)}, u32[]{:S(2)}, u32[]{:S(2)}) %collective-permute-start.5) | collective-permute-done | bytes 2097184 | tf_op jit(solution)/shard_map/ppermute | solution.py:420
  55.6 9.4 %projections.1 = (bf16[256,512]{1,0:T(8,128)(2,1)S(1)}, bf16[256,512]{1,0:T(8,128)(2,1)}, bf16[256,512]{1,0:T(8,128)(2,1)}) custom-call(bf16[256,4096]{1,0:T(8,128)(2,1)S(1)} %get-tuple-element.65.x_ref.rows_ref, bf16[3,4096,512]{2,1,0:T(8,128)(2,1)} %bitcast.15, f32[256,128]{1,0:T(8,128)S(1)} %get-tuple-element.117.a_ref, ...), custom_call_target="tpu_custom_call" | custom-call | flops 1024 | bytes 1024 | tf_op jit(solution)/shard_map/projections/pallas_call | solution.py:114
  65.0 7.4 %up_half.3.keep_ref = f32[256,2048]{1,0:T(8,128)S(1)} custom-call(s32[4]{0:T(128)S(1)} %get-tuple-element.119.spots_ref, bf16[256,4096]{1,0:T(8,128)(2,1)S(1)} %get-tuple-element.65.x_ref.rows_ref, bf16[512,2048]{1,0:T(8,128)(2,1)S(1)} %copy-done.2, bf16[512,2048]{1,0:T(8,128)(2,1)} %collective-permute-done.3.w1, ...), custom_call_target="tpu_custom_call" | custom-call | flops 1024 | bytes 1024 | tf_op jit(solution)/shard_map/up_half/pallas_call | solution.py:237
  72.4 5.2 %collective-permute-done.7.rows_ref = bf16[256,2048]{1,0:T(8,128)(2,1)S(1)} collective-permute-done((bf16[256,2048]{1,0:T(8,128)(2,1)S(1)}, bf16[256,2048]{1,0:T(8,128)(2,1)S(1)}, u32[]{:S(2)}, u32[]{:S(2)}) %collective-permute-start.7) | collective-permute-done | bytes 1048608 | tf_op jit(solution)/shard_map/ppermute | solution.py:420
  77.6 5.3 %up_half.4 = bf16[256,1280]{1,0:T(8,128)(2,1)S(1)} custom-call(s32[4]{0:T(128)S(1)} %get-tuple-element.118.spots_ref, bf16[256,2048]{1,0:T(8,128)(2,1)S(1)} %collective-permute-done.7.rows_ref, bf16[512,2048]{1,0:T(8,128)(2,1)S(1)} %copy-done.2, bf16[512,2048]{1,0:T(8,128)(2,1)} %collective-permute-done.3.w1, bf16[512,2048]{1,0:T(8,128)(2,1)} %collective-permute-done.4.w2, ...), custom_call_target="tpu_custom_call" | custom-call | flops 1024 | bytes 1024 | tf_op jit(solution)/shard_map/up_half/pallas_call | solution.py:237
  86.1 4.0 %up_half.5 = bf16[256,768]{1,0:T(8,128)(2,1)S(1)} custom-call(s32[4]{0:T(128)S(1)} %get-tuple-element.118.spots_ref, bf16[256,2048]{1,0:T(8,128)(2,1)S(1)} %collective-permute-done.7.rows_ref, bf16[512,2048]{1,0:T(8,128)(2,1)S(1)} %copy-done.2, bf16[512,2048]{1,0:T(8,128)(2,1)} %collective-permute-done.3.w1, bf16[512,2048]{1,0:T(8,128)(2,1)} %collective-permute-done.4.w2, ...), custom_call_target="tpu_custom_call" | custom-call | flops 1024 | bytes 1024 | tf_op jit(solution)/shard_map/up_half/pallas_call | solution.py:237
  90.8 3.7 %attention.1.c0 = bf16[256,512]{1,0:T(8,128)(2,1)S(1)} custom-call(s32[2]{0:T(128)S(1)} %copy-done.10, bf16[256,512]{1,0:T(8,128)(2,1)S(1)} %get-tuple-element.64.q_ref, bf16[256,512]{1,0:T(8,128)(2,1)S(1)} %copy-done.6, bf16[256,512]{1,0:T(8,128)(2,1)S(1)} %copy-done.7, bf16[2,1536,512]{2,1,0:T(8,128)(2,1)S(1)} %copy-done.3, bf16[2,1536,512]{2,1,0:T(8,128)(2,1)S(1)} %copy-done.4), custom_call_target="tpu_custom_call" | custom-call | flops 1024 | bytes 1024 | tf_op jit(solution)/shard_map/attention/pallas_call | solution.py:168
  96.1 15.2 %collective-permute-done.11.v3 = bf16[2048,128]{1,0:T(8,128)(2,1)S(1)} collective-permute-done((bf16[2048,128]{1,0:T(8,128)(2,1)}, bf16[2048,128]{1,0:T(8,128)(2,1)S(1)}, u32[]{:S(2)}, u32[]{:S(2)}) %collective-permute-start.11) | collective-permute-done | bytes 524320 | tf_op jit(solution)/shard_map/ppermute | solution.py:420
  115.0 3.8 %down_and_output.4 = (f32[512,128]{1,0:T(8,128)S(1)}, f32[512,128]{1,0:T(8,128)S(1)}, bf16[1024,128]{1,0:T(8,128)(2,1)S(1)}) custom-call(s32[8]{0:T(128)S(1)} %pad_add_fusion.place_ref, bf16[256,2048]{1,0:T(8,128)(2,1)S(1)} %gelu.1.a0, bf16[256,2048]{1,0:T(8,128)(2,1)S(1)} %collective-permute-done.12.a1, bf16[256,512]{1,0:T(8,128)(2,1)S(1)} %attention.1.c0, ...), custom_call_target="tpu_custom_call" | custom-call | flops 1024 | bytes 1024 | tf_op jit(solution)/shard_map/down_and_output/pallas_call | solution.py:335
  120.6 6.6 %collective-permute-done.18.v3 = bf16[2048,128]{1,0:T(8,128)(2,1)S(1)} collective-permute-done((bf16[2048,128]{1,0:T(8,128)(2,1)S(1)}, bf16[2048,128]{1,0:T(8,128)(2,1)S(1)}, u32[]{:S(2)}, u32[]{:S(2)}) %collective-permute-start.18) | collective-permute-done | bytes 524320 | tf_op jit(solution)/shard_map/ppermute | solution.py:420
  127.2 3.8 %down_and_output.6 = (f32[512,128]{1,0:T(8,128)S(1)}, f32[512,128]{1,0:T(8,128)S(1)}, bf16[1024,128]{1,0:T(8,128)(2,1)S(1)}) custom-call(s32[8]{0:T(128)S(1)} %pad_add_fusion.place_ref, bf16[256,2048]{1,0:T(8,128)(2,1)S(1)} %gelu.1.a0, bf16[256,2048]{1,0:T(8,128)(2,1)S(1)} %collective-permute-done.12.a1, bf16[256,512]{1,0:T(8,128)(2,1)S(1)} %attention.1.c0, ...), custom_call_target="tpu_custom_call" | custom-call | flops 1024 | bytes 1024 | tf_op jit(solution)/shard_map/down_and_output/pallas_call | solution.py:335
  132.7 2.7 %collective-permute-start.15 = (bf16[512,128]{1,0:T(8,128)(2,1)S(1)}, bf16[512,128]{1,0:T(8,128)(2,1)S(1)}, u32[]{:S(2)}, u32[]{:S(2)}) collective-permute-start(bf16[512,128]{1,0:T(8,128)(2,1)S(1)} %get-tuple-element.82), channel_id=1, source_target_pairs={{0,2},{1,3},{2,0},{3,1},{4,6},{5,7},{6,4},{7,5},{8,10},{9,11},{10,... | collective-permute-start | bytes 393224 | tf_op jit(solution)/shard_map/ppermute | solution.py:420
  135.4 3.8 %down_and_output.5 = (f32[512,128]{1,0:T(8,128)S(1)}, f32[512,128]{1,0:T(8,128)S(1)}, bf16[1024,128]{1,0:T(8,128)(2,1)S(1)}) custom-call(s32[8]{0:T(128)S(1)} %pad_add_fusion.place_ref, bf16[256,2048]{1,0:T(8,128)(2,1)S(1)} %gelu.1.a0, bf16[256,2048]{1,0:T(8,128)(2,1)S(1)} %collective-permute-done.12.a1, bf16[256,512]{1,0:T(8,128)(2,1)S(1)} %attention.1.c0, ...), custom_call_target="tpu_custom_call" | custom-call | flops 1024 | bytes 1024 | tf_op jit(solution)/shard_map/down_and_output/pallas_call | solution.py:335
  139.7 2.4 %collective-permute-done.19.came_ref = bf16[1024,128]{1,0:T(8,128)(2,1)S(1)} collective-permute-done((bf16[1024,128]{1,0:T(8,128)(2,1)S(1)}, bf16[1024,128]{1,0:T(8,128)(2,1)S(1)}, u32[]{:S(2)}, u32[]{:S(2)}) %collective-permute-start.19) | collective-permute-done | bytes 262176 | tf_op jit(solution)/shard_map/ppermute | solution.py:420
  142.3 3.4 %collective-permute-start.20 = (bf16[512,128]{1,0:T(8,128)(2,1)S(1)}, bf16[512,128]{1,0:T(8,128)(2,1)S(1)}, u32[]{:S(2)}, u32[]{:S(2)}) collective-permute-start(bf16[512,128]{1,0:T(8,128)(2,1)S(1)} %get-tuple-element.95), channel_id=1, source_target_pairs={{0,2},{1,3},{2,0},{3,1},{4,6},{5,7},{6,4},{7,5},{8,10},{9,11},{10,... | collective-permute-start | bytes 393224 | tf_op jit(solution)/shard_map/ppermute | solution.py:420
  145.7 3.8 %down_and_output.7 = (f32[512,128]{1,0:T(8,128)S(1)}, f32[512,128]{1,0:T(8,128)S(1)}, bf16[1024,128]{1,0:T(8,128)(2,1)S(1)}) custom-call(s32[8]{0:T(128)S(1)} %pad_add_fusion.place_ref, bf16[256,2048]{1,0:T(8,128)(2,1)S(1)} %gelu.1.a0, bf16[256,2048]{1,0:T(8,128)(2,1)S(1)} %collective-permute-done.12.a1, bf16[256,512]{1,0:T(8,128)(2,1)S(1)} %attention.1.c0, ...), custom_call_target="tpu_custom_call" | custom-call | flops 1024 | bytes 1024 | tf_op jit(solution)/shard_map/down_and_output/pallas_call | solution.py:335
  153.1 5.2 %collective-permute-done.21.refs_3_ = bf16[512,128]{1,0:T(8,128)(2,1)S(1)} collective-permute-done((bf16[512,128]{1,0:T(8,128)(2,1)S(1)}, bf16[512,128]{1,0:T(8,128)(2,1)S(1)}, u32[]{:S(2)}, u32[]{:S(2)}) %collective-permute-start.21) | collective-permute-done | bytes 131104 | tf_op jit(solution)/shard_map/ppermute | solution.py:420
  158.3 2.6 %collective-permute-start.24 = (bf16[512,128]{1,0:T(8,128)(2,1)S(1)}, bf16[512,128]{1,0:T(8,128)(2,1)S(1)}, u32[]{:S(2)}, u32[]{:S(2)}) collective-permute-start(bf16[512,128]{1,0:T(8,128)(2,1)S(1)} %get-tuple-element.108), channel_id=1, source_target_pairs={{0,2},{1,3},{2,0},{3,1},{4,6},{5,7},{6,4},{7,5},{8,10},{9,11},{10,... | collective-permute-start | bytes 393224 | tf_op jit(solution)/shard_map/ppermute | solution.py:420
  160.9 3.7 %collective-permute-done.24.refs_7_ = bf16[512,128]{1,0:T(8,128)(2,1)S(1)} collective-permute-done((bf16[512,128]{1,0:T(8,128)(2,1)S(1)}, bf16[512,128]{1,0:T(8,128)(2,1)S(1)}, u32[]{:S(2)}, u32[]{:S(2)}) %collective-permute-start.24) | collective-permute-done | bytes 131104 | tf_op jit(solution)/shard_map/ppermute | solution.py:420
  (82 shorter events, 31.5 us)
Async XLA Ops:
  0.6 49.0 %collective-permute-start.3 = (bf16[512,2048]{1,0:T(8,128)(2,1)}, bf16[512,2048]{1,0:T(8,128)(2,1)}, u32[]{:S(2)}, u32[]{:S(2)}) collective-permute-start(bf16[512,2048]{1,0:T(8,128)(2,1)} %w0.5), channel_id=1, source_target_pairs={{0,8},{4,12},{8,0},{12,4},{16,24},{20,28},{24,16},{28,20},{1,9},{5... | collective-permute-start | bytes 6291464 | tf_op jit(solution)/shard_map/ppermute | solution.py:420
  3.6 46.0 %collective-permute-start.4 = (bf16[512,2048]{1,0:T(8,128)(2,1)}, bf16[512,2048]{1,0:T(8,128)(2,1)}, u32[]{:S(2)}, u32[]{:S(2)}) collective-permute-start(bf16[512,2048]{1,0:T(8,128)(2,1)} %w0.5), channel_id=1, source_target_pairs={{0,4},{4,0},{8,12},{12,8},{16,20},{20,16},{24,28},{28,24},{1,5},{5... | collective-permute-start | bytes 6291464 | tf_op jit(solution)/shard_map/ppermute | solution.py:420
  3.6 48.3 %collective-permute-start.5 = (bf16[2048,512]{1,0:T(8,128)(2,1)}, bf16[2048,512]{1,0:T(8,128)(2,1)S(1)}, u32[]{:S(2)}, u32[]{:S(2)}) collective-permute-start(bf16[2048,512]{1,0:T(8,128)(2,1)} %v0.7), channel_id=1, source_target_pairs={{0,16},{4,20},{8,24},{12,28},{16,0},{20,4},{24,8},{28,12},{1,17},{... | collective-permute-start | bytes 6291464 | tf_op jit(solution)/shard_map/ppermute | solution.py:420
  5.2 26.5 %collective-permute-start = (bf16[256,1024]{1,0:T(8,128)(2,1)}, bf16[256,1024]{1,0:T(8,128)(2,1)S(1)}, u32[]{:S(2)}, u32[]{:S(2)}) collective-permute-start(bf16[256,1024]{1,0:T(8,128)(2,1)} %hidden_ref.1), channel_id=1, source_target_pairs={{0,2},{1,3},{2,0},{3,1},{4,6},{5,7},{6,4},{7,5},{8,10},{9,11},{10,... | collective-permute-start | bytes 1572872 | tf_op jit(solution)/shard_map/ppermute | solution.py:420
  7.7 25.5 %collective-permute-start.2 = (bf16[256,1024]{1,0:T(8,128)(2,1)}, bf16[256,1024]{1,0:T(8,128)(2,1)}, u32[]{:S(2)}, u32[]{:S(2)}) collective-permute-start(bf16[256,1024]{1,0:T(8,128)(2,1)} %hidden_ref.1), channel_id=1, source_target_pairs={{0,1},{1,0},{2,3},{3,2},{4,5},{5,4},{6,7},{7,6},{8,9},{9,8},{10,11... | collective-permute-start | bytes 1572872 | tf_op jit(solution)/shard_map/ppermute | solution.py:420
  31.7 13.2 %collective-permute-start.1 = (bf16[256,1024]{1,0:T(8,128)(2,1)S(1)}, bf16[256,1024]{1,0:T(8,128)(2,1)S(1)}, u32[]{:S(2)}, u32[]{:S(2)}) collective-permute-start(bf16[256,1024]{1,0:T(8,128)(2,1)S(1)} %collective-permute-done.refs_1_), channel_id=1, source_target_pairs={{0,1},{1,0},{2,3},{3,2},{4,5},{5,4},{6,7},{7,6},{8,9},{9,8},{10,11... | collective-permute-start | bytes 1572872 | tf_op jit(solution)/shard_map/ppermute | solution.py:420
  51.9 13.1 %collective-permute-start.6 = (bf16[512,2048]{1,0:T(8,128)(2,1)}, bf16[512,2048]{1,0:T(8,128)(2,1)S(1)}, u32[]{:S(2)}, u32[]{:S(2)}) collective-permute-start(bf16[512,2048]{1,0:T(8,128)(2,1)} %collective-permute-done.3.w1), channel_id=1, source_target_pairs={{0,4},{4,0},{8,12},{12,8},{16,20},{20,16},{24,28},{28,24},{1,5},{5... | collective-permute-start | bytes 6291464 | tf_op jit(solution)/shard_map/ppermute | solution.py:420
  51.9 60.4 %collective-permute-start.13 = (bf16[2048,512]{1,0:T(8,128)(2,1)S(1)}, bf16[2048,512]{1,0:T(8,128)(2,1)S(1)}, u32[]{:S(2)}, u32[]{:S(2)}) collective-permute-start(bf16[2048,512]{1,0:T(8,128)(2,1)S(1)} %copy-done.1), channel_id=1, source_target_pairs={{0,8},{4,12},{8,0},{12,4},{16,24},{20,28},{24,16},{28,20},{1,9},{5... | collective-permute-start | bytes 6291464 | tf_op jit(solution)/shard_map/ppermute | solution.py:420
  52.3 25.3 %collective-permute-start.7 = (bf16[256,2048]{1,0:T(8,128)(2,1)S(1)}, bf16[256,2048]{1,0:T(8,128)(2,1)S(1)}, u32[]{:S(2)}, u32[]{:S(2)}) collective-permute-start(bf16[256,2048]{1,0:T(8,128)(2,1)S(1)} %get-tuple-element.68), channel_id=1, source_target_pairs={{0,16},{4,20},{8,24},{12,28},{16,0},{20,4},{24,8},{28,12},{1,17},{... | collective-permute-start | bytes 3145736 | tf_op jit(solution)/shard_map/ppermute | solution.py:420
  82.9 28.3 %collective-permute-start.8 = (bf16[256,1280]{1,0:T(8,128)(2,1)S(1)}, bf16[256,1280]{1,0:T(8,128)(2,1)S(1)}, u32[]{:S(2)}, u32[]{:S(2)}) collective-permute-start(bf16[256,1280]{1,0:T(8,128)(2,1)S(1)} %up_half.4), channel_id=1, source_target_pairs={{0,16},{4,20},{8,24},{12,28},{16,0},{20,4},{24,8},{28,12},{1,17},{... | collective-permute-start | bytes 1966088 | tf_op jit(solution)/shard_map/ppermute | solution.py:420
  84.7 26.6 %collective-permute-start.11 = (bf16[2048,128]{1,0:T(8,128)(2,1)}, bf16[2048,128]{1,0:T(8,128)(2,1)S(1)}, u32[]{:S(2)}, u32[]{:S(2)}) collective-permute-start(bf16[2048,128]{1,0:T(8,128)(2,1)} %get-tuple-element.114), channel_id=1, source_target_pairs={{0,8},{4,12},{8,0},{12,4},{16,24},{20,28},{24,16},{28,20},{1,9},{5... | collective-permute-start | bytes 1572872 | tf_op jit(solution)/shard_map/ppermute | solution.py:420
  90.2 21.1 %collective-permute-start.9 = (bf16[256,768]{1,0:T(8,128)(2,1)S(1)}, bf16[256,768]{1,0:T(8,128)(2,1)S(1)}, u32[]{:S(2)}, u32[]{:S(2)}) collective-permute-start(bf16[256,768]{1,0:T(8,128)(2,1)S(1)} %up_half.5), channel_id=1, source_target_pairs={{0,16},{4,20},{8,24},{12,28},{16,0},{20,4},{24,8},{28,12},{1,17},{... | collective-permute-start | bytes 1179656 | tf_op jit(solution)/shard_map/ppermute | solution.py:420
  112.2 2.7 %collective-permute-start.12 = (bf16[256,2048]{1,0:T(8,128)(2,1)S(1)}, bf16[256,2048]{1,0:T(8,128)(2,1)S(1)}, u32[]{:S(2)}, u32[]{:S(2)}) collective-permute-start(bf16[256,2048]{1,0:T(8,128)(2,1)S(1)} %gelu.1.a0), channel_id=1, source_target_pairs={{0,4},{4,0},{8,12},{12,8},{16,20},{20,16},{24,28},{28,24},{1,5},{5... | collective-permute-start | bytes 3145736 | tf_op jit(solution)/shard_map/ppermute | solution.py:420
  112.4 14.8 %collective-permute-start.18 = (bf16[2048,128]{1,0:T(8,128)(2,1)S(1)}, bf16[2048,128]{1,0:T(8,128)(2,1)S(1)}, u32[]{:S(2)}, u32[]{:S(2)}) collective-permute-start(bf16[2048,128]{1,0:T(8,128)(2,1)S(1)} %get-tuple-element.90), channel_id=1, source_target_pairs={{0,16},{4,20},{8,24},{12,28},{16,0},{20,4},{24,8},{28,12},{1,17},{... | collective-permute-start | bytes 1572872 | tf_op jit(solution)/shard_map/ppermute | solution.py:420
  114.0 21.4 %collective-permute-start.16 = (bf16[2048,128]{1,0:T(8,128)(2,1)S(1)}, bf16[2048,128]{1,0:T(8,128)(2,1)S(1)}, u32[]{:S(2)}, u32[]{:S(2)}) collective-permute-start(bf16[2048,128]{1,0:T(8,128)(2,1)S(1)} %get-tuple-element.86), channel_id=1, source_target_pairs={{0,8},{4,12},{8,0},{12,4},{16,24},{20,28},{24,16},{28,20},{1,9},{5... | collective-permute-start | bytes 1572872 | tf_op jit(solution)/shard_map/ppermute | solution.py:420
  114.5 31.2 %collective-permute-start.22 = (bf16[2048,128]{1,0:T(8,128)(2,1)S(1)}, bf16[2048,128]{1,0:T(8,128)(2,1)S(1)}, u32[]{:S(2)}, u32[]{:S(2)}) collective-permute-start(bf16[2048,128]{1,0:T(8,128)(2,1)S(1)} %get-tuple-element.102), channel_id=1, source_target_pairs={{0,16},{4,20},{8,24},{12,28},{16,0},{20,4},{24,8},{28,12},{1,17},{... | collective-permute-start | bytes 1572872 | tf_op jit(solution)/shard_map/ppermute | solution.py:420
  118.8 13.9 %collective-permute-start.14 = (bf16[1024,128]{1,0:T(8,128)(2,1)S(1)}, bf16[1024,128]{1,0:T(8,128)(2,1)S(1)}, u32[]{:S(2)}, u32[]{:S(2)}) collective-permute-start(bf16[1024,128]{1,0:T(8,128)(2,1)S(1)} %get-tuple-element.80), channel_id=1, source_target_pairs={{0,1},{1,0},{2,3},{3,2},{4,5},{5,4},{6,7},{7,6},{8,9},{9,8},{10,11... | collective-permute-start | bytes 786440 | tf_op jit(solution)/shard_map/ppermute | solution.py:420
  131.0 11.1 %collective-permute-start.19 = (bf16[1024,128]{1,0:T(8,128)(2,1)S(1)}, bf16[1024,128]{1,0:T(8,128)(2,1)S(1)}, u32[]{:S(2)}, u32[]{:S(2)}) collective-permute-start(bf16[1024,128]{1,0:T(8,128)(2,1)S(1)} %get-tuple-element.93), channel_id=1, source_target_pairs={{0,1},{1,0},{2,3},{3,2},{4,5},{5,4},{6,7},{7,6},{8,9},{9,8},{10,11... | collective-permute-start | bytes 786440 | tf_op jit(solution)/shard_map/ppermute | solution.py:420
  132.7 9.5 %collective-permute-start.15 = (bf16[512,128]{1,0:T(8,128)(2,1)S(1)}, bf16[512,128]{1,0:T(8,128)(2,1)S(1)}, u32[]{:S(2)}, u32[]{:S(2)}) collective-permute-start(bf16[512,128]{1,0:T(8,128)(2,1)S(1)} %get-tuple-element.82), channel_id=1, source_target_pairs={{0,2},{1,3},{2,0},{3,1},{4,6},{5,7},{6,4},{7,5},{8,10},{9,11},{10,... | collective-permute-start | bytes 393224 | tf_op jit(solution)/shard_map/ppermute | solution.py:420
  139.2 11.8 %collective-permute-start.17 = (bf16[1024,128]{1,0:T(8,128)(2,1)S(1)}, bf16[1024,128]{1,0:T(8,128)(2,1)S(1)}, u32[]{:S(2)}, u32[]{:S(2)}) collective-permute-start(bf16[1024,128]{1,0:T(8,128)(2,1)S(1)} %get-tuple-element.89), channel_id=1, source_target_pairs={{0,1},{1,0},{2,3},{3,2},{4,5},{5,4},{6,7},{7,6},{8,9},{9,8},{10,11... | collective-permute-start | bytes 786440 | tf_op jit(solution)/shard_map/ppermute | solution.py:420
  142.3 8.7 %collective-permute-start.20 = (bf16[512,128]{1,0:T(8,128)(2,1)S(1)}, bf16[512,128]{1,0:T(8,128)(2,1)S(1)}, u32[]{:S(2)}, u32[]{:S(2)}) collective-permute-start(bf16[512,128]{1,0:T(8,128)(2,1)S(1)} %get-tuple-element.95), channel_id=1, source_target_pairs={{0,2},{1,3},{2,0},{3,1},{4,6},{5,7},{6,4},{7,5},{8,10},{9,11},{10,... | collective-permute-start | bytes 393224 | tf_op jit(solution)/shard_map/ppermute | solution.py:420
  149.6 8.7 %collective-permute-start.23 = (bf16[1024,128]{1,0:T(8,128)(2,1)S(1)}, bf16[1024,128]{1,0:T(8,128)(2,1)S(1)}, u32[]{:S(2)}, u32[]{:S(2)}) collective-permute-start(bf16[1024,128]{1,0:T(8,128)(2,1)S(1)} %get-tuple-element.105), channel_id=1, source_target_pairs={{0,1},{1,0},{2,3},{3,2},{4,5},{5,4},{6,7},{7,6},{8,9},{9,8},{10,11... | collective-permute-start | bytes 786440 | tf_op jit(solution)/shard_map/ppermute | solution.py:420
  151.0 7.3 %collective-permute-start.21 = (bf16[512,128]{1,0:T(8,128)(2,1)S(1)}, bf16[512,128]{1,0:T(8,128)(2,1)S(1)}, u32[]{:S(2)}, u32[]{:S(2)}) collective-permute-start(bf16[512,128]{1,0:T(8,128)(2,1)S(1)} %get-tuple-element.98), channel_id=1, source_target_pairs={{0,2},{1,3},{2,0},{3,1},{4,6},{5,7},{6,4},{7,5},{8,10},{9,11},{10,... | collective-permute-start | bytes 393224 | tf_op jit(solution)/shard_map/ppermute | solution.py:420
  158.3 6.3 %collective-permute-start.24 = (bf16[512,128]{1,0:T(8,128)(2,1)S(1)}, bf16[512,128]{1,0:T(8,128)(2,1)S(1)}, u32[]{:S(2)}, u32[]{:S(2)}) collective-permute-start(bf16[512,128]{1,0:T(8,128)(2,1)S(1)} %get-tuple-element.108), channel_id=1, source_target_pairs={{0,2},{1,3},{2,0},{3,1},{4,6},{5,7},{6,4},{7,5},{8,10},{9,11},{10,... | collective-permute-start | bytes 393224 | tf_op jit(solution)/shard_map/ppermute | solution.py:420
  (14 other events, 155.2 us)

commit v2 on v1

--- a/solution.py
+++ b/solution.py
@@ -285,12 +285,12 @@
     @pl.when(step == 0)
     def _():
         weight = jnp.concatenate([o0[...], o1[...], o2[...], o3[...]], axis=1)
-        total[:rows] = jnp.dot(c0[...], weight, preferred_element_type=f32)
-        total[rows:] = jnp.dot(c1[...], weight, preferred_element_type=f32)
+        context = jnp.concatenate([c0[...], c1[...]], axis=0)
+        total[...] = jnp.dot(context, weight, preferred_element_type=f32)
 
     weight = jnp.concatenate([v0[...], v1[...], v2[...], v3[...]], axis=1)
-    total[:rows] += jnp.dot(a0[...], weight, preferred_element_type=f32)
-    total[rows:] += jnp.dot(a1[...], weight, preferred_element_type=f32)
+    active = jnp.concatenate([a0[...], a1[...]], axis=0)
+    total[...] += jnp.dot(active, weight, preferred_element_type=f32)
 
     @pl.when(step == steps - 1)
     def _():
@@ -502,12 +502,9 @@
 
     blocks = me ^ (2 * chips)
     place = jnp.concatenate([blocks, line ^ (blocks >> 1)])
-    results, behind = {}, []
-    previous = None
+    results, far_sums = {}, []
     rows = active, active_other
-    for k in (0, 2, 1, 3):
-        if len(behind) == 2:
-            rows = after(rows, behind.pop(0))
+    for place_in_order, k in enumerate((0, 1, 2, 3)):
         own, hold, send = down_call(
             place,
             rows,
@@ -518,12 +515,15 @@
             quarter,
         )
         came = over_head(send, mask=1)
-        if previous is not None:
-            came = after(came, previous)
+        if place_in_order:
+            came = after(came, far_sums[max(0, place_in_order - 2)])
         own, second = sum_call(own, hold, came)
-        behind.append(second)
-        previous = over_head(second, mask=2)
-        results[k] = own, previous
+        if place_in_order == 0:
+            rows = after(rows, second)
+        far_sums.append(over_head(second, mask=2))
+        if place_in_order == 1:
+            rows = after(rows, far_sums[0])
+        results[k] = own, far_sums[-1]
     results = [results[k] for k in range(4)]
     own, send = join_call(results)
     other = over_req(send, mask=CORE)

time: 170 us -> 170 us (level); the launches traced: 168 us -> 170 us
  waiting for transfers between devices: 78.7 us -> 81.6 us
    ppermute x26, waiting for transfers between devices: 78.7 us -> 81.6 us  [swap(): return lax.ppermute(value, axis, [(i, i ^ mask) for i in range(size)])]
  transfers between devices with their start and end apart: 26 -> 26, of which waited for: 14 -> 15; matrix products, arithmetic and copies ran while one was open for 2% -> 2% of each run, Pallas kernels for 29% -> 29%
where the time goes in v2:
time: 170 us
  waiting for transfers between devices  81.6 us (48%)
  Pallas kernels  50 us (29%)
  starting transfers between devices  33.1 us (19%)
  other arithmetic  3.02 us (2%)
    ppermute x26, waiting for transfers between devices, swap(): return lax.ppermute(value, axis, [(i, i ^ mask) for i in range(size)])  81.6 us
    ppermute x26, starting transfers between devices, swap(): return lax.ppermute(value, axis, [(i, i ^ mask) for i in range(size)])  33.1 us
    pallas_call x3, Pallas kernels, up_half_call(): pl.pallas_call(up_half_kernel, grid_spec=pltpu.PrefetchScalarGridSpec(num...  16.7 us
    pallas_call x4, Pallas kernels, down_call(): pl.pallas_call(down_kernel, grid_spec=pltpu.PrefetchScalarGridSpec(num_sc...  15.2 us
    pallas_call x1, Pallas kernels, project_call(): pl.pallas_call(functools.partial(project_kernel, heads), grid=(3 * heads,...  9.42 us
    pallas_call x1, Pallas kernels, attend_call(): pl.pallas_call(functools.partial(attend_kernel, local // HD), grid_spec=p...  3.72 us
  transfers between devices with their start and end apart: 26, of which 15 were waited for; matrix products, arithmetic and copies ran while one was open for 2% of the time, Pallas kernels for 29%

profile of v2, /device:TPU:0, one launch (start us, length us, event | category | flops | bytes accessed | tf_op | source)
XLA Modules:
  0.0 169.6 jit_solution(12491852118628543846)
XLA Ops:
  0.6 3.0 %collective-permute-start.3 = (bf16[512,2048]{1,0:T(8,128)(2,1)}, bf16[512,2048]{1,0:T(8,128)(2,1)}, u32[]{:S(2)}, u32[]{:S(2)}) collective-permute-start(bf16[512,2048]{1,0:T(8,128)(2,1)} %w0.5), channel_id=1, source_target_pairs={{0,8},{4,12},{8,0},{12,4},{16,24},{20,28},{24,16},{28,20},{1,9},{5... | collective-permute-start | bytes 6291464 | tf_op jit(solution)/shard_map/ppermute | solution.py:420
  5.2 2.6 %collective-permute-start = (bf16[256,1024]{1,0:T(8,128)(2,1)}, bf16[256,1024]{1,0:T(8,128)(2,1)S(1)}, u32[]{:S(2)}, u32[]{:S(2)}) collective-permute-start(bf16[256,1024]{1,0:T(8,128)(2,1)} %hidden_ref.1), channel_id=1, source_target_pairs={{0,2},{1,3},{2,0},{3,1},{4,6},{5,7},{6,4},{7,5},{8,10},{9,11},{10,... | collective-permute-start | bytes 1572872 | tf_op jit(solution)/shard_map/ppermute | solution.py:420
  9.3 22.3 %collective-permute-done.refs_1_ = bf16[256,1024]{1,0:T(8,128)(2,1)S(1)} collective-permute-done((bf16[256,1024]{1,0:T(8,128)(2,1)}, bf16[256,1024]{1,0:T(8,128)(2,1)S(1)}, u32[]{:S(2)}, u32[]{:S(2)}) %collective-permute-start) | collective-permute-done | bytes 524320 | tf_op jit(solution)/shard_map/ppermute | solution.py:420
  34.7 10.2 %collective-permute-done.1.refs_2_ = bf16[256,1024]{1,0:T(8,128)(2,1)S(1)} collective-permute-done((bf16[256,1024]{1,0:T(8,128)(2,1)S(1)}, bf16[256,1024]{1,0:T(8,128)(2,1)S(1)}, u32[]{:S(2)}, u32[]{:S(2)}) %collective-permute-start.1) | collective-permute-done | bytes 524320 | tf_op jit(solution)/shard_map/ppermute | solution.py:420
  44.8 2.7 %layer_norm.1 = (bf16[256,4096]{1,0:T(8,128)(2,1)S(1)}, bf16[256,2048]{1,0:T(8,128)(2,1)S(1)}) custom-call(s32[5]{0:T(128)S(1)} %pad_add_fusion.1.order_ref, bf16[256,2048]{1,0:T(8,128)(2,1)S(1)} %pad_maximum_fusion.refs_0_, bf16[256,1024]{1,0:T(8,128)(2,1)S(1)} %collective-permute-done.refs_1_, bf16[256,1024]{1,0:T(8,128)(2,1)S(1)} %collective-permute-done.1.refs_2_, ...), custom_call_target="tpu_custom_call" | custom-call | flops 1024 | bytes 1024 | tf_op jit(solution)/shard_map/layer_norm/pallas_call | solution.py:60
  47.6 2.0 %collective-permute-done.3.w1 = bf16[512,2048]{1,0:T(8,128)(2,1)} collective-permute-done((bf16[512,2048]{1,0:T(8,128)(2,1)}, bf16[512,2048]{1,0:T(8,128)(2,1)}, u32[]{:S(2)}, u32[]{:S(2)}) %collective-permute-start.3) | collective-permute-done | bytes 2097184 | tf_op jit(solution)/shard_map/ppermute | solution.py:420
  49.6 2.3 %collective-permute-done.5.v2 = bf16[2048,512]{1,0:T(8,128)(2,1)S(1)} collective-permute-done((bf16[2048,512]{1,0:T(8,128)(2,1)}, bf16[2048,512]{1,0:T(8,128)(2,1)S(1)}, u32[]{:S(2)}, u32[]{:S(2)}) %collective-permute-start.5) | collective-permute-done | bytes 2097184 | tf_op jit(solution)/shard_map/ppermute | solution.py:420
  55.6 9.4 %projections.1 = (bf16[256,512]{1,0:T(8,128)(2,1)S(1)}, bf16[256,512]{1,0:T(8,128)(2,1)}, bf16[256,512]{1,0:T(8,128)(2,1)}) custom-call(bf16[256,4096]{1,0:T(8,128)(2,1)S(1)} %get-tuple-element.65.x_ref.rows_ref, bf16[3,4096,512]{2,1,0:T(8,128)(2,1)} %bitcast.15, f32[256,128]{1,0:T(8,128)S(1)} %get-tuple-element.117.a_ref, ...), custom_call_target="tpu_custom_call" | custom-call | flops 1024 | bytes 1024 | tf_op jit(solution)/shard_map/projections/pallas_call | solution.py:114
  65.0 7.4 %up_half.3.keep_ref = f32[256,2048]{1,0:T(8,128)S(1)} custom-call(s32[4]{0:T(128)S(1)} %get-tuple-element.119.spots_ref, bf16[256,4096]{1,0:T(8,128)(2,1)S(1)} %get-tuple-element.65.x_ref.rows_ref, bf16[512,2048]{1,0:T(8,128)(2,1)S(1)} %copy-done.2, bf16[512,2048]{1,0:T(8,128)(2,1)} %collective-permute-done.3.w1, ...), custom_call_target="tpu_custom_call" | custom-call | flops 1024 | bytes 1024 | tf_op jit(solution)/shard_map/up_half/pallas_call | solution.py:237
  72.4 5.2 %collective-permute-done.7.rows_ref = bf16[256,2048]{1,0:T(8,128)(2,1)S(1)} collective-permute-done((bf16[256,2048]{1,0:T(8,128)(2,1)S(1)}, bf16[256,2048]{1,0:T(8,128)(2,1)S(1)}, u32[]{:S(2)}, u32[]{:S(2)}) %collective-permute-start.7) | collective-permute-done | bytes 1048608 | tf_op jit(solution)/shard_map/ppermute | solution.py:420
  77.6 5.3 %up_half.4 = bf16[256,1280]{1,0:T(8,128)(2,1)S(1)} custom-call(s32[4]{0:T(128)S(1)} %get-tuple-element.118.spots_ref, bf16[256,2048]{1,0:T(8,128)(2,1)S(1)} %collective-permute-done.7.rows_ref, bf16[512,2048]{1,0:T(8,128)(2,1)S(1)} %copy-done.2, bf16[512,2048]{1,0:T(8,128)(2,1)} %collective-permute-done.3.w1, bf16[512,2048]{1,0:T(8,128)(2,1)} %collective-permute-done.4.w2, ...), custom_call_target="tpu_custom_call" | custom-call | flops 1024 | bytes 1024 | tf_op jit(solution)/shard_map/up_half/pallas_call | solution.py:237
  86.1 4.0 %up_half.5 = bf16[256,768]{1,0:T(8,128)(2,1)S(1)} custom-call(s32[4]{0:T(128)S(1)} %get-tuple-element.118.spots_ref, bf16[256,2048]{1,0:T(8,128)(2,1)S(1)} %collective-permute-done.7.rows_ref, bf16[512,2048]{1,0:T(8,128)(2,1)S(1)} %copy-done.2, bf16[512,2048]{1,0:T(8,128)(2,1)} %collective-permute-done.3.w1, bf16[512,2048]{1,0:T(8,128)(2,1)} %collective-permute-done.4.w2, ...), custom_call_target="tpu_custom_call" | custom-call | flops 1024 | bytes 1024 | tf_op jit(solution)/shard_map/up_half/pallas_call | solution.py:237
  90.8 3.7 %attention.1.c0 = bf16[256,512]{1,0:T(8,128)(2,1)S(1)} custom-call(s32[2]{0:T(128)S(1)} %copy-done.10, bf16[256,512]{1,0:T(8,128)(2,1)S(1)} %get-tuple-element.64.q_ref, bf16[256,512]{1,0:T(8,128)(2,1)S(1)} %copy-done.6, bf16[256,512]{1,0:T(8,128)(2,1)S(1)} %copy-done.7, bf16[2,1536,512]{2,1,0:T(8,128)(2,1)S(1)} %copy-done.3, bf16[2,1536,512]{2,1,0:T(8,128)(2,1)S(1)} %copy-done.4), custom_call_target="tpu_custom_call" | custom-call | flops 1024 | bytes 1024 | tf_op jit(solution)/shard_map/attention/pallas_call | solution.py:168
  96.1 15.2 %collective-permute-done.11.v3 = bf16[2048,128]{1,0:T(8,128)(2,1)S(1)} collective-permute-done((bf16[2048,128]{1,0:T(8,128)(2,1)}, bf16[2048,128]{1,0:T(8,128)(2,1)S(1)}, u32[]{:S(2)}, u32[]{:S(2)}) %collective-permute-start.11) | collective-permute-done | bytes 524320 | tf_op jit(solution)/shard_map/ppermute | solution.py:420
  115.0 3.8 %down_and_output.4 = (f32[512,128]{1,0:T(8,128)S(1)}, f32[512,128]{1,0:T(8,128)S(1)}, bf16[1024,128]{1,0:T(8,128)(2,1)S(1)}) custom-call(s32[8]{0:T(128)S(1)} %pad_add_fusion.place_ref, bf16[256,2048]{1,0:T(8,128)(2,1)S(1)} %gelu.1.a0, bf16[256,2048]{1,0:T(8,128)(2,1)S(1)} %collective-permute-done.12.a1, bf16[256,512]{1,0:T(8,128)(2,1)S(1)} %attention.1.c0, ...), custom_call_target="tpu_custom_call" | custom-call | flops 1024 | bytes 1024 | tf_op jit(solution)/shard_map/down_and_output/pallas_call | solution.py:335
  120.6 6.6 %collective-permute-done.14.came_ref = bf16[1024,128]{1,0:T(8,128)(2,1)S(1)} collective-permute-done((bf16[1024,128]{1,0:T(8,128)(2,1)S(1)}, bf16[1024,128]{1,0:T(8,128)(2,1)S(1)}, u32[]{:S(2)}, u32[]{:S(2)}) %collective-permute-start.14) | collective-permute-done | bytes 262176 | tf_op jit(solution)/shard_map/ppermute | solution.py:420
  127.2 2.7 %collective-permute-start.15 = (bf16[512,128]{1,0:T(8,128)(2,1)S(1)}, bf16[512,128]{1,0:T(8,128)(2,1)S(1)}, u32[]{:S(2)}, u32[]{:S(2)}) collective-permute-start(bf16[512,128]{1,0:T(8,128)(2,1)S(1)} %get-tuple-element.82), channel_id=1, source_target_pairs={{0,2},{1,3},{2,0},{3,1},{4,6},{5,7},{6,4},{7,5},{8,10},{9,11},{10,... | collective-permute-start | bytes 393224 | tf_op jit(solution)/shard_map/ppermute | solution.py:420
  129.9 3.8 %down_and_output.5 = (f32[512,128]{1,0:T(8,128)S(1)}, f32[512,128]{1,0:T(8,128)S(1)}, bf16[1024,128]{1,0:T(8,128)(2,1)S(1)}) custom-call(s32[8]{0:T(128)S(1)} %pad_add_fusion.place_ref, bf16[256,2048]{1,0:T(8,128)(2,1)S(1)} %gelu.1.a0, bf16[256,2048]{1,0:T(8,128)(2,1)S(1)} %collective-permute-done.12.a1, bf16[256,512]{1,0:T(8,128)(2,1)S(1)} %attention.1.c0, ...), custom_call_target="tpu_custom_call" | custom-call | flops 1024 | bytes 1024 | tf_op jit(solution)/shard_map/down_and_output/pallas_call | solution.py:335
  135.8 3.8 %down_and_output.6 = (f32[512,128]{1,0:T(8,128)S(1)}, f32[512,128]{1,0:T(8,128)S(1)}, bf16[1024,128]{1,0:T(8,128)(2,1)S(1)}) custom-call(s32[8]{0:T(128)S(1)} %pad_add_fusion.place_ref, bf16[256,2048]{1,0:T(8,128)(2,1)S(1)} %gelu.1.a0, bf16[256,2048]{1,0:T(8,128)(2,1)S(1)} %collective-permute-done.12.a1, bf16[256,512]{1,0:T(8,128)(2,1)S(1)} %attention.1.c0, ...), custom_call_target="tpu_custom_call" | custom-call | flops 1024 | bytes 1024 | tf_op jit(solution)/shard_map/down_and_output/pallas_call | solution.py:335
  140.1 3.8 %down_and_output.7 = (f32[512,128]{1,0:T(8,128)S(1)}, f32[512,128]{1,0:T(8,128)S(1)}, bf16[1024,128]{1,0:T(8,128)(2,1)S(1)}) custom-call(s32[8]{0:T(128)S(1)} %pad_add_fusion.place_ref, bf16[256,2048]{1,0:T(8,128)(2,1)S(1)} %gelu.1.a0, bf16[256,2048]{1,0:T(8,128)(2,1)S(1)} %collective-permute-done.12.a1, bf16[256,512]{1,0:T(8,128)(2,1)S(1)} %attention.1.c0, ...), custom_call_target="tpu_custom_call" | custom-call | flops 1024 | bytes 1024 | tf_op jit(solution)/shard_map/down_and_output/pallas_call | solution.py:335
  149.5 3.7 %collective-permute-start.21 = (bf16[512,128]{1,0:T(8,128)(2,1)S(1)}, bf16[512,128]{1,0:T(8,128)(2,1)S(1)}, u32[]{:S(2)}, u32[]{:S(2)}) collective-permute-start(bf16[512,128]{1,0:T(8,128)(2,1)S(1)} %get-tuple-element.101), channel_id=1, source_target_pairs={{0,2},{1,3},{2,0},{3,1},{4,6},{5,7},{6,4},{7,5},{8,10},{9,11},{10,... | collective-permute-start | bytes 393224 | tf_op jit(solution)/shard_map/ppermute | solution.py:420
  155.2 2.4 %collective-permute-done.23.came_ref = bf16[1024,128]{1,0:T(8,128)(2,1)S(1)} collective-permute-done((bf16[1024,128]{1,0:T(8,128)(2,1)S(1)}, bf16[1024,128]{1,0:T(8,128)(2,1)S(1)}, u32[]{:S(2)}, u32[]{:S(2)}) %collective-permute-start.23) | collective-permute-done | bytes 262176 | tf_op jit(solution)/shard_map/ppermute | solution.py:420
  158.8 4.1 %collective-permute-done.21.refs_5_ = bf16[512,128]{1,0:T(8,128)(2,1)S(1)} collective-permute-done((bf16[512,128]{1,0:T(8,128)(2,1)S(1)}, bf16[512,128]{1,0:T(8,128)(2,1)S(1)}, u32[]{:S(2)}, u32[]{:S(2)}) %collective-permute-start.21) | collective-permute-done | bytes 131104 | tf_op jit(solution)/shard_map/ppermute | solution.py:420
  162.9 3.6 %collective-permute-done.24.refs_7_ = bf16[512,128]{1,0:T(8,128)(2,1)S(1)} collective-permute-done((bf16[512,128]{1,0:T(8,128)(2,1)S(1)}, bf16[512,128]{1,0:T(8,128)(2,1)S(1)}, u32[]{:S(2)}, u32[]{:S(2)}) %collective-permute-start.24) | collective-permute-done | bytes 131104 | tf_op jit(solution)/shard_map/ppermute | solution.py:420
  (82 shorter events, 35.1 us)
Async XLA Ops:
  0.6 49.0 %collective-permute-start.3 = (bf16[512,2048]{1,0:T(8,128)(2,1)}, bf16[512,2048]{1,0:T(8,128)(2,1)}, u32[]{:S(2)}, u32[]{:S(2)}) collective-permute-start(bf16[512,2048]{1,0:T(8,128)(2,1)} %w0.5), channel_id=1, source_target_pairs={{0,8},{4,12},{8,0},{12,4},{16,24},{20,28},{24,16},{28,20},{1,9},{5... | collective-permute-start | bytes 6291464 | tf_op jit(solution)/shard_map/ppermute | solution.py:420
  3.6 46.0 %collective-permute-start.4 = (bf16[512,2048]{1,0:T(8,128)(2,1)}, bf16[512,2048]{1,0:T(8,128)(2,1)}, u32[]{:S(2)}, u32[]{:S(2)}) collective-permute-start(bf16[512,2048]{1,0:T(8,128)(2,1)} %w0.5), channel_id=1, source_target_pairs={{0,4},{4,0},{8,12},{12,8},{16,20},{20,16},{24,28},{28,24},{1,5},{5... | collective-permute-start | bytes 6291464 | tf_op jit(solution)/shard_map/ppermute | solution.py:420
  3.6 48.3 %collective-permute-start.5 = (bf16[2048,512]{1,0:T(8,128)(2,1)}, bf16[2048,512]{1,0:T(8,128)(2,1)S(1)}, u32[]{:S(2)}, u32[]{:S(2)}) collective-permute-start(bf16[2048,512]{1,0:T(8,128)(2,1)} %v0.7), channel_id=1, source_target_pairs={{0,16},{4,20},{8,24},{12,28},{16,0},{20,4},{24,8},{28,12},{1,17},{... | collective-permute-start | bytes 6291464 | tf_op jit(solution)/shard_map/ppermute | solution.py:420
  5.2 26.5 %collective-permute-start = (bf16[256,1024]{1,0:T(8,128)(2,1)}, bf16[256,1024]{1,0:T(8,128)(2,1)S(1)}, u32[]{:S(2)}, u32[]{:S(2)}) collective-permute-start(bf16[256,1024]{1,0:T(8,128)(2,1)} %hidden_ref.1), channel_id=1, source_target_pairs={{0,2},{1,3},{2,0},{3,1},{4,6},{5,7},{6,4},{7,5},{8,10},{9,11},{10,... | collective-permute-start | bytes 1572872 | tf_op jit(solution)/shard_map/ppermute | solution.py:420
  7.7 25.5 %collective-permute-start.2 = (bf16[256,1024]{1,0:T(8,128)(2,1)}, bf16[256,1024]{1,0:T(8,128)(2,1)}, u32[]{:S(2)}, u32[]{:S(2)}) collective-permute-start(bf16[256,1024]{1,0:T(8,128)(2,1)} %hidden_ref.1), channel_id=1, source_target_pairs={{0,1},{1,0},{2,3},{3,2},{4,5},{5,4},{6,7},{7,6},{8,9},{9,8},{10,11... | collective-permute-start | bytes 1572872 | tf_op jit(solution)/shard_map/ppermute | solution.py:420
  31.7 13.2 %collective-permute-start.1 = (bf16[256,1024]{1,0:T(8,128)(2,1)S(1)}, bf16[256,1024]{1,0:T(8,128)(2,1)S(1)}, u32[]{:S(2)}, u32[]{:S(2)}) collective-permute-start(bf16[256,1024]{1,0:T(8,128)(2,1)S(1)} %collective-permute-done.refs_1_), channel_id=1, source_target_pairs={{0,1},{1,0},{2,3},{3,2},{4,5},{5,4},{6,7},{7,6},{8,9},{9,8},{10,11... | collective-permute-start | bytes 1572872 | tf_op jit(solution)/shard_map/ppermute | solution.py:420
  51.9 13.1 %collective-permute-start.6 = (bf16[512,2048]{1,0:T(8,128)(2,1)}, bf16[512,2048]{1,0:T(8,128)(2,1)S(1)}, u32[]{:S(2)}, u32[]{:S(2)}) collective-permute-start(bf16[512,2048]{1,0:T(8,128)(2,1)} %collective-permute-done.3.w1), channel_id=1, source_target_pairs={{0,4},{4,0},{8,12},{12,8},{16,20},{20,16},{24,28},{28,24},{1,5},{5... | collective-permute-start | bytes 6291464 | tf_op jit(solution)/shard_map/ppermute | solution.py:420
  51.9 60.8 %collective-permute-start.13 = (bf16[2048,512]{1,0:T(8,128)(2,1)S(1)}, bf16[2048,512]{1,0:T(8,128)(2,1)S(1)}, u32[]{:S(2)}, u32[]{:S(2)}) collective-permute-start(bf16[2048,512]{1,0:T(8,128)(2,1)S(1)} %copy-done.1), channel_id=1, source_target_pairs={{0,8},{4,12},{8,0},{12,4},{16,24},{20,28},{24,16},{28,20},{1,9},{5... | collective-permute-start | bytes 6291464 | tf_op jit(solution)/shard_map/ppermute | solution.py:420
  52.3 25.3 %collective-permute-start.7 = (bf16[256,2048]{1,0:T(8,128)(2,1)S(1)}, bf16[256,2048]{1,0:T(8,128)(2,1)S(1)}, u32[]{:S(2)}, u32[]{:S(2)}) collective-permute-start(bf16[256,2048]{1,0:T(8,128)(2,1)S(1)} %get-tuple-element.68), channel_id=1, source_target_pairs={{0,16},{4,20},{8,24},{12,28},{16,0},{20,4},{24,8},{28,12},{1,17},{... | collective-permute-start | bytes 3145736 | tf_op jit(solution)/shard_map/ppermute | solution.py:420
  82.9 28.3 %collective-permute-start.8 = (bf16[256,1280]{1,0:T(8,128)(2,1)S(1)}, bf16[256,1280]{1,0:T(8,128)(2,1)S(1)}, u32[]{:S(2)}, u32[]{:S(2)}) collective-permute-start(bf16[256,1280]{1,0:T(8,128)(2,1)S(1)} %up_half.4), channel_id=1, source_target_pairs={{0,16},{4,20},{8,24},{12,28},{16,0},{20,4},{24,8},{28,12},{1,17},{... | collective-permute-start | bytes 1966088 | tf_op jit(solution)/shard_map/ppermute | solution.py:420
  84.7 26.6 %collective-permute-start.11 = (bf16[2048,128]{1,0:T(8,128)(2,1)}, bf16[2048,128]{1,0:T(8,128)(2,1)S(1)}, u32[]{:S(2)}, u32[]{:S(2)}) collective-permute-start(bf16[2048,128]{1,0:T(8,128)(2,1)} %get-tuple-element.114), channel_id=1, source_target_pairs={{0,8},{4,12},{8,0},{12,4},{16,24},{20,28},{24,16},{28,20},{1,9},{5... | collective-permute-start | bytes 1572872 | tf_op jit(solution)/shard_map/ppermute | solution.py:420
  90.2 21.1 %collective-permute-start.9 = (bf16[256,768]{1,0:T(8,128)(2,1)S(1)}, bf16[256,768]{1,0:T(8,128)(2,1)S(1)}, u32[]{:S(2)}, u32[]{:S(2)}) collective-permute-start(bf16[256,768]{1,0:T(8,128)(2,1)S(1)} %up_half.5), channel_id=1, source_target_pairs={{0,16},{4,20},{8,24},{12,28},{16,0},{20,4},{24,8},{28,12},{1,17},{... | collective-permute-start | bytes 1179656 | tf_op jit(solution)/shard_map/ppermute | solution.py:420
  112.2 2.7 %collective-permute-start.12 = (bf16[256,2048]{1,0:T(8,128)(2,1)S(1)}, bf16[256,2048]{1,0:T(8,128)(2,1)S(1)}, u32[]{:S(2)}, u32[]{:S(2)}) collective-permute-start(bf16[256,2048]{1,0:T(8,128)(2,1)S(1)} %gelu.1.a0), channel_id=1, source_target_pairs={{0,4},{4,0},{8,12},{12,8},{16,20},{20,16},{24,28},{28,24},{1,5},{5... | collective-permute-start | bytes 3145736 | tf_op jit(solution)/shard_map/ppermute | solution.py:420
  112.3 17.6 %collective-permute-start.16 = (bf16[2048,128]{1,0:T(8,128)(2,1)S(1)}, bf16[2048,128]{1,0:T(8,128)(2,1)S(1)}, u32[]{:S(2)}, u32[]{:S(2)}) collective-permute-start(bf16[2048,128]{1,0:T(8,128)(2,1)S(1)} %get-tuple-element.86), channel_id=1, source_target_pairs={{0,8},{4,12},{8,0},{12,4},{16,24},{20,28},{24,16},{28,20},{1,9},{5... | collective-permute-start | bytes 1572872 | tf_op jit(solution)/shard_map/ppermute | solution.py:420
  112.8 23.0 %collective-permute-start.19 = (bf16[2048,128]{1,0:T(8,128)(2,1)S(1)}, bf16[2048,128]{1,0:T(8,128)(2,1)S(1)}, u32[]{:S(2)}, u32[]{:S(2)}) collective-permute-start(bf16[2048,128]{1,0:T(8,128)(2,1)S(1)} %get-tuple-element.95), channel_id=1, source_target_pairs={{0,16},{4,20},{8,24},{12,28},{16,0},{20,4},{24,8},{28,12},{1,17},{... | collective-permute-start | bytes 1572872 | tf_op jit(solution)/shard_map/ppermute | solution.py:420
  114.6 25.5 %collective-permute-start.22 = (bf16[2048,128]{1,0:T(8,128)(2,1)S(1)}, bf16[2048,128]{1,0:T(8,128)(2,1)S(1)}, u32[]{:S(2)}, u32[]{:S(2)}) collective-permute-start(bf16[2048,128]{1,0:T(8,128)(2,1)S(1)} %get-tuple-element.102), channel_id=1, source_target_pairs={{0,16},{4,20},{8,24},{12,28},{16,0},{20,4},{24,8},{28,12},{1,17},{... | collective-permute-start | bytes 1572872 | tf_op jit(solution)/shard_map/ppermute | solution.py:420
  118.8 8.4 %collective-permute-start.14 = (bf16[1024,128]{1,0:T(8,128)(2,1)S(1)}, bf16[1024,128]{1,0:T(8,128)(2,1)S(1)}, u32[]{:S(2)}, u32[]{:S(2)}) collective-permute-start(bf16[1024,128]{1,0:T(8,128)(2,1)S(1)} %get-tuple-element.80), channel_id=1, source_target_pairs={{0,1},{1,0},{2,3},{3,2},{4,5},{5,4},{6,7},{7,6},{8,9},{9,8},{10,11... | collective-permute-start | bytes 786440 | tf_op jit(solution)/shard_map/ppermute | solution.py:420
  127.2 8.5 %collective-permute-start.15 = (bf16[512,128]{1,0:T(8,128)(2,1)S(1)}, bf16[512,128]{1,0:T(8,128)(2,1)S(1)}, u32[]{:S(2)}, u32[]{:S(2)}) collective-permute-start(bf16[512,128]{1,0:T(8,128)(2,1)S(1)} %get-tuple-element.82), channel_id=1, source_target_pairs={{0,2},{1,3},{2,0},{3,1},{4,6},{5,7},{6,4},{7,5},{8,10},{9,11},{10,... | collective-permute-start | bytes 393224 | tf_op jit(solution)/shard_map/ppermute | solution.py:420
  133.7 11.9 %collective-permute-start.17 = (bf16[1024,128]{1,0:T(8,128)(2,1)S(1)}, bf16[1024,128]{1,0:T(8,128)(2,1)S(1)}, u32[]{:S(2)}, u32[]{:S(2)}) collective-permute-start(bf16[1024,128]{1,0:T(8,128)(2,1)S(1)} %get-tuple-element.89), channel_id=1, source_target_pairs={{0,1},{1,0},{2,3},{3,2},{4,5},{5,4},{6,7},{7,6},{8,9},{9,8},{10,11... | collective-permute-start | bytes 786440 | tf_op jit(solution)/shard_map/ppermute | solution.py:420
  139.6 9.9 %collective-permute-start.20 = (bf16[1024,128]{1,0:T(8,128)(2,1)S(1)}, bf16[1024,128]{1,0:T(8,128)(2,1)S(1)}, u32[]{:S(2)}, u32[]{:S(2)}) collective-permute-start(bf16[1024,128]{1,0:T(8,128)(2,1)S(1)} %get-tuple-element.98), channel_id=1, source_target_pairs={{0,1},{1,0},{2,3},{3,2},{4,5},{5,4},{6,7},{7,6},{8,9},{9,8},{10,11... | collective-permute-start | bytes 786440 | tf_op jit(solution)/shard_map/ppermute | solution.py:420
  143.9 13.7 %collective-permute-start.23 = (bf16[1024,128]{1,0:T(8,128)(2,1)S(1)}, bf16[1024,128]{1,0:T(8,128)(2,1)S(1)}, u32[]{:S(2)}, u32[]{:S(2)}) collective-permute-start(bf16[1024,128]{1,0:T(8,128)(2,1)S(1)} %get-tuple-element.105), channel_id=1, source_target_pairs={{0,1},{1,0},{2,3},{3,2},{4,5},{5,4},{6,7},{7,6},{8,9},{9,8},{10,11... | collective-permute-start | bytes 786440 | tf_op jit(solution)/shard_map/ppermute | solution.py:420
  145.7 9.6 %collective-permute-start.18 = (bf16[512,128]{1,0:T(8,128)(2,1)S(1)}, bf16[512,128]{1,0:T(8,128)(2,1)S(1)}, u32[]{:S(2)}, u32[]{:S(2)}) collective-permute-start(bf16[512,128]{1,0:T(8,128)(2,1)S(1)} %get-tuple-element.92), channel_id=1, source_target_pairs={{0,2},{1,3},{2,0},{3,1},{4,6},{5,7},{6,4},{7,5},{8,10},{9,11},{10,... | collective-permute-start | bytes 393224 | tf_op jit(solution)/shard_map/ppermute | solution.py:420
  149.5 13.4 %collective-permute-start.21 = (bf16[512,128]{1,0:T(8,128)(2,1)S(1)}, bf16[512,128]{1,0:T(8,128)(2,1)S(1)}, u32[]{:S(2)}, u32[]{:S(2)}) collective-permute-start(bf16[512,128]{1,0:T(8,128)(2,1)S(1)} %get-tuple-element.101), channel_id=1, source_target_pairs={{0,2},{1,3},{2,0},{3,1},{4,6},{5,7},{6,4},{7,5},{8,10},{9,11},{10,... | collective-permute-start | bytes 393224 | tf_op jit(solution)/shard_map/ppermute | solution.py:420
  157.6 8.9 %collective-permute-start.24 = (bf16[512,128]{1,0:T(8,128)(2,1)S(1)}, bf16[512,128]{1,0:T(8,128)(2,1)S(1)}, u32[]{:S(2)}, u32[]{:S(2)}) collective-permute-start(bf16[512,128]{1,0:T(8,128)(2,1)S(1)} %get-tuple-element.108), channel_id=1, source_target_pairs={{0,2},{1,3},{2,0},{3,1},{4,6},{5,7},{6,4},{7,5},{8,10},{9,11},{10,... | collective-permute-start | bytes 393224 | tf_op jit(solution)/shard_map/ppermute | solution.py:420
  (14 other events, 169.8 us)

commit v3 on v2

--- a/solution.py
+++ b/solution.py
@@ -282,42 +282,47 @@
     steps = pl.num_programs(0)
     rows, width = a0.shape[0], v0.shape[1]
 
+    weight = jnp.concatenate([v0[...], v1[...], v2[...], v3[...]], axis=1)
+    active = jnp.concatenate([a0[...], a1[...]], axis=0)
+    part = jnp.dot(active, weight, preferred_element_type=f32)
+
     @pl.when(step == 0)
     def _():
-        weight = jnp.concatenate([o0[...], o1[...], o2[...], o3[...]], axis=1)
+        out_weight = jnp.concatenate([o0[...], o1[...], o2[...], o3[...]], axis=1)
         context = jnp.concatenate([c0[...], c1[...]], axis=0)
-        total[...] = jnp.dot(context, weight, preferred_element_type=f32)
-
-    weight = jnp.concatenate([v0[...], v1[...], v2[...], v3[...]], axis=1)
-    active = jnp.concatenate([a0[...], a1[...]], axis=0)
-    total[...] += jnp.dot(active, weight, preferred_element_type=f32)
+        total[...] = part + jnp.dot(context, out_weight, preferred_element_type=f32)
+
+    @pl.when((step > 0) & (step < steps - 1))
+    def _():
+        total[...] += part
 
     @pl.when(step == steps - 1)
     def _():
         for k in range(4):
             columns = slice(k * width, (k + 1) * width)
+            found = total[:, columns] + part[:, columns]
 
             @pl.when(place_ref[4 + k] == 0)
             def _():
-                own_ref[...] = total[:, columns]
+                own_ref[...] = found
 
             @pl.when(place_ref[4 + k] == 1)
             def _():
-                send_ref[: 2 * rows] = total[:, columns].astype(bf16)
+                send_ref[: 2 * rows] = found.astype(bf16)
 
             @pl.when(place_ref[4 + k] == 2)
             def _():
-                hold_ref[...] = total[:, columns]
+                hold_ref[...] = found
 
             @pl.when(place_ref[4 + k] == 3)
             def _():
-                send_ref[2 * rows :] = total[:, columns].astype(bf16)
+                send_ref[2 * rows :] = found.astype(bf16)
 
 
 def down_call(place, active, context, weights, out_weight, start, width):
     rows, depth = active[0].shape
     local = context[0].shape[1]
-    steps = 4
+    steps = 2
     part = depth // steps
     per = out_weight.shape[1] // 8 // width
     in_specs = [pl.BlockSpec((rows, part), lambda s, place: (0, s))] * 2
@@ -460,9 +465,10 @@
     order = jnp.concatenate([line ^ chips, (1 - (me >> 2))[None]])
     normed, for_other = norm_call(order, 4, [pair, far, last], affine, split=True)
     normed_other = over_req(for_other, mask=Y)
-    up_x, up_core, down_y, normed_next = lax.optimization_barrier((up_x, up_core, down_y, normed))
+    up_x, up_core, normed_next = lax.optimization_barrier((up_x, up_core, normed))
     up_x_core = over_req(up_x, mask=CORE)
     down_x = over_req(after(down_weight, up_x), mask=X)
+    down_y, normed_next = lax.optimization_barrier((down_y, normed_next))
 
     half = down_weight.shape[1] // 2
     quarter = half // 2
@@ -481,24 +487,24 @@
     keep = up_half_call(blocks, after(normed, query), weights, 0, units, f32)
     other = after(normed_other, keep)
     came = []
-    cut = units * 5 // 8
-    for start, stop in ((0, cut), (cut, units)):
+    cuts = [0, units * 5 // 8, units]
+    for start, stop in zip(cuts, cuts[1:]):
         send = up_half_call(blocks & 3, other, weights, start, stop, bf16)
         came.append(over_req(send, mask=Y))
         other = after(other, send)
 
-    query = after(query, other)
+    query = after(query, send)
     context = attend_call(cached_len, query, new_key, new_value, key_cache, value_cache)
     context_other = over_req(context, mask=CORE)
 
-    came, context_other, diagonal[0] = lax.optimization_barrier((came, context_other, diagonal[0]))
+    came, context_other = lax.optimization_barrier((came, context_other))
     diagonal.append(over_req(after(forward_y[1], diagonal[0]), mask=X))
     forward_x = [down_x[:, half + k * quarter : half + (k + 1) * quarter] for k in range(2)]
     forward_x = after(forward_x, came)
     diagonal += [over_req(part, mask=Y) for part in forward_x]
 
     active = gelu_call(keep, came, up_bias)
-    active_other = over_req(active, mask=CORE)
+    active_other = over_req(after(active, diagonal[0]), mask=CORE)
 
     blocks = me ^ (2 * chips)
     place = jnp.concatenate([blocks, line ^ (blocks >> 1)])

time: 170 us -> 169 us (level)
  transfers between devices with their start and end apart: 26 -> 26, of which waited for: 15 -> 15; matrix products, arithmetic and copies ran while one was open for 2% -> 2% of each run, Pallas kernels for 29% -> 28%
where the time goes in v3:
time: 169 us; the launch traced here: 168 us
  waiting for transfers between devices  81.3 us (48%)
  Pallas kernels  48.7 us (29%)
  starting transfers between devices  33.3 us (20%)
  other arithmetic  3.02 us (2%)
    ppermute x26, waiting for transfers between devices, swap(): return lax.ppermute(value, axis, [(i, i ^ mask) for i in range(size)])  81.3 us
    ppermute x26, starting transfers between devices, swap(): return lax.ppermute(value, axis, [(i, i ^ mask) for i in range(size)])  33.3 us
    pallas_call x3, Pallas kernels, up_half_call(): pl.pallas_call(up_half_kernel, grid_spec=pltpu.PrefetchScalarGridSpec(num...  16.7 us
    pallas_call x4, Pallas kernels, down_call(): pl.pallas_call(down_kernel, grid_spec=pltpu.PrefetchScalarGridSpec(num_sc...  14 us
    pallas_call x1, Pallas kernels, project_call(): pl.pallas_call(functools.partial(project_kernel, heads), grid=(3 * heads,...  9.42 us
    pallas_call x1, Pallas kernels, attend_call(): pl.pallas_call(functools.partial(attend_kernel, local // HD), grid_spec=p...  3.72 us
  transfers between devices with their start and end apart: 26, of which 15 were waited for; matrix products, arithmetic and copies ran while one was open for 2% of the time, Pallas kernels for 28%

profile of v3, /device:TPU:0, one launch (start us, length us, event | category | flops | bytes accessed | tf_op | source)
XLA Modules:
  0.0 168.2 jit_solution(10996146805492171507)
XLA Ops:
  0.6 3.0 %collective-permute-start.4 = (bf16[512,2048]{1,0:T(8,128)(2,1)}, bf16[512,2048]{1,0:T(8,128)(2,1)}, u32[]{:S(2)}, u32[]{:S(2)}) collective-permute-start(bf16[512,2048]{1,0:T(8,128)(2,1)} %w0.5), channel_id=1, source_target_pairs={{0,8},{4,12},{8,0},{12,4},{16,24},{20,28},{24,16},{28,20},{1,9},{5... | collective-permute-start | bytes 6291464 | tf_op jit(solution)/shard_map/ppermute | solution.py:425
  3.6 2.6 %collective-permute-start = (bf16[256,1024]{1,0:T(8,128)(2,1)}, bf16[256,1024]{1,0:T(8,128)(2,1)S(1)}, u32[]{:S(2)}, u32[]{:S(2)}) collective-permute-start(bf16[256,1024]{1,0:T(8,128)(2,1)} %hidden_ref.1), channel_id=1, source_target_pairs={{0,2},{1,3},{2,0},{3,1},{4,6},{5,7},{6,4},{7,5},{8,10},{9,11},{10,... | collective-permute-start | bytes 1572872 | tf_op jit(solution)/shard_map/ppermute | solution.py:425
  9.3 21.1 %collective-permute-done.refs_1_ = bf16[256,1024]{1,0:T(8,128)(2,1)S(1)} collective-permute-done((bf16[256,1024]{1,0:T(8,128)(2,1)}, bf16[256,1024]{1,0:T(8,128)(2,1)S(1)}, u32[]{:S(2)}, u32[]{:S(2)}) %collective-permute-start) | collective-permute-done | bytes 524320 | tf_op jit(solution)/shard_map/ppermute | solution.py:425
  33.4 10.5 %collective-permute-done.1.refs_2_ = bf16[256,1024]{1,0:T(8,128)(2,1)S(1)} collective-permute-done((bf16[256,1024]{1,0:T(8,128)(2,1)S(1)}, bf16[256,1024]{1,0:T(8,128)(2,1)S(1)}, u32[]{:S(2)}, u32[]{:S(2)}) %collective-permute-start.1) | collective-permute-done | bytes 524320 | tf_op jit(solution)/shard_map/ppermute | solution.py:425
  43.9 2.7 %layer_norm.1 = (bf16[256,4096]{1,0:T(8,128)(2,1)S(1)}, bf16[256,2048]{1,0:T(8,128)(2,1)S(1)}) custom-call(s32[5]{0:T(128)S(1)} %pad_add_fusion.1.order_ref, bf16[256,2048]{1,0:T(8,128)(2,1)S(1)} %pad_maximum_fusion.refs_0_, bf16[256,1024]{1,0:T(8,128)(2,1)S(1)} %collective-permute-done.refs_1_, bf16[256,1024]{1,0:T(8,128)(2,1)S(1)} %collective-permute-done.1.refs_2_, ...), custom_call_target="tpu_custom_call" | custom-call | flops 1024 | bytes 1024 | tf_op jit(solution)/shard_map/layer_norm/pallas_call | solution.py:60
  46.7 2.9 %collective-permute-done.4.w1 = bf16[512,2048]{1,0:T(8,128)(2,1)} collective-permute-done((bf16[512,2048]{1,0:T(8,128)(2,1)}, bf16[512,2048]{1,0:T(8,128)(2,1)}, u32[]{:S(2)}, u32[]{:S(2)}) %collective-permute-start.4) | collective-permute-done | bytes 2097184 | tf_op jit(solution)/shard_map/ppermute | solution.py:425
  53.5 3.0 %collective-permute-done.3.v2 = bf16[2048,512]{1,0:T(8,128)(2,1)S(1)} collective-permute-done((bf16[2048,512]{1,0:T(8,128)(2,1)}, bf16[2048,512]{1,0:T(8,128)(2,1)S(1)}, u32[]{:S(2)}, u32[]{:S(2)}) %collective-permute-start.3) | collective-permute-done | bytes 2097184 | tf_op jit(solution)/shard_map/ppermute | solution.py:425
  57.4 9.4 %projections.1 = (bf16[256,512]{1,0:T(8,128)(2,1)S(1)}, bf16[256,512]{1,0:T(8,128)(2,1)}, bf16[256,512]{1,0:T(8,128)(2,1)}) custom-call(bf16[256,4096]{1,0:T(8,128)(2,1)S(1)} %get-tuple-element.68.x_ref.rows_ref, bf16[3,4096,512]{2,1,0:T(8,128)(2,1)} %bitcast.15, f32[256,128]{1,0:T(8,128)S(1)} %get-tuple-element.121.a_ref, ...), custom_call_target="tpu_custom_call" | custom-call | flops 1024 | bytes 1024 | tf_op jit(solution)/shard_map/projections/pallas_call | solution.py:114
  66.8 7.4 %up_half.3.keep_ref = f32[256,2048]{1,0:T(8,128)S(1)} custom-call(s32[4]{0:T(128)S(1)} %get-tuple-element.123.spots_ref, bf16[256,4096]{1,0:T(8,128)(2,1)S(1)} %get-tuple-element.68.x_ref.rows_ref, bf16[512,2048]{1,0:T(8,128)(2,1)S(1)} %copy-done.2, bf16[512,2048]{1,0:T(8,128)(2,1)} %collective-permute-done.4.w1, ...), custom_call_target="tpu_custom_call" | custom-call | flops 1024 | bytes 1024 | tf_op jit(solution)/shard_map/up_half/pallas_call | solution.py:237
  74.2 3.7 %collective-permute-done.7.rows_ref = bf16[256,2048]{1,0:T(8,128)(2,1)S(1)} collective-permute-done((bf16[256,2048]{1,0:T(8,128)(2,1)S(1)}, bf16[256,2048]{1,0:T(8,128)(2,1)S(1)}, u32[]{:S(2)}, u32[]{:S(2)}) %collective-permute-start.7) | collective-permute-done | bytes 1048608 | tf_op jit(solution)/shard_map/ppermute | solution.py:425
  78.0 5.3 %up_half.4 = bf16[256,1280]{1,0:T(8,128)(2,1)S(1)} custom-call(s32[4]{0:T(128)S(1)} %get-tuple-element.122.spots_ref, bf16[256,2048]{1,0:T(8,128)(2,1)S(1)} %collective-permute-done.7.rows_ref, bf16[512,2048]{1,0:T(8,128)(2,1)S(1)} %copy-done.2, bf16[512,2048]{1,0:T(8,128)(2,1)} %collective-permute-done.4.w1, bf16[512,2048]{1,0:T(8,128)(2,1)} %collective-permute-done.5.w2, ...), custom_call_target="tpu_custom_call" | custom-call | flops 1024 | bytes 1024 | tf_op jit(solution)/shard_map/up_half/pallas_call | solution.py:237
  85.4 4.0 %up_half.5 = bf16[256,768]{1,0:T(8,128)(2,1)S(1)} custom-call(s32[4]{0:T(128)S(1)} %get-tuple-element.122.spots_ref, bf16[256,2048]{1,0:T(8,128)(2,1)S(1)} %collective-permute-done.7.rows_ref, bf16[512,2048]{1,0:T(8,128)(2,1)S(1)} %copy-done.2, bf16[512,2048]{1,0:T(8,128)(2,1)} %collective-permute-done.4.w1, bf16[512,2048]{1,0:T(8,128)(2,1)} %collective-permute-done.5.w2, ...), custom_call_target="tpu_custom_call" | custom-call | flops 1024 | bytes 1024 | tf_op jit(solution)/shard_map/up_half/pallas_call | solution.py:237
  90.0 3.7 %attention.1.c0 = bf16[256,512]{1,0:T(8,128)(2,1)S(1)} custom-call(s32[2]{0:T(128)S(1)} %copy-done.10, bf16[256,512]{1,0:T(8,128)(2,1)S(1)} %get-tuple-element.74.q_ref, bf16[256,512]{1,0:T(8,128)(2,1)S(1)} %copy-done.6, bf16[256,512]{1,0:T(8,128)(2,1)S(1)} %copy-done.7, bf16[2,1536,512]{2,1,0:T(8,128)(2,1)S(1)} %copy-done.3, bf16[2,1536,512]{2,1,0:T(8,128)(2,1)S(1)} %copy-done.4), custom_call_target="tpu_custom_call" | custom-call | flops 1024 | bytes 1024 | tf_op jit(solution)/shard_map/attention/pallas_call | solution.py:168
  95.3 12.1 %collective-permute-done.9.refs_1_ = bf16[256,768]{1,0:T(8,128)(2,1)S(1)} collective-permute-done((bf16[256,768]{1,0:T(8,128)(2,1)S(1)}, bf16[256,768]{1,0:T(8,128)(2,1)S(1)}, u32[]{:S(2)}, u32[]{:S(2)}) %collective-permute-start.9) | collective-permute-done | bytes 393248 | tf_op jit(solution)/shard_map/ppermute | solution.py:425
  112.9 3.4 %down_and_output.4 = (f32[512,128]{1,0:T(8,128)S(1)}, f32[512,128]{1,0:T(8,128)S(1)}, bf16[1024,128]{1,0:T(8,128)(2,1)S(1)}) custom-call(s32[8]{0:T(128)S(1)} %pad_add_fusion.place_ref, bf16[256,2048]{1,0:T(8,128)(2,1)S(1)} %gelu.1.a0, bf16[256,2048]{1,0:T(8,128)(2,1)S(1)} %collective-permute-done.12.a1, bf16[256,512]{1,0:T(8,128)(2,1)S(1)} %attention.1.c0, ...), custom_call_target="tpu_custom_call" | custom-call | flops 1024 | bytes 1024 | tf_op jit(solution)/shard_map/down_and_output/pallas_call | solution.py:340
  118.0 6.3 %collective-permute-done.14.came_ref = bf16[1024,128]{1,0:T(8,128)(2,1)S(1)} collective-permute-done((bf16[1024,128]{1,0:T(8,128)(2,1)S(1)}, bf16[1024,128]{1,0:T(8,128)(2,1)S(1)}, u32[]{:S(2)}, u32[]{:S(2)}) %collective-permute-start.14) | collective-permute-done | bytes 262176 | tf_op jit(solution)/shard_map/ppermute | solution.py:425
  124.4 2.7 %collective-permute-start.15 = (bf16[512,128]{1,0:T(8,128)(2,1)S(1)}, bf16[512,128]{1,0:T(8,128)(2,1)S(1)}, u32[]{:S(2)}, u32[]{:S(2)}) collective-permute-start(bf16[512,128]{1,0:T(8,128)(2,1)S(1)} %get-tuple-element.86), channel_id=1, source_target_pairs={{0,2},{1,3},{2,0},{3,1},{4,6},{5,7},{6,4},{7,5},{8,10},{9,11},{10,... | collective-permute-start | bytes 393224 | tf_op jit(solution)/shard_map/ppermute | solution.py:425
  127.0 3.5 %down_and_output.5 = (f32[512,128]{1,0:T(8,128)S(1)}, f32[512,128]{1,0:T(8,128)S(1)}, bf16[1024,128]{1,0:T(8,128)(2,1)S(1)}) custom-call(s32[8]{0:T(128)S(1)} %pad_add_fusion.place_ref, bf16[256,2048]{1,0:T(8,128)(2,1)S(1)} %gelu.1.a0, bf16[256,2048]{1,0:T(8,128)(2,1)S(1)} %collective-permute-done.12.a1, bf16[256,512]{1,0:T(8,128)(2,1)S(1)} %attention.1.c0, ...), custom_call_target="tpu_custom_call" | custom-call | flops 1024 | bytes 1024 | tf_op jit(solution)/shard_map/down_and_output/pallas_call | solution.py:340
  132.4 3.4 %down_and_output.7 = (f32[512,128]{1,0:T(8,128)S(1)}, f32[512,128]{1,0:T(8,128)S(1)}, bf16[1024,128]{1,0:T(8,128)(2,1)S(1)}) custom-call(s32[8]{0:T(128)S(1)} %pad_add_fusion.place_ref, bf16[256,2048]{1,0:T(8,128)(2,1)S(1)} %gelu.1.a0, bf16[256,2048]{1,0:T(8,128)(2,1)S(1)} %collective-permute-done.12.a1, bf16[256,512]{1,0:T(8,128)(2,1)S(1)} %attention.1.c0, ...), custom_call_target="tpu_custom_call" | custom-call | flops 1024 | bytes 1024 | tf_op jit(solution)/shard_map/down_and_output/pallas_call | solution.py:340
  136.6 3.6 %down_and_output.6 = (f32[512,128]{1,0:T(8,128)S(1)}, f32[512,128]{1,0:T(8,128)S(1)}, bf16[1024,128]{1,0:T(8,128)(2,1)S(1)}) custom-call(s32[8]{0:T(128)S(1)} %pad_add_fusion.place_ref, bf16[256,2048]{1,0:T(8,128)(2,1)S(1)} %gelu.1.a0, bf16[256,2048]{1,0:T(8,128)(2,1)S(1)} %collective-permute-done.12.a1, bf16[256,512]{1,0:T(8,128)(2,1)S(1)} %attention.1.c0, ...), custom_call_target="tpu_custom_call" | custom-call | flops 1024 | bytes 1024 | tf_op jit(solution)/shard_map/down_and_output/pallas_call | solution.py:340
  144.1 3.8 %collective-permute-done.23.came_ref = bf16[1024,128]{1,0:T(8,128)(2,1)S(1)} collective-permute-done((bf16[1024,128]{1,0:T(8,128)(2,1)S(1)}, bf16[1024,128]{1,0:T(8,128)(2,1)S(1)}, u32[]{:S(2)}, u32[]{:S(2)}) %collective-permute-start.23) | collective-permute-done | bytes 262176 | tf_op jit(solution)/shard_map/ppermute | solution.py:425
  148.0 2.4 %collective-permute-done.18.refs_3_ = bf16[512,128]{1,0:T(8,128)(2,1)S(1)} collective-permute-done((bf16[512,128]{1,0:T(8,128)(2,1)S(1)}, bf16[512,128]{1,0:T(8,128)(2,1)S(1)}, u32[]{:S(2)}, u32[]{:S(2)}) %collective-permute-start.18) | collective-permute-done | bytes 131104 | tf_op jit(solution)/shard_map/ppermute | solution.py:425
  150.5 3.4 %collective-permute-start.24 = (bf16[512,128]{1,0:T(8,128)(2,1)S(1)}, bf16[512,128]{1,0:T(8,128)(2,1)S(1)}, u32[]{:S(2)}, u32[]{:S(2)}) collective-permute-start(bf16[512,128]{1,0:T(8,128)(2,1)S(1)} %get-tuple-element.112), channel_id=1, source_target_pairs={{0,2},{1,3},{2,0},{3,1},{4,6},{5,7},{6,4},{7,5},{8,10},{9,11},{10,... | collective-permute-start | bytes 393224 | tf_op jit(solution)/shard_map/ppermute | solution.py:425
  154.0 9.5 %collective-permute-done.24.refs_7_ = bf16[512,128]{1,0:T(8,128)(2,1)S(1)} collective-permute-done((bf16[512,128]{1,0:T(8,128)(2,1)S(1)}, bf16[512,128]{1,0:T(8,128)(2,1)S(1)}, u32[]{:S(2)}, u32[]{:S(2)}) %collective-permute-start.24) | collective-permute-done | bytes 131104 | tf_op jit(solution)/shard_map/ppermute | solution.py:425
  (82 shorter events, 33.6 us)
Async XLA Ops:
  0.6 49.0 %collective-permute-start.4 = (bf16[512,2048]{1,0:T(8,128)(2,1)}, bf16[512,2048]{1,0:T(8,128)(2,1)}, u32[]{:S(2)}, u32[]{:S(2)}) collective-permute-start(bf16[512,2048]{1,0:T(8,128)(2,1)} %w0.5), channel_id=1, source_target_pairs={{0,8},{4,12},{8,0},{12,4},{16,24},{20,28},{24,16},{28,20},{1,9},{5... | collective-permute-start | bytes 6291464 | tf_op jit(solution)/shard_map/ppermute | solution.py:425
  3.6 46.0 %collective-permute-start.5 = (bf16[512,2048]{1,0:T(8,128)(2,1)}, bf16[512,2048]{1,0:T(8,128)(2,1)}, u32[]{:S(2)}, u32[]{:S(2)}) collective-permute-start(bf16[512,2048]{1,0:T(8,128)(2,1)} %w0.5), channel_id=1, source_target_pairs={{0,4},{4,0},{8,12},{12,8},{16,20},{20,16},{24,28},{28,24},{1,5},{5... | collective-permute-start | bytes 6291464 | tf_op jit(solution)/shard_map/ppermute | solution.py:425
  3.6 26.8 %collective-permute-start = (bf16[256,1024]{1,0:T(8,128)(2,1)}, bf16[256,1024]{1,0:T(8,128)(2,1)S(1)}, u32[]{:S(2)}, u32[]{:S(2)}) collective-permute-start(bf16[256,1024]{1,0:T(8,128)(2,1)} %hidden_ref.1), channel_id=1, source_target_pairs={{0,2},{1,3},{2,0},{3,1},{4,6},{5,7},{6,4},{7,5},{8,10},{9,11},{10,... | collective-permute-start | bytes 1572872 | tf_op jit(solution)/shard_map/ppermute | solution.py:425
  6.2 25.7 %collective-permute-start.2 = (bf16[256,1024]{1,0:T(8,128)(2,1)}, bf16[256,1024]{1,0:T(8,128)(2,1)}, u32[]{:S(2)}, u32[]{:S(2)}) collective-permute-start(bf16[256,1024]{1,0:T(8,128)(2,1)} %hidden_ref.1), channel_id=1, source_target_pairs={{0,1},{1,0},{2,3},{3,2},{4,5},{5,4},{6,7},{7,6},{8,9},{9,8},{10,11... | collective-permute-start | bytes 1572872 | tf_op jit(solution)/shard_map/ppermute | solution.py:425
  7.8 48.7 %collective-permute-start.3 = (bf16[2048,512]{1,0:T(8,128)(2,1)}, bf16[2048,512]{1,0:T(8,128)(2,1)S(1)}, u32[]{:S(2)}, u32[]{:S(2)}) collective-permute-start(bf16[2048,512]{1,0:T(8,128)(2,1)} %v0.7), channel_id=1, source_target_pairs={{0,16},{4,20},{8,24},{12,28},{16,0},{20,4},{24,8},{28,12},{1,17},{... | collective-permute-start | bytes 6291464 | tf_op jit(solution)/shard_map/ppermute | solution.py:425
  30.4 13.5 %collective-permute-start.1 = (bf16[256,1024]{1,0:T(8,128)(2,1)S(1)}, bf16[256,1024]{1,0:T(8,128)(2,1)S(1)}, u32[]{:S(2)}, u32[]{:S(2)}) collective-permute-start(bf16[256,1024]{1,0:T(8,128)(2,1)S(1)} %collective-permute-done.refs_1_), channel_id=1, source_target_pairs={{0,1},{1,0},{2,3},{3,2},{4,5},{5,4},{6,7},{7,6},{8,9},{9,8},{10,11... | collective-permute-start | bytes 1572872 | tf_op jit(solution)/shard_map/ppermute | solution.py:425
  49.6 17.2 %collective-permute-start.6 = (bf16[512,2048]{1,0:T(8,128)(2,1)}, bf16[512,2048]{1,0:T(8,128)(2,1)S(1)}, u32[]{:S(2)}, u32[]{:S(2)}) collective-permute-start(bf16[512,2048]{1,0:T(8,128)(2,1)} %collective-permute-done.4.w1), channel_id=1, source_target_pairs={{0,4},{4,0},{8,12},{12,8},{16,20},{20,16},{24,28},{28,24},{1,5},{5... | collective-permute-start | bytes 6291464 | tf_op jit(solution)/shard_map/ppermute | solution.py:425
  49.7 61.0 %collective-permute-start.13 = (bf16[2048,512]{1,0:T(8,128)(2,1)S(1)}, bf16[2048,512]{1,0:T(8,128)(2,1)S(1)}, u32[]{:S(2)}, u32[]{:S(2)}) collective-permute-start(bf16[2048,512]{1,0:T(8,128)(2,1)S(1)} %copy-done.1), channel_id=1, source_target_pairs={{0,8},{4,12},{8,0},{12,4},{16,24},{20,28},{24,16},{28,20},{1,9},{5... | collective-permute-start | bytes 6291464 | tf_op jit(solution)/shard_map/ppermute | solution.py:425
  51.4 26.5 %collective-permute-start.7 = (bf16[256,2048]{1,0:T(8,128)(2,1)S(1)}, bf16[256,2048]{1,0:T(8,128)(2,1)S(1)}, u32[]{:S(2)}, u32[]{:S(2)}) collective-permute-start(bf16[256,2048]{1,0:T(8,128)(2,1)S(1)} %get-tuple-element.71), channel_id=1, source_target_pairs={{0,16},{4,20},{8,24},{12,28},{16,0},{20,4},{24,8},{28,12},{1,17},{... | collective-permute-start | bytes 3145736 | tf_op jit(solution)/shard_map/ppermute | solution.py:425
  83.3 24.2 %collective-permute-start.8 = (bf16[256,1280]{1,0:T(8,128)(2,1)S(1)}, bf16[256,1280]{1,0:T(8,128)(2,1)S(1)}, u32[]{:S(2)}, u32[]{:S(2)}) collective-permute-start(bf16[256,1280]{1,0:T(8,128)(2,1)S(1)} %up_half.4), channel_id=1, source_target_pairs={{0,16},{4,20},{8,24},{12,28},{16,0},{20,4},{24,8},{28,12},{1,17},{... | collective-permute-start | bytes 1966088 | tf_op jit(solution)/shard_map/ppermute | solution.py:425
  84.8 24.1 %collective-permute-start.11 = (bf16[2048,128]{1,0:T(8,128)(2,1)}, bf16[2048,128]{1,0:T(8,128)(2,1)S(1)}, u32[]{:S(2)}, u32[]{:S(2)}) collective-permute-start(bf16[2048,128]{1,0:T(8,128)(2,1)} %get-tuple-element.118), channel_id=1, source_target_pairs={{0,8},{4,12},{8,0},{12,4},{16,24},{20,28},{24,16},{28,20},{1,9},{5... | collective-permute-start | bytes 1572872 | tf_op jit(solution)/shard_map/ppermute | solution.py:425
  89.4 18.1 %collective-permute-start.9 = (bf16[256,768]{1,0:T(8,128)(2,1)S(1)}, bf16[256,768]{1,0:T(8,128)(2,1)S(1)}, u32[]{:S(2)}, u32[]{:S(2)}) collective-permute-start(bf16[256,768]{1,0:T(8,128)(2,1)S(1)} %up_half.5), channel_id=1, source_target_pairs={{0,16},{4,20},{8,24},{12,28},{16,0},{20,4},{24,8},{28,12},{1,17},{... | collective-permute-start | bytes 1179656 | tf_op jit(solution)/shard_map/ppermute | solution.py:425
  108.9 4.0 %collective-permute-start.12 = (bf16[256,2048]{1,0:T(8,128)(2,1)S(1)}, bf16[256,2048]{1,0:T(8,128)(2,1)S(1)}, u32[]{:S(2)}, u32[]{:S(2)}) collective-permute-start(bf16[256,2048]{1,0:T(8,128)(2,1)S(1)} %gelu.1.a0), channel_id=1, source_target_pairs={{0,4},{4,0},{8,12},{12,8},{16,20},{20,16},{24,28},{28,24},{1,5},{5... | collective-permute-start | bytes 3145736 | tf_op jit(solution)/shard_map/ppermute | solution.py:425
  108.9 18.1 %collective-permute-start.16 = (bf16[2048,128]{1,0:T(8,128)(2,1)S(1)}, bf16[2048,128]{1,0:T(8,128)(2,1)S(1)}, u32[]{:S(2)}, u32[]{:S(2)}) collective-permute-start(bf16[2048,128]{1,0:T(8,128)(2,1)S(1)} %get-tuple-element.90), channel_id=1, source_target_pairs={{0,8},{4,12},{8,0},{12,4},{16,24},{20,28},{24,16},{28,20},{1,9},{5... | collective-permute-start | bytes 1572872 | tf_op jit(solution)/shard_map/ppermute | solution.py:425
  110.8 21.6 %collective-permute-start.22 = (bf16[2048,128]{1,0:T(8,128)(2,1)S(1)}, bf16[2048,128]{1,0:T(8,128)(2,1)S(1)}, u32[]{:S(2)}, u32[]{:S(2)}) collective-permute-start(bf16[2048,128]{1,0:T(8,128)(2,1)S(1)} %get-tuple-element.106), channel_id=1, source_target_pairs={{0,16},{4,20},{8,24},{12,28},{16,0},{20,4},{24,8},{28,12},{1,17},{... | collective-permute-start | bytes 1572872 | tf_op jit(solution)/shard_map/ppermute | solution.py:425
  112.3 24.2 %collective-permute-start.19 = (bf16[2048,128]{1,0:T(8,128)(2,1)S(1)}, bf16[2048,128]{1,0:T(8,128)(2,1)S(1)}, u32[]{:S(2)}, u32[]{:S(2)}) collective-permute-start(bf16[2048,128]{1,0:T(8,128)(2,1)S(1)} %get-tuple-element.99), channel_id=1, source_target_pairs={{0,16},{4,20},{8,24},{12,28},{16,0},{20,4},{24,8},{28,12},{1,17},{... | collective-permute-start | bytes 1572872 | tf_op jit(solution)/shard_map/ppermute | solution.py:425
  116.4 7.9 %collective-permute-start.14 = (bf16[1024,128]{1,0:T(8,128)(2,1)S(1)}, bf16[1024,128]{1,0:T(8,128)(2,1)S(1)}, u32[]{:S(2)}, u32[]{:S(2)}) collective-permute-start(bf16[1024,128]{1,0:T(8,128)(2,1)S(1)} %get-tuple-element.84), channel_id=1, source_target_pairs={{0,1},{1,0},{2,3},{3,2},{4,5},{5,4},{6,7},{7,6},{8,9},{9,8},{10,11... | collective-permute-start | bytes 786440 | tf_op jit(solution)/shard_map/ppermute | solution.py:425
  124.4 8.0 %collective-permute-start.15 = (bf16[512,128]{1,0:T(8,128)(2,1)S(1)}, bf16[512,128]{1,0:T(8,128)(2,1)S(1)}, u32[]{:S(2)}, u32[]{:S(2)}) collective-permute-start(bf16[512,128]{1,0:T(8,128)(2,1)S(1)} %get-tuple-element.86), channel_id=1, source_target_pairs={{0,2},{1,3},{2,0},{3,1},{4,6},{5,7},{6,4},{7,5},{8,10},{9,11},{10,... | collective-permute-start | bytes 393224 | tf_op jit(solution)/shard_map/ppermute | solution.py:425
  130.5 11.2 %collective-permute-start.17 = (bf16[1024,128]{1,0:T(8,128)(2,1)S(1)}, bf16[1024,128]{1,0:T(8,128)(2,1)S(1)}, u32[]{:S(2)}, u32[]{:S(2)}) collective-permute-start(bf16[1024,128]{1,0:T(8,128)(2,1)S(1)} %get-tuple-element.93), channel_id=1, source_target_pairs={{0,1},{1,0},{2,3},{3,2},{4,5},{5,4},{6,7},{7,6},{8,9},{9,8},{10,11... | collective-permute-start | bytes 786440 | tf_op jit(solution)/shard_map/ppermute | solution.py:425
  135.9 12.1 %collective-permute-start.23 = (bf16[1024,128]{1,0:T(8,128)(2,1)S(1)}, bf16[1024,128]{1,0:T(8,128)(2,1)S(1)}, u32[]{:S(2)}, u32[]{:S(2)}) collective-permute-start(bf16[1024,128]{1,0:T(8,128)(2,1)S(1)} %get-tuple-element.109), channel_id=1, source_target_pairs={{0,1},{1,0},{2,3},{3,2},{4,5},{5,4},{6,7},{7,6},{8,9},{9,8},{10,11... | collective-permute-start | bytes 786440 | tf_op jit(solution)/shard_map/ppermute | solution.py:425
  140.2 13.7 %collective-permute-start.20 = (bf16[1024,128]{1,0:T(8,128)(2,1)S(1)}, bf16[1024,128]{1,0:T(8,128)(2,1)S(1)}, u32[]{:S(2)}, u32[]{:S(2)}) collective-permute-start(bf16[1024,128]{1,0:T(8,128)(2,1)S(1)} %get-tuple-element.102), channel_id=1, source_target_pairs={{0,1},{1,0},{2,3},{3,2},{4,5},{5,4},{6,7},{7,6},{8,9},{9,8},{10,11... | collective-permute-start | bytes 786440 | tf_op jit(solution)/shard_map/ppermute | solution.py:425
  141.7 8.7 %collective-permute-start.18 = (bf16[512,128]{1,0:T(8,128)(2,1)S(1)}, bf16[512,128]{1,0:T(8,128)(2,1)S(1)}, u32[]{:S(2)}, u32[]{:S(2)}) collective-permute-start(bf16[512,128]{1,0:T(8,128)(2,1)S(1)} %get-tuple-element.96), channel_id=1, source_target_pairs={{0,2},{1,3},{2,0},{3,1},{4,6},{5,7},{6,4},{7,5},{8,10},{9,11},{10,... | collective-permute-start | bytes 393224 | tf_op jit(solution)/shard_map/ppermute | solution.py:425
  150.5 13.1 %collective-permute-start.24 = (bf16[512,128]{1,0:T(8,128)(2,1)S(1)}, bf16[512,128]{1,0:T(8,128)(2,1)S(1)}, u32[]{:S(2)}, u32[]{:S(2)}) collective-permute-start(bf16[512,128]{1,0:T(8,128)(2,1)S(1)} %get-tuple-element.112), channel_id=1, source_target_pairs={{0,2},{1,3},{2,0},{3,1},{4,6},{5,7},{6,4},{7,5},{8,10},{9,11},{10,... | collective-permute-start | bytes 393224 | tf_op jit(solution)/shard_map/ppermute | solution.py:425
  154.0 11.2 %collective-permute-start.21 = (bf16[512,128]{1,0:T(8,128)(2,1)S(1)}, bf16[512,128]{1,0:T(8,128)(2,1)S(1)}, u32[]{:S(2)}, u32[]{:S(2)}) collective-permute-start(bf16[512,128]{1,0:T(8,128)(2,1)S(1)} %get-tuple-element.105), channel_id=1, source_target_pairs={{0,2},{1,3},{2,0},{3,1},{4,6},{5,7},{6,4},{7,5},{8,10},{9,11},{10,... | collective-permute-start | bytes 393224 | tf_op jit(solution)/shard_map/ppermute | solution.py:425
  (14 other events, 169.1 us)

commit v4 on v3

--- a/solution.py
+++ b/solution.py
@@ -508,9 +508,13 @@
 
     blocks = me ^ (2 * chips)
     place = jnp.concatenate([blocks, line ^ (blocks >> 1)])
-    results, far_sums = {}, []
+    results, near_sums, far_sums = [], [], []
     rows = active, active_other
-    for place_in_order, k in enumerate((0, 1, 2, 3)):
+    for k in range(4):
+        if k >= 2:
+            rows = after(rows, near_sums[k - 2])
+        if k == 3:
+            rows = after(rows, far_sums[0])
         own, hold, send = down_call(
             place,
             rows,
@@ -520,17 +524,14 @@
             k * quarter,
             quarter,
         )
+        rows = after(rows, send)
         came = over_head(send, mask=1)
-        if place_in_order:
-            came = after(came, far_sums[max(0, place_in_order - 2)])
+        if k:
+            came = after(came, far_sums[-1])
         own, second = sum_call(own, hold, came)
-        if place_in_order == 0:
-            rows = after(rows, second)
+        near_sums.append(second)
         far_sums.append(over_head(second, mask=2))
-        if place_in_order == 1:
-            rows = after(rows, far_sums[0])
-        results[k] = own, far_sums[-1]
-    results = [results[k] for k in range(4)]
+        results.append((own, far_sums[-1]))
     own, send = join_call(results)
     other = over_req(send, mask=CORE)
     hidden_out = close_call(side[None], hidden_in, down_bias, own, other)

time: 169 us -> 167 us (0.988)
  waiting for transfers between devices: 81.3 us -> 76.8 us
  starting transfers between devices: 33.3 us -> 36 us
    ppermute x26, waiting for transfers between devices: 81.3 us -> 76.8 us  [swap(): return lax.ppermute(value, axis, [(i, i ^ mask) for i in range(size)])]
    ppermute x26, starting transfers between devices: 33.3 us -> 36 us  [swap(): return lax.ppermute(value, axis, [(i, i ^ mask) for i in range(size)])]
  transfers between devices with their start and end apart: 26 -> 26, of which waited for: 15 -> 13; matrix products, arithmetic and copies ran while one was open for 2% -> 2% of each run, Pallas kernels for 28% -> 29%
where the time goes in v4:
time: 167 us; the launch traced here: 166 us
  waiting for transfers between devices  76.8 us (46%)
  Pallas kernels  48.7 us (29%)
  starting transfers between devices  36 us (22%)
  other arithmetic  3.02 us (2%)
    ppermute x26, waiting for transfers between devices, swap(): return lax.ppermute(value, axis, [(i, i ^ mask) for i in range(size)])  76.8 us
    ppermute x26, starting transfers between devices, swap(): return lax.ppermute(value, axis, [(i, i ^ mask) for i in range(size)])  36 us
    pallas_call x3, Pallas kernels, up_half_call(): pl.pallas_call(up_half_kernel, grid_spec=pltpu.PrefetchScalarGridSpec(num...  16.7 us
    pallas_call x4, Pallas kernels, down_call(): pl.pallas_call(down_kernel, grid_spec=pltpu.PrefetchScalarGridSpec(num_sc...  13.9 us
    pallas_call x1, Pallas kernels, project_call(): pl.pallas_call(functools.partial(project_kernel, heads), grid=(3 * heads,...  9.42 us
    pallas_call x1, Pallas kernels, attend_call(): pl.pallas_call(functools.partial(attend_kernel, local // HD), grid_spec=p...  3.72 us
  transfers between devices with their start and end apart: 26, of which 13 were waited for; matrix products, arithmetic and copies ran while one was open for 2% of the time, Pallas kernels for 29%

profile of v4, /device:TPU:0, one launch (start us, length us, event | category | flops | bytes accessed | tf_op | source)
XLA Modules:
  0.0 166.4 jit_solution(4262483670119571142)
XLA Ops:
  0.6 3.0 %collective-permute-start.4 = (bf16[512,2048]{1,0:T(8,128)(2,1)}, bf16[512,2048]{1,0:T(8,128)(2,1)}, u32[]{:S(2)}, u32[]{:S(2)}) collective-permute-start(bf16[512,2048]{1,0:T(8,128)(2,1)} %w0.5), channel_id=1, source_target_pairs={{0,8},{4,12},{8,0},{12,4},{16,24},{20,28},{24,16},{28,20},{1,9},{5... | collective-permute-start | bytes 6291464 | tf_op jit(solution)/shard_map/ppermute | solution.py:425
  9.3 21.1 %collective-permute-done.refs_1_ = bf16[256,1024]{1,0:T(8,128)(2,1)S(1)} collective-permute-done((bf16[256,1024]{1,0:T(8,128)(2,1)}, bf16[256,1024]{1,0:T(8,128)(2,1)S(1)}, u32[]{:S(2)}, u32[]{:S(2)}) %collective-permute-start) | collective-permute-done | bytes 524320 | tf_op jit(solution)/shard_map/ppermute | solution.py:425
  33.4 10.5 %collective-permute-done.1.refs_2_ = bf16[256,1024]{1,0:T(8,128)(2,1)S(1)} collective-permute-done((bf16[256,1024]{1,0:T(8,128)(2,1)S(1)}, bf16[256,1024]{1,0:T(8,128)(2,1)S(1)}, u32[]{:S(2)}, u32[]{:S(2)}) %collective-permute-start.1) | collective-permute-done | bytes 524320 | tf_op jit(solution)/shard_map/ppermute | solution.py:425
  43.9 2.7 %layer_norm.1 = (bf16[256,4096]{1,0:T(8,128)(2,1)S(1)}, bf16[256,2048]{1,0:T(8,128)(2,1)S(1)}) custom-call(s32[5]{0:T(128)S(1)} %pad_add_fusion.1.order_ref, bf16[256,2048]{1,0:T(8,128)(2,1)S(1)} %pad_maximum_fusion.refs_0_, bf16[256,1024]{1,0:T(8,128)(2,1)S(1)} %collective-permute-done.refs_1_, bf16[256,1024]{1,0:T(8,128)(2,1)S(1)} %collective-permute-done.1.refs_2_, ...), custom_call_target="tpu_custom_call" | custom-call | flops 1024 | bytes 1024 | tf_op jit(solution)/shard_map/layer_norm/pallas_call | solution.py:60
  46.7 2.9 %collective-permute-done.4.w1 = bf16[512,2048]{1,0:T(8,128)(2,1)} collective-permute-done((bf16[512,2048]{1,0:T(8,128)(2,1)}, bf16[512,2048]{1,0:T(8,128)(2,1)}, u32[]{:S(2)}, u32[]{:S(2)}) %collective-permute-start.4) | collective-permute-done | bytes 2097184 | tf_op jit(solution)/shard_map/ppermute | solution.py:425
  53.5 3.0 %collective-permute-done.3.v2 = bf16[2048,512]{1,0:T(8,128)(2,1)S(1)} collective-permute-done((bf16[2048,512]{1,0:T(8,128)(2,1)}, bf16[2048,512]{1,0:T(8,128)(2,1)S(1)}, u32[]{:S(2)}, u32[]{:S(2)}) %collective-permute-start.3) | collective-permute-done | bytes 2097184 | tf_op jit(solution)/shard_map/ppermute | solution.py:425
  57.4 9.4 %projections.1 = (bf16[256,512]{1,0:T(8,128)(2,1)S(1)}, bf16[256,512]{1,0:T(8,128)(2,1)}, bf16[256,512]{1,0:T(8,128)(2,1)}) custom-call(bf16[256,4096]{1,0:T(8,128)(2,1)S(1)} %get-tuple-element.76.x_ref.rows_ref, bf16[3,4096,512]{2,1,0:T(8,128)(2,1)} %bitcast.15, f32[256,128]{1,0:T(8,128)S(1)} %get-tuple-element.137.a_ref, ...), custom_call_target="tpu_custom_call" | custom-call | flops 1024 | bytes 1024 | tf_op jit(solution)/shard_map/projections/pallas_call | solution.py:114
  66.8 7.4 %up_half.3.keep_ref = f32[256,2048]{1,0:T(8,128)S(1)} custom-call(s32[4]{0:T(128)S(1)} %get-tuple-element.139.spots_ref, bf16[256,4096]{1,0:T(8,128)(2,1)S(1)} %get-tuple-element.76.x_ref.rows_ref, bf16[512,2048]{1,0:T(8,128)(2,1)S(1)} %copy-done.2, bf16[512,2048]{1,0:T(8,128)(2,1)} %collective-permute-done.4.w1, ...), custom_call_target="tpu_custom_call" | custom-call | flops 1024 | bytes 1024 | tf_op jit(solution)/shard_map/up_half/pallas_call | solution.py:237
  74.2 3.7 %collective-permute-done.7.rows_ref = bf16[256,2048]{1,0:T(8,128)(2,1)S(1)} collective-permute-done((bf16[256,2048]{1,0:T(8,128)(2,1)S(1)}, bf16[256,2048]{1,0:T(8,128)(2,1)S(1)}, u32[]{:S(2)}, u32[]{:S(2)}) %collective-permute-start.7) | collective-permute-done | bytes 1048608 | tf_op jit(solution)/shard_map/ppermute | solution.py:425
  78.0 5.3 %up_half.4 = bf16[256,1280]{1,0:T(8,128)(2,1)S(1)} custom-call(s32[4]{0:T(128)S(1)} %get-tuple-element.138.spots_ref, bf16[256,2048]{1,0:T(8,128)(2,1)S(1)} %collective-permute-done.7.rows_ref, bf16[512,2048]{1,0:T(8,128)(2,1)S(1)} %copy-done.2, bf16[512,2048]{1,0:T(8,128)(2,1)} %collective-permute-done.4.w1, bf16[512,2048]{1,0:T(8,128)(2,1)} %collective-permute-done.5.w2, ...), custom_call_target="tpu_custom_call" | custom-call | flops 1024 | bytes 1024 | tf_op jit(solution)/shard_map/up_half/pallas_call | solution.py:237
  85.4 4.0 %up_half.5 = bf16[256,768]{1,0:T(8,128)(2,1)S(1)} custom-call(s32[4]{0:T(128)S(1)} %get-tuple-element.138.spots_ref, bf16[256,2048]{1,0:T(8,128)(2,1)S(1)} %collective-permute-done.7.rows_ref, bf16[512,2048]{1,0:T(8,128)(2,1)S(1)} %copy-done.2, bf16[512,2048]{1,0:T(8,128)(2,1)} %collective-permute-done.4.w1, bf16[512,2048]{1,0:T(8,128)(2,1)} %collective-permute-done.5.w2, ...), custom_call_target="tpu_custom_call" | custom-call | flops 1024 | bytes 1024 | tf_op jit(solution)/shard_map/up_half/pallas_call | solution.py:237
  90.0 3.7 %attention.1.c0 = bf16[256,512]{1,0:T(8,128)(2,1)S(1)} custom-call(s32[2]{0:T(128)S(1)} %copy-done.10, bf16[256,512]{1,0:T(8,128)(2,1)S(1)} %get-tuple-element.82.q_ref, bf16[256,512]{1,0:T(8,128)(2,1)S(1)} %copy-done.6, bf16[256,512]{1,0:T(8,128)(2,1)S(1)} %copy-done.7, bf16[2,1536,512]{2,1,0:T(8,128)(2,1)S(1)} %copy-done.3, bf16[2,1536,512]{2,1,0:T(8,128)(2,1)S(1)} %copy-done.4), custom_call_target="tpu_custom_call" | custom-call | flops 1024 | bytes 1024 | tf_op jit(solution)/shard_map/attention/pallas_call | solution.py:168
  95.3 12.1 %collective-permute-done.9.refs_1_ = bf16[256,768]{1,0:T(8,128)(2,1)S(1)} collective-permute-done((bf16[256,768]{1,0:T(8,128)(2,1)S(1)}, bf16[256,768]{1,0:T(8,128)(2,1)S(1)}, u32[]{:S(2)}, u32[]{:S(2)}) %collective-permute-start.9) | collective-permute-done | bytes 393248 | tf_op jit(solution)/shard_map/ppermute | solution.py:425
  112.9 3.4 %down_and_output.4 = (f32[512,128]{1,0:T(8,128)S(1)}, f32[512,128]{1,0:T(8,128)S(1)}, bf16[1024,128]{1,0:T(8,128)(2,1)S(1)}) custom-call(s32[8]{0:T(128)S(1)} %pad_add_fusion.place_ref, bf16[256,2048]{1,0:T(8,128)(2,1)S(1)} %gelu.1.a0, bf16[256,2048]{1,0:T(8,128)(2,1)S(1)} %collective-permute-done.12.a1, bf16[256,512]{1,0:T(8,128)(2,1)S(1)} %attention.1.c0, ...), custom_call_target="tpu_custom_call" | custom-call | flops 1024 | bytes 1024 | tf_op jit(solution)/shard_map/down_and_output/pallas_call | solution.py:340
  118.0 5.3 %collective-permute-done.16.v3 = bf16[2048,128]{1,0:T(8,128)(2,1)S(1)} collective-permute-done((bf16[2048,128]{1,0:T(8,128)(2,1)S(1)}, bf16[2048,128]{1,0:T(8,128)(2,1)S(1)}, u32[]{:S(2)}, u32[]{:S(2)}) %collective-permute-start.16) | collective-permute-done | bytes 524320 | tf_op jit(solution)/shard_map/ppermute | solution.py:425
  123.3 3.4 %down_and_output.5 = (f32[512,128]{1,0:T(8,128)S(1)}, f32[512,128]{1,0:T(8,128)S(1)}, bf16[1024,128]{1,0:T(8,128)(2,1)S(1)}) custom-call(s32[8]{0:T(128)S(1)} %pad_add_fusion.place_ref, bf16[256,2048]{1,0:T(8,128)(2,1)S(1)} %gelu.1.a0, bf16[256,2048]{1,0:T(8,128)(2,1)S(1)} %collective-permute-done.12.a1, bf16[256,512]{1,0:T(8,128)(2,1)S(1)} %attention.1.c0, ...), custom_call_target="tpu_custom_call" | custom-call | flops 1024 | bytes 1024 | tf_op jit(solution)/shard_map/down_and_output/pallas_call | solution.py:340
  128.7 2.7 %collective-permute-start.15 = (bf16[512,128]{1,0:T(8,128)(2,1)S(1)}, bf16[512,128]{1,0:T(8,128)(2,1)S(1)}, u32[]{:S(2)}, u32[]{:S(2)}) collective-permute-start(bf16[512,128]{1,0:T(8,128)(2,1)S(1)} %get-tuple-element.94), channel_id=1, source_target_pairs={{0,2},{1,3},{2,0},{3,1},{4,6},{5,7},{6,4},{7,5},{8,10},{9,11},{10,... | collective-permute-start | bytes 393224 | tf_op jit(solution)/shard_map/ppermute | solution.py:425
  131.4 3.4 %down_and_output.6 = (f32[512,128]{1,0:T(8,128)S(1)}, f32[512,128]{1,0:T(8,128)S(1)}, bf16[1024,128]{1,0:T(8,128)(2,1)S(1)}) custom-call(s32[8]{0:T(128)S(1)} %pad_add_fusion.place_ref, bf16[256,2048]{1,0:T(8,128)(2,1)S(1)} %gelu.1.a0, bf16[256,2048]{1,0:T(8,128)(2,1)S(1)} %collective-permute-done.12.a1, bf16[256,512]{1,0:T(8,128)(2,1)S(1)} %attention.1.c0, ...), custom_call_target="tpu_custom_call" | custom-call | flops 1024 | bytes 1024 | tf_op jit(solution)/shard_map/down_and_output/pallas_call | solution.py:340
  135.3 3.2 %collective-permute-done.17.came_ref = bf16[1024,128]{1,0:T(8,128)(2,1)S(1)} collective-permute-done((bf16[1024,128]{1,0:T(8,128)(2,1)S(1)}, bf16[1024,128]{1,0:T(8,128)(2,1)S(1)}, u32[]{:S(2)}, u32[]{:S(2)}) %collective-permute-start.17) | collective-permute-done | bytes 262176 | tf_op jit(solution)/shard_map/ppermute | solution.py:425
  138.6 3.0 %collective-permute-start.18 = (bf16[512,128]{1,0:T(8,128)(2,1)S(1)}, bf16[512,128]{1,0:T(8,128)(2,1)S(1)}, u32[]{:S(2)}, u32[]{:S(2)}) collective-permute-start(bf16[512,128]{1,0:T(8,128)(2,1)S(1)} %get-tuple-element.104), channel_id=1, source_target_pairs={{0,2},{1,3},{2,0},{3,1},{4,6},{5,7},{6,4},{7,5},{8,10},{9,11},{10,... | collective-permute-start | bytes 393224 | tf_op jit(solution)/shard_map/ppermute | solution.py:425
  141.7 3.6 %down_and_output.7 = (f32[512,128]{1,0:T(8,128)S(1)}, f32[512,128]{1,0:T(8,128)S(1)}, bf16[1024,128]{1,0:T(8,128)(2,1)S(1)}) custom-call(s32[8]{0:T(128)S(1)} %pad_add_fusion.place_ref, bf16[256,2048]{1,0:T(8,128)(2,1)S(1)} %gelu.1.a0, bf16[256,2048]{1,0:T(8,128)(2,1)S(1)} %collective-permute-done.12.a1, bf16[256,512]{1,0:T(8,128)(2,1)S(1)} %attention.1.c0, ...), custom_call_target="tpu_custom_call" | custom-call | flops 1024 | bytes 1024 | tf_op jit(solution)/shard_map/down_and_output/pallas_call | solution.py:340
  149.6 4.9 %collective-permute-done.23.came_ref = bf16[1024,128]{1,0:T(8,128)(2,1)S(1)} collective-permute-done((bf16[1024,128]{1,0:T(8,128)(2,1)S(1)}, bf16[1024,128]{1,0:T(8,128)(2,1)S(1)}, u32[]{:S(2)}, u32[]{:S(2)}) %collective-permute-start.23) | collective-permute-done | bytes 262176 | tf_op jit(solution)/shard_map/ppermute | solution.py:425
  154.6 2.8 %collective-permute-start.24 = (bf16[512,128]{1,0:T(8,128)(2,1)S(1)}, bf16[512,128]{1,0:T(8,128)(2,1)S(1)}, u32[]{:S(2)}, u32[]{:S(2)}) collective-permute-start(bf16[512,128]{1,0:T(8,128)(2,1)S(1)} %get-tuple-element.128), channel_id=1, source_target_pairs={{0,2},{1,3},{2,0},{3,1},{4,6},{5,7},{6,4},{7,5},{8,10},{9,11},{10,... | collective-permute-start | bytes 393224 | tf_op jit(solution)/shard_map/ppermute | solution.py:425
  157.4 6.0 %collective-permute-done.24.refs_7_ = bf16[512,128]{1,0:T(8,128)(2,1)S(1)} collective-permute-done((bf16[512,128]{1,0:T(8,128)(2,1)S(1)}, bf16[512,128]{1,0:T(8,128)(2,1)S(1)}, u32[]{:S(2)}, u32[]{:S(2)}) %collective-permute-start.24) | collective-permute-done | bytes 131104 | tf_op jit(solution)/shard_map/ppermute | solution.py:425
  (82 shorter events, 34.7 us)
Async XLA Ops:
  0.6 49.0 %collective-permute-start.4 = (bf16[512,2048]{1,0:T(8,128)(2,1)}, bf16[512,2048]{1,0:T(8,128)(2,1)}, u32[]{:S(2)}, u32[]{:S(2)}) collective-permute-start(bf16[512,2048]{1,0:T(8,128)(2,1)} %w0.5), channel_id=1, source_target_pairs={{0,8},{4,12},{8,0},{12,4},{16,24},{20,28},{24,16},{28,20},{1,9},{5... | collective-permute-start | bytes 6291464 | tf_op jit(solution)/shard_map/ppermute | solution.py:425
  3.6 46.0 %collective-permute-start.5 = (bf16[512,2048]{1,0:T(8,128)(2,1)}, bf16[512,2048]{1,0:T(8,128)(2,1)}, u32[]{:S(2)}, u32[]{:S(2)}) collective-permute-start(bf16[512,2048]{1,0:T(8,128)(2,1)} %w0.5), channel_id=1, source_target_pairs={{0,4},{4,0},{8,12},{12,8},{16,20},{20,16},{24,28},{28,24},{1,5},{5... | collective-permute-start | bytes 6291464 | tf_op jit(solution)/shard_map/ppermute | solution.py:425
  3.6 26.8 %collective-permute-start = (bf16[256,1024]{1,0:T(8,128)(2,1)}, bf16[256,1024]{1,0:T(8,128)(2,1)S(1)}, u32[]{:S(2)}, u32[]{:S(2)}) collective-permute-start(bf16[256,1024]{1,0:T(8,128)(2,1)} %hidden_ref.1), channel_id=1, source_target_pairs={{0,2},{1,3},{2,0},{3,1},{4,6},{5,7},{6,4},{7,5},{8,10},{9,11},{10,... | collective-permute-start | bytes 1572872 | tf_op jit(solution)/shard_map/ppermute | solution.py:425
  6.2 25.7 %collective-permute-start.2 = (bf16[256,1024]{1,0:T(8,128)(2,1)}, bf16[256,1024]{1,0:T(8,128)(2,1)}, u32[]{:S(2)}, u32[]{:S(2)}) collective-permute-start(bf16[256,1024]{1,0:T(8,128)(2,1)} %hidden_ref.1), channel_id=1, source_target_pairs={{0,1},{1,0},{2,3},{3,2},{4,5},{5,4},{6,7},{7,6},{8,9},{9,8},{10,11... | collective-permute-start | bytes 1572872 | tf_op jit(solution)/shard_map/ppermute | solution.py:425
  7.8 48.7 %collective-permute-start.3 = (bf16[2048,512]{1,0:T(8,128)(2,1)}, bf16[2048,512]{1,0:T(8,128)(2,1)S(1)}, u32[]{:S(2)}, u32[]{:S(2)}) collective-permute-start(bf16[2048,512]{1,0:T(8,128)(2,1)} %v0.7), channel_id=1, source_target_pairs={{0,16},{4,20},{8,24},{12,28},{16,0},{20,4},{24,8},{28,12},{1,17},{... | collective-permute-start | bytes 6291464 | tf_op jit(solution)/shard_map/ppermute | solution.py:425
  30.4 13.5 %collective-permute-start.1 = (bf16[256,1024]{1,0:T(8,128)(2,1)S(1)}, bf16[256,1024]{1,0:T(8,128)(2,1)S(1)}, u32[]{:S(2)}, u32[]{:S(2)}) collective-permute-start(bf16[256,1024]{1,0:T(8,128)(2,1)S(1)} %collective-permute-done.refs_1_), channel_id=1, source_target_pairs={{0,1},{1,0},{2,3},{3,2},{4,5},{5,4},{6,7},{7,6},{8,9},{9,8},{10,11... | collective-permute-start | bytes 1572872 | tf_op jit(solution)/shard_map/ppermute | solution.py:425
  49.6 17.2 %collective-permute-start.6 = (bf16[512,2048]{1,0:T(8,128)(2,1)}, bf16[512,2048]{1,0:T(8,128)(2,1)S(1)}, u32[]{:S(2)}, u32[]{:S(2)}) collective-permute-start(bf16[512,2048]{1,0:T(8,128)(2,1)} %collective-permute-done.4.w1), channel_id=1, source_target_pairs={{0,4},{4,0},{8,12},{12,8},{16,20},{20,16},{24,28},{28,24},{1,5},{5... | collective-permute-start | bytes 6291464 | tf_op jit(solution)/shard_map/ppermute | solution.py:425
  49.7 61.0 %collective-permute-start.13 = (bf16[2048,512]{1,0:T(8,128)(2,1)S(1)}, bf16[2048,512]{1,0:T(8,128)(2,1)S(1)}, u32[]{:S(2)}, u32[]{:S(2)}) collective-permute-start(bf16[2048,512]{1,0:T(8,128)(2,1)S(1)} %copy-done.1), channel_id=1, source_target_pairs={{0,8},{4,12},{8,0},{12,4},{16,24},{20,28},{24,16},{28,20},{1,9},{5... | collective-permute-start | bytes 6291464 | tf_op jit(solution)/shard_map/ppermute | solution.py:425
  51.4 26.5 %collective-permute-start.7 = (bf16[256,2048]{1,0:T(8,128)(2,1)S(1)}, bf16[256,2048]{1,0:T(8,128)(2,1)S(1)}, u32[]{:S(2)}, u32[]{:S(2)}) collective-permute-start(bf16[256,2048]{1,0:T(8,128)(2,1)S(1)} %get-tuple-element.79), channel_id=1, source_target_pairs={{0,16},{4,20},{8,24},{12,28},{16,0},{20,4},{24,8},{28,12},{1,17},{... | collective-permute-start | bytes 3145736 | tf_op jit(solution)/shard_map/ppermute | solution.py:425
  83.3 24.2 %collective-permute-start.8 = (bf16[256,1280]{1,0:T(8,128)(2,1)S(1)}, bf16[256,1280]{1,0:T(8,128)(2,1)S(1)}, u32[]{:S(2)}, u32[]{:S(2)}) collective-permute-start(bf16[256,1280]{1,0:T(8,128)(2,1)S(1)} %up_half.4), channel_id=1, source_target_pairs={{0,16},{4,20},{8,24},{12,28},{16,0},{20,4},{24,8},{28,12},{1,17},{... | collective-permute-start | bytes 1966088 | tf_op jit(solution)/shard_map/ppermute | solution.py:425
  84.8 24.1 %collective-permute-start.11 = (bf16[2048,128]{1,0:T(8,128)(2,1)}, bf16[2048,128]{1,0:T(8,128)(2,1)S(1)}, u32[]{:S(2)}, u32[]{:S(2)}) collective-permute-start(bf16[2048,128]{1,0:T(8,128)(2,1)} %get-tuple-element.134), channel_id=1, source_target_pairs={{0,8},{4,12},{8,0},{12,4},{16,24},{20,28},{24,16},{28,20},{1,9},{5... | collective-permute-start | bytes 1572872 | tf_op jit(solution)/shard_map/ppermute | solution.py:425
  89.4 18.1 %collective-permute-start.9 = (bf16[256,768]{1,0:T(8,128)(2,1)S(1)}, bf16[256,768]{1,0:T(8,128)(2,1)S(1)}, u32[]{:S(2)}, u32[]{:S(2)}) collective-permute-start(bf16[256,768]{1,0:T(8,128)(2,1)S(1)} %up_half.5), channel_id=1, source_target_pairs={{0,16},{4,20},{8,24},{12,28},{16,0},{20,4},{24,8},{28,12},{1,17},{... | collective-permute-start | bytes 1179656 | tf_op jit(solution)/shard_map/ppermute | solution.py:425
  108.9 4.0 %collective-permute-start.12 = (bf16[256,2048]{1,0:T(8,128)(2,1)S(1)}, bf16[256,2048]{1,0:T(8,128)(2,1)S(1)}, u32[]{:S(2)}, u32[]{:S(2)}) collective-permute-start(bf16[256,2048]{1,0:T(8,128)(2,1)S(1)} %gelu.1.a0), channel_id=1, source_target_pairs={{0,4},{4,0},{8,12},{12,8},{16,20},{20,16},{24,28},{28,24},{1,5},{5... | collective-permute-start | bytes 3145736 | tf_op jit(solution)/shard_map/ppermute | solution.py:425
  108.9 14.3 %collective-permute-start.16 = (bf16[2048,128]{1,0:T(8,128)(2,1)S(1)}, bf16[2048,128]{1,0:T(8,128)(2,1)S(1)}, u32[]{:S(2)}, u32[]{:S(2)}) collective-permute-start(bf16[2048,128]{1,0:T(8,128)(2,1)S(1)} %get-tuple-element.98), channel_id=1, source_target_pairs={{0,8},{4,12},{8,0},{12,4},{16,24},{20,28},{24,16},{28,20},{1,9},{5... | collective-permute-start | bytes 1572872 | tf_op jit(solution)/shard_map/ppermute | solution.py:425
  110.8 20.6 %collective-permute-start.19 = (bf16[2048,128]{1,0:T(8,128)(2,1)S(1)}, bf16[2048,128]{1,0:T(8,128)(2,1)S(1)}, u32[]{:S(2)}, u32[]{:S(2)}) collective-permute-start(bf16[2048,128]{1,0:T(8,128)(2,1)S(1)} %get-tuple-element.109), channel_id=1, source_target_pairs={{0,16},{4,20},{8,24},{12,28},{16,0},{20,4},{24,8},{28,12},{1,17},{... | collective-permute-start | bytes 1572872 | tf_op jit(solution)/shard_map/ppermute | solution.py:425
  112.3 29.3 %collective-permute-start.22 = (bf16[2048,128]{1,0:T(8,128)(2,1)S(1)}, bf16[2048,128]{1,0:T(8,128)(2,1)S(1)}, u32[]{:S(2)}, u32[]{:S(2)}) collective-permute-start(bf16[2048,128]{1,0:T(8,128)(2,1)S(1)} %get-tuple-element.122), channel_id=1, source_target_pairs={{0,16},{4,20},{8,24},{12,28},{16,0},{20,4},{24,8},{28,12},{1,17},{... | collective-permute-start | bytes 1572872 | tf_op jit(solution)/shard_map/ppermute | solution.py:425
  116.4 12.3 %collective-permute-start.14 = (bf16[1024,128]{1,0:T(8,128)(2,1)S(1)}, bf16[1024,128]{1,0:T(8,128)(2,1)S(1)}, u32[]{:S(2)}, u32[]{:S(2)}) collective-permute-start(bf16[1024,128]{1,0:T(8,128)(2,1)S(1)} %get-tuple-element.92), channel_id=1, source_target_pairs={{0,1},{1,0},{2,3},{3,2},{4,5},{5,4},{6,7},{7,6},{8,9},{9,8},{10,11... | collective-permute-start | bytes 786440 | tf_op jit(solution)/shard_map/ppermute | solution.py:425
  126.7 11.8 %collective-permute-start.17 = (bf16[1024,128]{1,0:T(8,128)(2,1)S(1)}, bf16[1024,128]{1,0:T(8,128)(2,1)S(1)}, u32[]{:S(2)}, u32[]{:S(2)}) collective-permute-start(bf16[1024,128]{1,0:T(8,128)(2,1)S(1)} %get-tuple-element.101), channel_id=1, source_target_pairs={{0,1},{1,0},{2,3},{3,2},{4,5},{5,4},{6,7},{7,6},{8,9},{9,8},{10,11... | collective-permute-start | bytes 786440 | tf_op jit(solution)/shard_map/ppermute | solution.py:425
  128.7 9.9 %collective-permute-start.15 = (bf16[512,128]{1,0:T(8,128)(2,1)S(1)}, bf16[512,128]{1,0:T(8,128)(2,1)S(1)}, u32[]{:S(2)}, u32[]{:S(2)}) collective-permute-start(bf16[512,128]{1,0:T(8,128)(2,1)S(1)} %get-tuple-element.94), channel_id=1, source_target_pairs={{0,2},{1,3},{2,0},{3,1},{4,6},{5,7},{6,4},{7,5},{8,10},{9,11},{10,... | collective-permute-start | bytes 393224 | tf_op jit(solution)/shard_map/ppermute | solution.py:425
  134.8 12.3 %collective-permute-start.20 = (bf16[1024,128]{1,0:T(8,128)(2,1)S(1)}, bf16[1024,128]{1,0:T(8,128)(2,1)S(1)}, u32[]{:S(2)}, u32[]{:S(2)}) collective-permute-start(bf16[1024,128]{1,0:T(8,128)(2,1)S(1)} %get-tuple-element.112), channel_id=1, source_target_pairs={{0,1},{1,0},{2,3},{3,2},{4,5},{5,4},{6,7},{7,6},{8,9},{9,8},{10,11... | collective-permute-start | bytes 786440 | tf_op jit(solution)/shard_map/ppermute | solution.py:425
  138.6 8.5 %collective-permute-start.18 = (bf16[512,128]{1,0:T(8,128)(2,1)S(1)}, bf16[512,128]{1,0:T(8,128)(2,1)S(1)}, u32[]{:S(2)}, u32[]{:S(2)}) collective-permute-start(bf16[512,128]{1,0:T(8,128)(2,1)S(1)} %get-tuple-element.104), channel_id=1, source_target_pairs={{0,2},{1,3},{2,0},{3,1},{4,6},{5,7},{6,4},{7,5},{8,10},{9,11},{10,... | collective-permute-start | bytes 393224 | tf_op jit(solution)/shard_map/ppermute | solution.py:425
  145.3 9.2 %collective-permute-start.23 = (bf16[1024,128]{1,0:T(8,128)(2,1)S(1)}, bf16[1024,128]{1,0:T(8,128)(2,1)S(1)}, u32[]{:S(2)}, u32[]{:S(2)}) collective-permute-start(bf16[1024,128]{1,0:T(8,128)(2,1)S(1)} %get-tuple-element.125), channel_id=1, source_target_pairs={{0,1},{1,0},{2,3},{3,2},{4,5},{5,4},{6,7},{7,6},{8,9},{9,8},{10,11... | collective-permute-start | bytes 786440 | tf_op jit(solution)/shard_map/ppermute | solution.py:425
  147.2 7.4 %collective-permute-start.21 = (bf16[512,128]{1,0:T(8,128)(2,1)S(1)}, bf16[512,128]{1,0:T(8,128)(2,1)S(1)}, u32[]{:S(2)}, u32[]{:S(2)}) collective-permute-start(bf16[512,128]{1,0:T(8,128)(2,1)S(1)} %get-tuple-element.115), channel_id=1, source_target_pairs={{0,2},{1,3},{2,0},{3,1},{4,6},{5,7},{6,4},{7,5},{8,10},{9,11},{10,... | collective-permute-start | bytes 393224 | tf_op jit(solution)/shard_map/ppermute | solution.py:425
  154.6 8.7 %collective-permute-start.24 = (bf16[512,128]{1,0:T(8,128)(2,1)S(1)}, bf16[512,128]{1,0:T(8,128)(2,1)S(1)}, u32[]{:S(2)}, u32[]{:S(2)}) collective-permute-start(bf16[512,128]{1,0:T(8,128)(2,1)S(1)} %get-tuple-element.128), channel_id=1, source_target_pairs={{0,2},{1,3},{2,0},{3,1},{4,6},{5,7},{6,4},{7,5},{8,10},{9,11},{10,... | collective-permute-start | bytes 393224 | tf_op jit(solution)/shard_map/ppermute | solution.py:425
  (14 other events, 155.3 us)

commit v5 on v4

--- a/solution.py
+++ b/solution.py
@@ -211,23 +211,62 @@
     )(spots, normed, *weights, bias[None])
 
 
-def up_half_kernel(spots_ref, rows_ref, w0, w1, w2, w3, out_ref, x_ref):
-    depth = w0.shape[0]
-
-    @pl.when(pl.program_id(0) == 0)
-    def _():
-        for k in range(4):
-            columns = pl.ds(pl.multiple_of(spots_ref[k] * depth, depth), depth)
-            x_ref[:, k * depth : (k + 1) * depth] = rows_ref[:, columns]
-
-    weight = jnp.concatenate([w0[...], w1[...], w2[...], w3[...]], axis=0)
-    out_ref[...] = jnp.dot(x_ref[...], weight, preferred_element_type=f32).astype(out_ref.dtype)
+def up_half_kernel(spots_ref, rows_ref, w0, w1, w2, w3, out_ref, sum_ref):
+    step = pl.program_id(0)
+    steps = pl.num_programs(0)
+    part = w0.shape[0]
+    total = None
+    for k, weight in enumerate((w0, w1, w2, w3)):
+        columns = pl.ds(pl.multiple_of((spots_ref[k] * steps + step) * part, part), part)
+        found = jnp.dot(rows_ref[:, columns], weight[...], preferred_element_type=f32)
+        total = found if total is None else total + found
+
+    @pl.when(step == 0)
+    def _():
+        sum_ref[...] = total
+
+    @pl.when(step == steps - 1)
+    def _():
+        out_ref[...] = (sum_ref[...] + total).astype(out_ref.dtype)
 
 
 def up_half_call(spots, x, weights, start, stop, dtype):
     rows = x.shape[0]
     width = stop - start
-    depth = 4 * weights[0].shape[0]
+    steps = 2
+    part = weights[0].shape[0] // steps
+    column = start // width
+    in_specs = [pl.BlockSpec(x.shape, lambda s, spots: (0, 0))]
+    in_specs += [pl.BlockSpec((part, width), lambda s, spots: (s, column))] * 4
+    return pl.pallas_call(
+        up_half_kernel,
+        grid_spec=pltpu.PrefetchScalarGridSpec(
+            num_scalar_prefetch=1,
+            grid=(steps,),
+            in_specs=in_specs,
+            out_specs=pl.BlockSpec((rows, width), lambda s, spots: (0, 0)),
+            scratch_shapes=[pltpu.VMEM((rows, width), f32)],
+        ),
+        out_shape=jax.ShapeDtypeStruct((rows, width), dtype),
+        compiler_params=params(28),
+        cost_estimate=cost(),
+        name="up_half",
+    )(spots, x, *weights)
+
+
+def up_rest_kernel(spots_ref, rows_ref, w0, w1, w2, w3, out_ref):
+    depth = w0.shape[0]
+    total = None
+    for k, weight in enumerate((w0, w1, w2, w3)):
+        columns = pl.ds(pl.multiple_of(spots_ref[k] * depth, depth), depth)
+        part = jnp.dot(rows_ref[:, columns], weight[...], preferred_element_type=f32)
+        total = part if total is None else total + part
+    out_ref[...] = total.astype(out_ref.dtype)
+
+
+def up_rest_call(spots, x, weights, start, stop, dtype):
+    rows = x.shape[0]
+    width = stop - start
     block = 256
     steps = width // block
     first = start // block
@@ -235,18 +274,17 @@
         pl.BlockSpec((w.shape[0], block), lambda n, spots: (0, first + n)) for w in weights
     ]
     return pl.pallas_call(
-        up_half_kernel,
+        up_rest_kernel,
         grid_spec=pltpu.PrefetchScalarGridSpec(
             num_scalar_prefetch=1,
             grid=(steps,),
             in_specs=in_specs,
             out_specs=pl.BlockSpec((rows, block), lambda n, spots: (0, n)),
-            scratch_shapes=[pltpu.VMEM((rows, depth), bf16)],
         ),
         out_shape=jax.ShapeDtypeStruct((rows, width), dtype),
         compiler_params=params(28),
         cost_estimate=cost(),
-        name="up_half",
+        name="up_rest",
     )(spots, x, *weights)
 
 
@@ -460,7 +498,9 @@
     last = over_head(far, mask=1)
     pair = jnp.concatenate([hidden_in, near], axis=1)
     affine = jnp.stack([norm_gain, norm_shift])
-    last, pair, affine = lax.optimization_barrier((last, pair, affine))
+    quarter = down_weight.shape[1] // 4
+    mine = [down_weight[:, k * quarter : (k + 1) * quarter] for k in range(4)]
+    last, pair, affine, mine = lax.optimization_barrier((last, pair, affine, mine))
 
     order = jnp.concatenate([line ^ chips, (1 - (me >> 2))[None]])
     normed, for_other = norm_call(order, 4, [pair, far, last], affine, split=True)
@@ -471,7 +511,6 @@
     down_y, normed_next = lax.optimization_barrier((down_y, normed_next))
 
     half = down_weight.shape[1] // 2
-    quarter = half // 2
     forward_y = [down_y[:, k * quarter : (k + 1) * quarter] for k in range(2)]
     diagonal = [over_req(forward_y[0], mask=X)]
     normed_next, forward_y = lax.optimization_barrier((normed_next, forward_y))
@@ -487,9 +526,9 @@
     keep = up_half_call(blocks, after(normed, query), weights, 0, units, f32)
     other = after(normed_other, keep)
     came = []
-    cuts = [0, units * 5 // 8, units]
-    for start, stop in zip(cuts, cuts[1:]):
-        send = up_half_call(blocks & 3, other, weights, start, stop, bf16)
+    cut = units * 5 // 8
+    for call, start, stop in ((up_half_call, 0, cut), (up_rest_call, cut, units)):
+        send = call(blocks & 3, other, weights, start, stop, bf16)
         came.append(over_req(send, mask=Y))
         other = after(other, send)
 
@@ -519,7 +558,12 @@
             place,
             rows,
             (context, context_other),
-            [(down_weight, k), (down_x, k), (down_y, k), (diagonal[k], 0)],
+            [
+                (mine[k], 0),
+                (down_x, k) if k < 2 else (forward_x[k - 2], 0),
+                (forward_y[k], 0) if k < 2 else (down_y, k),
+                (diagonal[k], 0),
+            ],
             output_weight,
             k * quarter,
             quarter,

time: 167 us -> 165 us (0.988)
  local copies, waits for them, and re-layouts: 0.99 us -> 4.2 us
  Pallas kernels: 48.7 us -> 46.2 us
  waiting for transfers between devices: 76.8 us -> 74.9 us
    pallas_call x3 -> x2, Pallas kernels: 16.7 us -> 8.23 us  [up_half_call(): pl.pallas_call(up_half_kernel, grid_spec=pltpu.PrefetchScalarGridSpec(num...]
    pallas_call x0 -> x1, Pallas kernels: none -> 3.86 us  [up_rest_call(): pl.pallas_call(up_rest_kernel, grid_spec=pltpu.PrefetchScalarGridSpec(num...]
    slice x0 -> x1, local copies, waits for them, and re-layouts: none -> 2.76 us  [body_small(): mine = [down_weight[:, k * quarter:(k + 1) * quarter] for k in range(4)]]
    ppermute x26, waiting for transfers between devices: 76.8 us -> 74.9 us  [swap(): return lax.ppermute(value, axis, [(i, i ^ mask) for i in range(size)])]
  transfers between devices with their start and end apart: 26 -> 26, of which waited for: 13 -> 14; matrix products, arithmetic and copies ran while one was open for 2% -> 4% of each run, Pallas kernels for 29% -> 27%
where the time goes in v5:
time: 165 us; the launch traced here: 164 us
  waiting for transfers between devices  74.9 us (45%)
  Pallas kernels  46.2 us (28%)
  starting transfers between devices  35.9 us (22%)
  local copies, waits for them, and re-layouts  4.2 us (3%)
  other arithmetic  2.12 us (1%)
    ppermute x26, waiting for transfers between devices, swap(): return lax.ppermute(value, axis, [(i, i ^ mask) for i in range(size)])  74.9 us
    ppermute x26, starting transfers between devices, swap(): return lax.ppermute(value, axis, [(i, i ^ mask) for i in range(size)])  35.9 us
    pallas_call x4, Pallas kernels, down_call(): pl.pallas_call(down_kernel, grid_spec=pltpu.PrefetchScalarGridSpec(num_sc...  14.5 us
    pallas_call x1, Pallas kernels, project_call(): pl.pallas_call(functools.partial(project_kernel, heads), grid=(3 * heads,...  9.45 us
    pallas_call x2, Pallas kernels, up_half_call(): pl.pallas_call(up_half_kernel, grid_spec=pltpu.PrefetchScalarGridSpec(num...  8.23 us
    pallas_call x1, Pallas kernels, norm_call(): pl.pallas_call(functools.partial(norm_kernel, count, split), grid_spec=pl...  4.16 us
    pallas_call x1, Pallas kernels, up_rest_call(): pl.pallas_call(up_rest_kernel, grid_spec=pltpu.PrefetchScalarGridSpec(num...  3.86 us
    pallas_call x1, Pallas kernels, attend_call(): pl.pallas_call(functools.partial(attend_kernel, local // HD), grid_spec=p...  3.81 us
  transfers between devices with their start and end apart: 26, of which 14 were waited for; matrix products, arithmetic and copies ran while one was open for 4% of the time, Pallas kernels for 27%

profile of v5, /device:TPU:0, one launch (start us, length us, event | category | flops | bytes accessed | tf_op | source)
XLA Modules:
  0.0 164.3 jit_solution(14185155310176621284)
XLA Ops:
  0.7 3.0 %collective-permute-start.4 = (bf16[512,2048]{1,0:T(8,128)(2,1)}, bf16[512,2048]{1,0:T(8,128)(2,1)S(1)}, u32[]{:S(2)}, u32[]{:S(2)}) collective-permute-start(bf16[512,2048]{1,0:T(8,128)(2,1)} %w0.5), channel_id=1, source_target_pairs={{0,8},{4,12},{8,0},{12,4},{16,24},{20,28},{24,16},{28,20},{1,9},{5... | collective-permute-start | bytes 6291464 | tf_op jit(solution)/shard_map/ppermute | solution.py:463
  3.7 2.6 %collective-permute-start = (bf16[256,1024]{1,0:T(8,128)(2,1)}, bf16[256,1024]{1,0:T(8,128)(2,1)}, u32[]{:S(2)}, u32[]{:S(2)}) collective-permute-start(bf16[256,1024]{1,0:T(8,128)(2,1)} %hidden_ref.1), channel_id=1, source_target_pairs={{0,2},{1,3},{2,0},{3,1},{4,6},{5,7},{6,4},{7,5},{8,10},{9,11},{10,... | collective-permute-start | bytes 1572872 | tf_op jit(solution)/shard_map/ppermute | solution.py:463
  9.4 2.8 %fusion.13 = (bf16[2048,128]{1,0:T(8,128)(2,1)S(1)}, bf16[2048,128]{1,0:T(8,128)(2,1)}, bf16[2048,128]{1,0:T(8,128)(2,1)}, bf16[2048,128]{1,0:T(8,128)(2,1)}) fusion(bf16[2048,512]{1,0:T(8,128)(2,1)} %param.20), kind=kLoop, calls=%fused_computation.31 | loop fusion | bytes 4194304 | tf_op jit(solution)/shard_map/slice | solution.py:502
  12.1 18.4 %collective-permute-done.refs_1_ = bf16[256,1024]{1,0:T(8,128)(2,1)} collective-permute-done((bf16[256,1024]{1,0:T(8,128)(2,1)}, bf16[256,1024]{1,0:T(8,128)(2,1)}, u32[]{:S(2)}, u32[]{:S(2)}) %collective-permute-start) | collective-permute-done | bytes 524320 | tf_op jit(solution)/shard_map/ppermute | solution.py:463
  32.6 11.8 %collective-permute-done.1.refs_2_ = bf16[256,1024]{1,0:T(8,128)(2,1)} collective-permute-done((bf16[256,1024]{1,0:T(8,128)(2,1)}, bf16[256,1024]{1,0:T(8,128)(2,1)}, u32[]{:S(2)}, u32[]{:S(2)}) %collective-permute-start.1) | collective-permute-done | bytes 524320 | tf_op jit(solution)/shard_map/ppermute | solution.py:463
  44.4 4.2 %layer_norm.1 = (bf16[256,4096]{1,0:T(8,128)(2,1)S(1)}, bf16[256,2048]{1,0:T(8,128)(2,1)S(1)}) custom-call(s32[5]{0:T(128)S(1)} %pad_add_fusion.1.order_ref, bf16[256,2048]{1,0:T(8,128)(2,1)S(1)} %pad_maximum_fusion.refs_0_, bf16[256,1024]{1,0:T(8,128)(2,1)} %collective-permute-done.refs_1_, bf16[256,1024]{1,0:T(8,128)(2,1)} %collective-permute-done.1.refs_2_, ...), custom_call_target="tpu_custom_call" | custom-call | flops 1024 | bytes 1024 | tf_op jit(solution)/shard_map/layer_norm/pallas_call | solution.py:60
  53.5 3.2 %collective-permute-done.3.v2 = bf16[2048,512]{1,0:T(8,128)(2,1)} collective-permute-done((bf16[2048,512]{1,0:T(8,128)(2,1)}, bf16[2048,512]{1,0:T(8,128)(2,1)}, u32[]{:S(2)}, u32[]{:S(2)}) %collective-permute-start.3) | collective-permute-done | bytes 2097184 | tf_op jit(solution)/shard_map/ppermute | solution.py:463
  58.0 9.5 %projections.1 = (bf16[256,512]{1,0:T(8,128)(2,1)S(1)}, bf16[256,512]{1,0:T(8,128)(2,1)}, bf16[256,512]{1,0:T(8,128)(2,1)}) custom-call(bf16[256,4096]{1,0:T(8,128)(2,1)S(1)} %get-tuple-element.81.x_ref.rows_ref, bf16[3,4096,512]{2,1,0:T(8,128)(2,1)} %bitcast.15, f32[256,128]{1,0:T(8,128)S(1)} %get-tuple-element.151.a_ref, ...), custom_call_target="tpu_custom_call" | custom-call | flops 1024 | bytes 1024 | tf_op jit(solution)/shard_map/projections/pallas_call | solution.py:114
  67.4 4.6 %up_half.2.keep_ref = f32[256,2048]{1,0:T(8,128)S(1)} custom-call(s32[4]{0:T(128)S(1)} %get-tuple-element.153.spots_ref, bf16[256,4096]{1,0:T(8,128)(2,1)S(1)} %get-tuple-element.81.x_ref.rows_ref, bf16[512,2048]{1,0:T(8,128)(2,1)S(1)} %copy-done.1, bf16[512,2048]{1,0:T(8,128)(2,1)S(1)} %collective-permute-done.4.w1, ...), custom_call_target="tpu_custom_call" | custom-call | flops 1024 | bytes 1024 | tf_op jit(solution)/shard_map/up_half/pallas_call | solution.py:241
  72.0 6.0 %collective-permute-done.7.rows_ref = bf16[256,2048]{1,0:T(8,128)(2,1)S(1)} collective-permute-done((bf16[256,2048]{1,0:T(8,128)(2,1)S(1)}, bf16[256,2048]{1,0:T(8,128)(2,1)S(1)}, u32[]{:S(2)}, u32[]{:S(2)}) %collective-permute-start.7) | collective-permute-done | bytes 1048608 | tf_op jit(solution)/shard_map/ppermute | solution.py:463
  78.0 3.6 %up_half.3 = bf16[256,1280]{1,0:T(8,128)(2,1)S(1)} custom-call(s32[4]{0:T(128)S(1)} %get-tuple-element.152.spots_ref, bf16[256,2048]{1,0:T(8,128)(2,1)S(1)} %collective-permute-done.7.rows_ref, bf16[512,2048]{1,0:T(8,128)(2,1)S(1)} %copy-done.1, bf16[512,2048]{1,0:T(8,128)(2,1)S(1)} %collective-permute-done.4.w1, ...), custom_call_target="tpu_custom_call" | custom-call | flops 1024 | bytes 1024 | tf_op jit(solution)/shard_map/up_half/pallas_call | solution.py:241
  83.8 3.9 %up_rest.1 = bf16[256,768]{1,0:T(8,128)(2,1)S(1)} custom-call(s32[4]{0:T(128)S(1)} %get-tuple-element.152.spots_ref, bf16[256,2048]{1,0:T(8,128)(2,1)S(1)} %collective-permute-done.7.rows_ref, bf16[512,2048]{1,0:T(8,128)(2,1)S(1)} %copy-done.1, bf16[512,2048]{1,0:T(8,128)(2,1)S(1)} %collective-permute-done.4.w1, ...), custom_call_target="tpu_custom_call" | custom-call | flops 1024 | bytes 1024 | tf_op jit(solution)/shard_map/up_rest/pallas_call | solution.py:276
  88.2 3.8 %attention.1.c0 = bf16[256,512]{1,0:T(8,128)(2,1)S(1)} custom-call(s32[2]{0:T(128)S(1)} %copy-done.12, bf16[256,512]{1,0:T(8,128)(2,1)S(1)} %get-tuple-element.87.q_ref, bf16[256,512]{1,0:T(8,128)(2,1)S(1)} %copy-done.8, bf16[256,512]{1,0:T(8,128)(2,1)S(1)} %copy-done.9, bf16[2,1536,512]{2,1,0:T(8,128)(2,1)S(1)} %copy-done.2, bf16[2,1536,512]{2,1,0:T(8,128)(2,1)S(1)} %copy-done.3), custom_call_target="tpu_custom_call" | custom-call | flops 1024 | bytes 1024 | tf_op jit(solution)/shard_map/attention/pallas_call | solution.py:168
  93.7 12.2 %collective-permute-done.9.refs_1_ = bf16[256,768]{1,0:T(8,128)(2,1)S(1)} collective-permute-done((bf16[256,768]{1,0:T(8,128)(2,1)S(1)}, bf16[256,768]{1,0:T(8,128)(2,1)S(1)}, u32[]{:S(2)}, u32[]{:S(2)}) %collective-permute-start.9) | collective-permute-done | bytes 393248 | tf_op jit(solution)/shard_map/ppermute | solution.py:463
  112.9 3.3 %down_and_output.4 = (f32[512,128]{1,0:T(8,128)S(1)}, f32[512,128]{1,0:T(8,128)S(1)}, bf16[1024,128]{1,0:T(8,128)(2,1)S(1)}) custom-call(s32[8]{0:T(128)S(1)} %pad_add_fusion.place_ref, bf16[256,2048]{1,0:T(8,128)(2,1)S(1)} %gelu.1.a0, bf16[256,2048]{1,0:T(8,128)(2,1)S(1)} %collective-permute-done.12.a1, bf16[256,512]{1,0:T(8,128)(2,1)S(1)} %attention.1.c0, ...), custom_call_target="tpu_custom_call" | custom-call | flops 1024 | bytes 1024 | tf_op jit(solution)/shard_map/down_and_output/pallas_call | solution.py:378
  117.8 5.4 %collective-permute-done.16.v3 = bf16[2048,128]{1,0:T(8,128)(2,1)S(1)} collective-permute-done((bf16[2048,128]{1,0:T(8,128)(2,1)S(1)}, bf16[2048,128]{1,0:T(8,128)(2,1)S(1)}, u32[]{:S(2)}, u32[]{:S(2)}) %collective-permute-start.16) | collective-permute-done | bytes 524320 | tf_op jit(solution)/shard_map/ppermute | solution.py:463
  123.2 3.3 %down_and_output.5 = (f32[512,128]{1,0:T(8,128)S(1)}, f32[512,128]{1,0:T(8,128)S(1)}, bf16[1024,128]{1,0:T(8,128)(2,1)S(1)}) custom-call(s32[8]{0:T(128)S(1)} %pad_add_fusion.place_ref, bf16[256,2048]{1,0:T(8,128)(2,1)S(1)} %gelu.1.a0, bf16[256,2048]{1,0:T(8,128)(2,1)S(1)} %collective-permute-done.12.a1, bf16[256,512]{1,0:T(8,128)(2,1)S(1)} %attention.1.c0, ...), custom_call_target="tpu_custom_call" | custom-call | flops 1024 | bytes 1024 | tf_op jit(solution)/shard_map/down_and_output/pallas_call | solution.py:378
  128.4 2.6 %collective-permute-start.15 = (bf16[512,128]{1,0:T(8,128)(2,1)S(1)}, bf16[512,128]{1,0:T(8,128)(2,1)S(1)}, u32[]{:S(2)}, u32[]{:S(2)}) collective-permute-start(bf16[512,128]{1,0:T(8,128)(2,1)S(1)} %get-tuple-element.101), channel_id=1, source_target_pairs={{0,2},{1,3},{2,0},{3,1},{4,6},{5,7},{6,4},{7,5},{8,10},{9,11},{10,... | collective-permute-start | bytes 393224 | tf_op jit(solution)/shard_map/ppermute | solution.py:463
  131.1 4.0 %down_and_output.6 = (f32[512,128]{1,0:T(8,128)S(1)}, f32[512,128]{1,0:T(8,128)S(1)}, bf16[1024,128]{1,0:T(8,128)(2,1)S(1)}) custom-call(s32[8]{0:T(128)S(1)} %pad_add_fusion.place_ref, bf16[256,2048]{1,0:T(8,128)(2,1)S(1)} %gelu.1.a0, bf16[256,2048]{1,0:T(8,128)(2,1)S(1)} %collective-permute-done.12.a1, bf16[256,512]{1,0:T(8,128)(2,1)S(1)} %attention.1.c0, ...), custom_call_target="tpu_custom_call" | custom-call | flops 1024 | bytes 1024 | tf_op jit(solution)/shard_map/down_and_output/pallas_call | solution.py:378
  138.0 3.4 %collective-permute-start.18 = (bf16[512,128]{1,0:T(8,128)(2,1)S(1)}, bf16[512,128]{1,0:T(8,128)(2,1)S(1)}, u32[]{:S(2)}, u32[]{:S(2)}) collective-permute-start(bf16[512,128]{1,0:T(8,128)(2,1)S(1)} %get-tuple-element.112), channel_id=1, source_target_pairs={{0,2},{1,3},{2,0},{3,1},{4,6},{5,7},{6,4},{7,5},{8,10},{9,11},{10,... | collective-permute-start | bytes 393224 | tf_op jit(solution)/shard_map/ppermute | solution.py:463
  141.4 3.9 %down_and_output.7 = (f32[512,128]{1,0:T(8,128)S(1)}, f32[512,128]{1,0:T(8,128)S(1)}, bf16[1024,128]{1,0:T(8,128)(2,1)S(1)}) custom-call(s32[8]{0:T(128)S(1)} %pad_add_fusion.place_ref, bf16[256,2048]{1,0:T(8,128)(2,1)S(1)} %gelu.1.a0, bf16[256,2048]{1,0:T(8,128)(2,1)S(1)} %collective-permute-done.12.a1, bf16[256,512]{1,0:T(8,128)(2,1)S(1)} %attention.1.c0, ...), custom_call_target="tpu_custom_call" | custom-call | flops 1024 | bytes 1024 | tf_op jit(solution)/shard_map/down_and_output/pallas_call | solution.py:378
  149.1 5.1 %collective-permute-done.23.came_ref = bf16[1024,128]{1,0:T(8,128)(2,1)S(1)} collective-permute-done((bf16[1024,128]{1,0:T(8,128)(2,1)S(1)}, bf16[1024,128]{1,0:T(8,128)(2,1)S(1)}, u32[]{:S(2)}, u32[]{:S(2)}) %collective-permute-start.23) | collective-permute-done | bytes 262176 | tf_op jit(solution)/shard_map/ppermute | solution.py:463
  154.3 2.8 %collective-permute-start.24 = (bf16[512,128]{1,0:T(8,128)(2,1)S(1)}, bf16[512,128]{1,0:T(8,128)(2,1)S(1)}, u32[]{:S(2)}, u32[]{:S(2)}) collective-permute-start(bf16[512,128]{1,0:T(8,128)(2,1)S(1)} %get-tuple-element.138), channel_id=1, source_target_pairs={{0,2},{1,3},{2,0},{3,1},{4,6},{5,7},{6,4},{7,5},{8,10},{9,11},{10,... | collective-permute-start | bytes 393224 | tf_op jit(solution)/shard_map/ppermute | solution.py:463
  157.1 4.1 %collective-permute-done.24.refs_7_ = bf16[512,128]{1,0:T(8,128)(2,1)S(1)} collective-permute-done((bf16[512,128]{1,0:T(8,128)(2,1)S(1)}, bf16[512,128]{1,0:T(8,128)(2,1)S(1)}, u32[]{:S(2)}, u32[]{:S(2)}) %collective-permute-start.24) | collective-permute-done | bytes 131104 | tf_op jit(solution)/shard_map/ppermute | solution.py:463
  (93 shorter events, 35.9 us)
Async XLA Ops:
  0.7 48.8 %collective-permute-start.4 = (bf16[512,2048]{1,0:T(8,128)(2,1)}, bf16[512,2048]{1,0:T(8,128)(2,1)S(1)}, u32[]{:S(2)}, u32[]{:S(2)}) collective-permute-start(bf16[512,2048]{1,0:T(8,128)(2,1)} %w0.5), channel_id=1, source_target_pairs={{0,8},{4,12},{8,0},{12,4},{16,24},{20,28},{24,16},{28,20},{1,9},{5... | collective-permute-start | bytes 6291464 | tf_op jit(solution)/shard_map/ppermute | solution.py:463
  3.7 45.8 %collective-permute-start.5 = (bf16[512,2048]{1,0:T(8,128)(2,1)}, bf16[512,2048]{1,0:T(8,128)(2,1)}, u32[]{:S(2)}, u32[]{:S(2)}) collective-permute-start(bf16[512,2048]{1,0:T(8,128)(2,1)} %w0.5), channel_id=1, source_target_pairs={{0,4},{4,0},{8,12},{12,8},{16,20},{20,16},{24,28},{28,24},{1,5},{5... | collective-permute-start | bytes 6291464 | tf_op jit(solution)/shard_map/ppermute | solution.py:463
  3.7 26.9 %collective-permute-start = (bf16[256,1024]{1,0:T(8,128)(2,1)}, bf16[256,1024]{1,0:T(8,128)(2,1)}, u32[]{:S(2)}, u32[]{:S(2)}) collective-permute-start(bf16[256,1024]{1,0:T(8,128)(2,1)} %hidden_ref.1), channel_id=1, source_target_pairs={{0,2},{1,3},{2,0},{3,1},{4,6},{5,7},{6,4},{7,5},{8,10},{9,11},{10,... | collective-permute-start | bytes 1572872 | tf_op jit(solution)/shard_map/ppermute | solution.py:463
  6.3 25.0 %collective-permute-start.2 = (bf16[256,1024]{1,0:T(8,128)(2,1)}, bf16[256,1024]{1,0:T(8,128)(2,1)}, u32[]{:S(2)}, u32[]{:S(2)}) collective-permute-start(bf16[256,1024]{1,0:T(8,128)(2,1)} %hidden_ref.1), channel_id=1, source_target_pairs={{0,1},{1,0},{2,3},{3,2},{4,5},{5,4},{6,7},{7,6},{8,9},{9,8},{10,11... | collective-permute-start | bytes 1572872 | tf_op jit(solution)/shard_map/ppermute | solution.py:463
  7.8 48.8 %collective-permute-start.3 = (bf16[2048,512]{1,0:T(8,128)(2,1)}, bf16[2048,512]{1,0:T(8,128)(2,1)}, u32[]{:S(2)}, u32[]{:S(2)}) collective-permute-start(bf16[2048,512]{1,0:T(8,128)(2,1)} %param.20), channel_id=1, source_target_pairs={{0,16},{4,20},{8,24},{12,28},{16,0},{20,4},{24,8},{28,12},{1,17},{... | collective-permute-start | bytes 6291464 | tf_op jit(solution)/shard_map/ppermute | solution.py:463
  30.6 13.8 %collective-permute-start.1 = (bf16[256,1024]{1,0:T(8,128)(2,1)}, bf16[256,1024]{1,0:T(8,128)(2,1)}, u32[]{:S(2)}, u32[]{:S(2)}) collective-permute-start(bf16[256,1024]{1,0:T(8,128)(2,1)} %collective-permute-done.refs_1_), channel_id=1, source_target_pairs={{0,1},{1,0},{2,3},{3,2},{4,5},{5,4},{6,7},{7,6},{8,9},{9,8},{10,11... | collective-permute-start | bytes 1572872 | tf_op jit(solution)/shard_map/ppermute | solution.py:463
  49.5 17.9 %collective-permute-start.6 = (bf16[512,2048]{1,0:T(8,128)(2,1)S(1)}, bf16[512,2048]{1,0:T(8,128)(2,1)S(1)}, u32[]{:S(2)}, u32[]{:S(2)}) collective-permute-start(bf16[512,2048]{1,0:T(8,128)(2,1)S(1)} %collective-permute-done.4.w1), channel_id=1, source_target_pairs={{0,4},{4,0},{8,12},{12,8},{16,20},{20,16},{24,28},{28,24},{1,5},{5... | collective-permute-start | bytes 6291464 | tf_op jit(solution)/shard_map/ppermute | solution.py:463
  49.6 61.0 %collective-permute-start.13 = (bf16[2048,512]{1,0:T(8,128)(2,1)S(1)}, bf16[2048,512]{1,0:T(8,128)(2,1)S(1)}, u32[]{:S(2)}, u32[]{:S(2)}) collective-permute-start(bf16[2048,512]{1,0:T(8,128)(2,1)S(1)} %copy-done.13), channel_id=1, source_target_pairs={{0,8},{4,12},{8,0},{12,4},{16,24},{20,28},{24,16},{28,20},{1,9},{5... | collective-permute-start | bytes 6291464 | tf_op jit(solution)/shard_map/ppermute | solution.py:463
  51.4 26.6 %collective-permute-start.7 = (bf16[256,2048]{1,0:T(8,128)(2,1)S(1)}, bf16[256,2048]{1,0:T(8,128)(2,1)S(1)}, u32[]{:S(2)}, u32[]{:S(2)}) collective-permute-start(bf16[256,2048]{1,0:T(8,128)(2,1)S(1)} %get-tuple-element.84), channel_id=1, source_target_pairs={{0,16},{4,20},{8,24},{12,28},{16,0},{20,4},{24,8},{28,12},{1,17},{... | collective-permute-start | bytes 3145736 | tf_op jit(solution)/shard_map/ppermute | solution.py:463
  81.7 24.2 %collective-permute-start.8 = (bf16[256,1280]{1,0:T(8,128)(2,1)S(1)}, bf16[256,1280]{1,0:T(8,128)(2,1)S(1)}, u32[]{:S(2)}, u32[]{:S(2)}) collective-permute-start(bf16[256,1280]{1,0:T(8,128)(2,1)S(1)} %up_half.3), channel_id=1, source_target_pairs={{0,16},{4,20},{8,24},{12,28},{16,0},{20,4},{24,8},{28,12},{1,17},{... | collective-permute-start | bytes 1966088 | tf_op jit(solution)/shard_map/ppermute | solution.py:463
  83.2 25.6 %collective-permute-start.11 = (bf16[2048,128]{1,0:T(8,128)(2,1)S(1)}, bf16[2048,128]{1,0:T(8,128)(2,1)S(1)}, u32[]{:S(2)}, u32[]{:S(2)}) collective-permute-start(bf16[2048,128]{1,0:T(8,128)(2,1)S(1)} %get-tuple-element.96.v2), channel_id=1, source_target_pairs={{0,8},{4,12},{8,0},{12,4},{16,24},{20,28},{24,16},{28,20},{1,9},{5... | collective-permute-start | bytes 1572872 | tf_op jit(solution)/shard_map/ppermute | solution.py:463
  87.6 18.2 %collective-permute-start.9 = (bf16[256,768]{1,0:T(8,128)(2,1)S(1)}, bf16[256,768]{1,0:T(8,128)(2,1)S(1)}, u32[]{:S(2)}, u32[]{:S(2)}) collective-permute-start(bf16[256,768]{1,0:T(8,128)(2,1)S(1)} %up_rest.1), channel_id=1, source_target_pairs={{0,16},{4,20},{8,24},{12,28},{16,0},{20,4},{24,8},{28,12},{1,17},{... | collective-permute-start | bytes 1179656 | tf_op jit(solution)/shard_map/ppermute | solution.py:463
  108.9 4.0 %collective-permute-start.12 = (bf16[256,2048]{1,0:T(8,128)(2,1)S(1)}, bf16[256,2048]{1,0:T(8,128)(2,1)S(1)}, u32[]{:S(2)}, u32[]{:S(2)}) collective-permute-start(bf16[256,2048]{1,0:T(8,128)(2,1)S(1)} %gelu.1.a0), channel_id=1, source_target_pairs={{0,4},{4,0},{8,12},{12,8},{16,20},{20,16},{24,28},{28,24},{1,5},{5... | collective-permute-start | bytes 3145736 | tf_op jit(solution)/shard_map/ppermute | solution.py:463
  108.9 14.3 %collective-permute-start.16 = (bf16[2048,128]{1,0:T(8,128)(2,1)S(1)}, bf16[2048,128]{1,0:T(8,128)(2,1)S(1)}, u32[]{:S(2)}, u32[]{:S(2)}) collective-permute-start(bf16[2048,128]{1,0:T(8,128)(2,1)S(1)} %get-tuple-element.106.v2), channel_id=1, source_target_pairs={{0,8},{4,12},{8,0},{12,4},{16,24},{20,28},{24,16},{28,20},{1,9},{5... | collective-permute-start | bytes 1572872 | tf_op jit(solution)/shard_map/ppermute | solution.py:463
  110.7 20.4 %collective-permute-start.19 = (bf16[2048,128]{1,0:T(8,128)(2,1)S(1)}, bf16[2048,128]{1,0:T(8,128)(2,1)S(1)}, u32[]{:S(2)}, u32[]{:S(2)}) collective-permute-start(bf16[2048,128]{1,0:T(8,128)(2,1)S(1)} %get-tuple-element.118.v1), channel_id=1, source_target_pairs={{0,16},{4,20},{8,24},{12,28},{16,0},{20,4},{24,8},{28,12},{1,17},{... | collective-permute-start | bytes 1572872 | tf_op jit(solution)/shard_map/ppermute | solution.py:463
  112.3 29.2 %collective-permute-start.22 = (bf16[2048,128]{1,0:T(8,128)(2,1)S(1)}, bf16[2048,128]{1,0:T(8,128)(2,1)S(1)}, u32[]{:S(2)}, u32[]{:S(2)}) collective-permute-start(bf16[2048,128]{1,0:T(8,128)(2,1)S(1)} %get-tuple-element.132.v1), channel_id=1, source_target_pairs={{0,16},{4,20},{8,24},{12,28},{16,0},{20,4},{24,8},{28,12},{1,17},{... | collective-permute-start | bytes 1572872 | tf_op jit(solution)/shard_map/ppermute | solution.py:463
  116.2 12.2 %collective-permute-start.14 = (bf16[1024,128]{1,0:T(8,128)(2,1)S(1)}, bf16[1024,128]{1,0:T(8,128)(2,1)S(1)}, u32[]{:S(2)}, u32[]{:S(2)}) collective-permute-start(bf16[1024,128]{1,0:T(8,128)(2,1)S(1)} %get-tuple-element.99), channel_id=1, source_target_pairs={{0,1},{1,0},{2,3},{3,2},{4,5},{5,4},{6,7},{7,6},{8,9},{9,8},{10,11... | collective-permute-start | bytes 786440 | tf_op jit(solution)/shard_map/ppermute | solution.py:463
  126.5 11.2 %collective-permute-start.17 = (bf16[1024,128]{1,0:T(8,128)(2,1)S(1)}, bf16[1024,128]{1,0:T(8,128)(2,1)S(1)}, u32[]{:S(2)}, u32[]{:S(2)}) collective-permute-start(bf16[1024,128]{1,0:T(8,128)(2,1)S(1)} %get-tuple-element.109), channel_id=1, source_target_pairs={{0,1},{1,0},{2,3},{3,2},{4,5},{5,4},{6,7},{7,6},{8,9},{9,8},{10,11... | collective-permute-start | bytes 786440 | tf_op jit(solution)/shard_map/ppermute | solution.py:463
  128.4 9.5 %collective-permute-start.15 = (bf16[512,128]{1,0:T(8,128)(2,1)S(1)}, bf16[512,128]{1,0:T(8,128)(2,1)S(1)}, u32[]{:S(2)}, u32[]{:S(2)}) collective-permute-start(bf16[512,128]{1,0:T(8,128)(2,1)S(1)} %get-tuple-element.101), channel_id=1, source_target_pairs={{0,2},{1,3},{2,0},{3,1},{4,6},{5,7},{6,4},{7,5},{8,10},{9,11},{10,... | collective-permute-start | bytes 393224 | tf_op jit(solution)/shard_map/ppermute | solution.py:463
  135.2 11.9 %collective-permute-start.20 = (bf16[1024,128]{1,0:T(8,128)(2,1)S(1)}, bf16[1024,128]{1,0:T(8,128)(2,1)S(1)}, u32[]{:S(2)}, u32[]{:S(2)}) collective-permute-start(bf16[1024,128]{1,0:T(8,128)(2,1)S(1)} %get-tuple-element.121), channel_id=1, source_target_pairs={{0,1},{1,0},{2,3},{3,2},{4,5},{5,4},{6,7},{7,6},{8,9},{9,8},{10,11... | collective-permute-start | bytes 786440 | tf_op jit(solution)/shard_map/ppermute | solution.py:463
  138.0 9.1 %collective-permute-start.18 = (bf16[512,128]{1,0:T(8,128)(2,1)S(1)}, bf16[512,128]{1,0:T(8,128)(2,1)S(1)}, u32[]{:S(2)}, u32[]{:S(2)}) collective-permute-start(bf16[512,128]{1,0:T(8,128)(2,1)S(1)} %get-tuple-element.112), channel_id=1, source_target_pairs={{0,2},{1,3},{2,0},{3,1},{4,6},{5,7},{6,4},{7,5},{8,10},{9,11},{10,... | collective-permute-start | bytes 393224 | tf_op jit(solution)/shard_map/ppermute | solution.py:463
  145.3 8.9 %collective-permute-start.23 = (bf16[1024,128]{1,0:T(8,128)(2,1)S(1)}, bf16[1024,128]{1,0:T(8,128)(2,1)S(1)}, u32[]{:S(2)}, u32[]{:S(2)}) collective-permute-start(bf16[1024,128]{1,0:T(8,128)(2,1)S(1)} %get-tuple-element.135), channel_id=1, source_target_pairs={{0,1},{1,0},{2,3},{3,2},{4,5},{5,4},{6,7},{7,6},{8,9},{9,8},{10,11... | collective-permute-start | bytes 786440 | tf_op jit(solution)/shard_map/ppermute | solution.py:463
  147.1 7.1 %collective-permute-start.21 = (bf16[512,128]{1,0:T(8,128)(2,1)S(1)}, bf16[512,128]{1,0:T(8,128)(2,1)S(1)}, u32[]{:S(2)}, u32[]{:S(2)}) collective-permute-start(bf16[512,128]{1,0:T(8,128)(2,1)S(1)} %get-tuple-element.124), channel_id=1, source_target_pairs={{0,2},{1,3},{2,0},{3,1},{4,6},{5,7},{6,4},{7,5},{8,10},{9,11},{10,... | collective-permute-start | bytes 393224 | tf_op jit(solution)/shard_map/ppermute | solution.py:463
  154.3 6.9 %collective-permute-start.24 = (bf16[512,128]{1,0:T(8,128)(2,1)S(1)}, bf16[512,128]{1,0:T(8,128)(2,1)S(1)}, u32[]{:S(2)}, u32[]{:S(2)}) collective-permute-start(bf16[512,128]{1,0:T(8,128)(2,1)S(1)} %get-tuple-element.138), channel_id=1, source_target_pairs={{0,2},{1,3},{2,0},{3,1},{4,6},{5,7},{6,4},{7,5},{8,10},{9,11},{10,... | collective-permute-start | bytes 393224 | tf_op jit(solution)/shard_map/ppermute | solution.py:463
  (19 other events, 258.9 us)

commit v6 on v5

--- a/solution.py
+++ b/solution.py
@@ -540,7 +540,7 @@
     diagonal.append(over_req(after(forward_y[1], diagonal[0]), mask=X))
     forward_x = [down_x[:, half + k * quarter : half + (k + 1) * quarter] for k in range(2)]
     forward_x = after(forward_x, came)
-    diagonal += [over_req(part, mask=Y) for part in forward_x]
+    diagonal.append(over_req(forward_x[0], mask=Y))
 
     active = gelu_call(keep, came, up_bias)
     active_other = over_req(after(active, diagonal[0]), mask=CORE)
@@ -569,6 +569,8 @@
             quarter,
         )
         rows = after(rows, send)
+        if k == 0:
+            diagonal.append(over_req(after(forward_x[1], send), mask=Y))
         came = over_head(send, mask=1)
         if k:
             came = after(came, far_sums[-1])

time: 165 us -> 165 us (level)
  transfers between devices with their start and end apart: 26 -> 26, of which waited for: 14 -> 15; matrix products, arithmetic and copies ran while one was open for 4% -> 4% of each run, Pallas kernels for 27% -> 27%
where the time goes in v6:
time: 165 us; the launch traced here: 164 us
  waiting for transfers between devices  74.5 us (45%)
  Pallas kernels  46.2 us (28%)
  starting transfers between devices  36.3 us (22%)
  local copies, waits for them, and re-layouts  4.2 us (3%)
  other arithmetic  2.12 us (1%)
    ppermute x26, waiting for transfers between devices, swap(): return lax.ppermute(value, axis, [(i, i ^ mask) for i in range(size)])  74.5 us
    ppermute x26, starting transfers between devices, swap(): return lax.ppermute(value, axis, [(i, i ^ mask) for i in range(size)])  36.3 us
    pallas_call x4, Pallas kernels, down_call(): pl.pallas_call(down_kernel, grid_spec=pltpu.PrefetchScalarGridSpec(num_sc...  14.5 us
    pallas_call x1, Pallas kernels, project_call(): pl.pallas_call(functools.partial(project_kernel, heads), grid=(3 * heads,...  9.45 us
    pallas_call x2, Pallas kernels, up_half_call(): pl.pallas_call(up_half_kernel, grid_spec=pltpu.PrefetchScalarGridSpec(num...  8.23 us
    pallas_call x1, Pallas kernels, norm_call(): pl.pallas_call(functools.partial(norm_kernel, count, split), grid_spec=pl...  4.16 us
    pallas_call x1, Pallas kernels, up_rest_call(): pl.pallas_call(up_rest_kernel, grid_spec=pltpu.PrefetchScalarGridSpec(num...  3.86 us
    pallas_call x1, Pallas kernels, attend_call(): pl.pallas_call(functools.partial(attend_kernel, local // HD), grid_spec=p...  3.81 us
  transfers between devices with their start and end apart: 26, of which 15 were waited for; matrix products, arithmetic and copies ran while one was open for 4% of the time, Pallas kernels for 27%

profile of v6, /device:TPU:0, one launch (start us, length us, event | category | flops | bytes accessed | tf_op | source)
XLA Modules:
  0.0 164.3 jit_solution(3544820850379739759)
XLA Ops:
  0.7 3.0 %collective-permute-start.4 = (bf16[512,2048]{1,0:T(8,128)(2,1)}, bf16[512,2048]{1,0:T(8,128)(2,1)S(1)}, u32[]{:S(2)}, u32[]{:S(2)}) collective-permute-start(bf16[512,2048]{1,0:T(8,128)(2,1)} %w0.5), channel_id=1, source_target_pairs={{0,8},{4,12},{8,0},{12,4},{16,24},{20,28},{24,16},{28,20},{1,9},{5... | collective-permute-start | bytes 6291464 | tf_op jit(solution)/shard_map/ppermute | solution.py:463
  3.7 2.6 %collective-permute-start = (bf16[256,1024]{1,0:T(8,128)(2,1)}, bf16[256,1024]{1,0:T(8,128)(2,1)}, u32[]{:S(2)}, u32[]{:S(2)}) collective-permute-start(bf16[256,1024]{1,0:T(8,128)(2,1)} %hidden_ref.1), channel_id=1, source_target_pairs={{0,2},{1,3},{2,0},{3,1},{4,6},{5,7},{6,4},{7,5},{8,10},{9,11},{10,... | collective-permute-start | bytes 1572872 | tf_op jit(solution)/shard_map/ppermute | solution.py:463
  9.4 2.8 %fusion.13 = (bf16[2048,128]{1,0:T(8,128)(2,1)S(1)}, bf16[2048,128]{1,0:T(8,128)(2,1)}, bf16[2048,128]{1,0:T(8,128)(2,1)}, bf16[2048,128]{1,0:T(8,128)(2,1)}) fusion(bf16[2048,512]{1,0:T(8,128)(2,1)} %param.20), kind=kLoop, calls=%fused_computation.31 | loop fusion | bytes 4194304 | tf_op jit(solution)/shard_map/slice | solution.py:502
  12.1 18.4 %collective-permute-done.refs_1_ = bf16[256,1024]{1,0:T(8,128)(2,1)} collective-permute-done((bf16[256,1024]{1,0:T(8,128)(2,1)}, bf16[256,1024]{1,0:T(8,128)(2,1)}, u32[]{:S(2)}, u32[]{:S(2)}) %collective-permute-start) | collective-permute-done | bytes 524320 | tf_op jit(solution)/shard_map/ppermute | solution.py:463
  32.6 11.8 %collective-permute-done.1.refs_2_ = bf16[256,1024]{1,0:T(8,128)(2,1)} collective-permute-done((bf16[256,1024]{1,0:T(8,128)(2,1)}, bf16[256,1024]{1,0:T(8,128)(2,1)}, u32[]{:S(2)}, u32[]{:S(2)}) %collective-permute-start.1) | collective-permute-done | bytes 524320 | tf_op jit(solution)/shard_map/ppermute | solution.py:463
  44.4 4.2 %layer_norm.1 = (bf16[256,4096]{1,0:T(8,128)(2,1)S(1)}, bf16[256,2048]{1,0:T(8,128)(2,1)S(1)}) custom-call(s32[5]{0:T(128)S(1)} %pad_add_fusion.1.order_ref, bf16[256,2048]{1,0:T(8,128)(2,1)S(1)} %pad_maximum_fusion.refs_0_, bf16[256,1024]{1,0:T(8,128)(2,1)} %collective-permute-done.refs_1_, bf16[256,1024]{1,0:T(8,128)(2,1)} %collective-permute-done.1.refs_2_, ...), custom_call_target="tpu_custom_call" | custom-call | flops 1024 | bytes 1024 | tf_op jit(solution)/shard_map/layer_norm/pallas_call | solution.py:60
  53.5 3.2 %collective-permute-done.3.v2 = bf16[2048,512]{1,0:T(8,128)(2,1)} collective-permute-done((bf16[2048,512]{1,0:T(8,128)(2,1)}, bf16[2048,512]{1,0:T(8,128)(2,1)}, u32[]{:S(2)}, u32[]{:S(2)}) %collective-permute-start.3) | collective-permute-done | bytes 2097184 | tf_op jit(solution)/shard_map/ppermute | solution.py:463
  58.0 9.5 %projections.1 = (bf16[256,512]{1,0:T(8,128)(2,1)S(1)}, bf16[256,512]{1,0:T(8,128)(2,1)}, bf16[256,512]{1,0:T(8,128)(2,1)}) custom-call(bf16[256,4096]{1,0:T(8,128)(2,1)S(1)} %get-tuple-element.82.x_ref.rows_ref, bf16[3,4096,512]{2,1,0:T(8,128)(2,1)} %bitcast.15, f32[256,128]{1,0:T(8,128)S(1)} %get-tuple-element.153.a_ref, ...), custom_call_target="tpu_custom_call" | custom-call | flops 1024 | bytes 1024 | tf_op jit(solution)/shard_map/projections/pallas_call | solution.py:114
  67.4 4.6 %up_half.2.keep_ref = f32[256,2048]{1,0:T(8,128)S(1)} custom-call(s32[4]{0:T(128)S(1)} %get-tuple-element.155.spots_ref, bf16[256,4096]{1,0:T(8,128)(2,1)S(1)} %get-tuple-element.82.x_ref.rows_ref, bf16[512,2048]{1,0:T(8,128)(2,1)S(1)} %copy-done.1, bf16[512,2048]{1,0:T(8,128)(2,1)S(1)} %collective-permute-done.4.w1, ...), custom_call_target="tpu_custom_call" | custom-call | flops 1024 | bytes 1024 | tf_op jit(solution)/shard_map/up_half/pallas_call | solution.py:241
  72.0 6.0 %collective-permute-done.7.rows_ref = bf16[256,2048]{1,0:T(8,128)(2,1)S(1)} collective-permute-done((bf16[256,2048]{1,0:T(8,128)(2,1)S(1)}, bf16[256,2048]{1,0:T(8,128)(2,1)S(1)}, u32[]{:S(2)}, u32[]{:S(2)}) %collective-permute-start.7) | collective-permute-done | bytes 1048608 | tf_op jit(solution)/shard_map/ppermute | solution.py:463
  78.0 3.6 %up_half.3 = bf16[256,1280]{1,0:T(8,128)(2,1)S(1)} custom-call(s32[4]{0:T(128)S(1)} %get-tuple-element.154.spots_ref, bf16[256,2048]{1,0:T(8,128)(2,1)S(1)} %collective-permute-done.7.rows_ref, bf16[512,2048]{1,0:T(8,128)(2,1)S(1)} %copy-done.1, bf16[512,2048]{1,0:T(8,128)(2,1)S(1)} %collective-permute-done.4.w1, ...), custom_call_target="tpu_custom_call" | custom-call | flops 1024 | bytes 1024 | tf_op jit(solution)/shard_map/up_half/pallas_call | solution.py:241
  83.8 3.9 %up_rest.1 = bf16[256,768]{1,0:T(8,128)(2,1)S(1)} custom-call(s32[4]{0:T(128)S(1)} %get-tuple-element.154.spots_ref, bf16[256,2048]{1,0:T(8,128)(2,1)S(1)} %collective-permute-done.7.rows_ref, bf16[512,2048]{1,0:T(8,128)(2,1)S(1)} %copy-done.1, bf16[512,2048]{1,0:T(8,128)(2,1)S(1)} %collective-permute-done.4.w1, ...), custom_call_target="tpu_custom_call" | custom-call | flops 1024 | bytes 1024 | tf_op jit(solution)/shard_map/up_rest/pallas_call | solution.py:276
  88.2 3.8 %attention.1.c0 = bf16[256,512]{1,0:T(8,128)(2,1)S(1)} custom-call(s32[2]{0:T(128)S(1)} %copy-done.12, bf16[256,512]{1,0:T(8,128)(2,1)S(1)} %get-tuple-element.88.q_ref, bf16[256,512]{1,0:T(8,128)(2,1)S(1)} %copy-done.8, bf16[256,512]{1,0:T(8,128)(2,1)S(1)} %copy-done.9, bf16[2,1536,512]{2,1,0:T(8,128)(2,1)S(1)} %copy-done.2, bf16[2,1536,512]{2,1,0:T(8,128)(2,1)S(1)} %copy-done.3), custom_call_target="tpu_custom_call" | custom-call | flops 1024 | bytes 1024 | tf_op jit(solution)/shard_map/attention/pallas_call | solution.py:168
  93.7 12.2 %collective-permute-done.9.refs_1_ = bf16[256,768]{1,0:T(8,128)(2,1)S(1)} collective-permute-done((bf16[256,768]{1,0:T(8,128)(2,1)S(1)}, bf16[256,768]{1,0:T(8,128)(2,1)S(1)}, u32[]{:S(2)}, u32[]{:S(2)}) %collective-permute-start.9) | collective-permute-done | bytes 393248 | tf_op jit(solution)/shard_map/ppermute | solution.py:463
  112.4 3.3 %down_and_output.4 = (f32[512,128]{1,0:T(8,128)S(1)}, f32[512,128]{1,0:T(8,128)S(1)}, bf16[1024,128]{1,0:T(8,128)(2,1)S(1)}) custom-call(s32[8]{0:T(128)S(1)} %pad_add_fusion.place_ref, bf16[256,2048]{1,0:T(8,128)(2,1)S(1)} %gelu.1.a0, bf16[256,2048]{1,0:T(8,128)(2,1)S(1)} %collective-permute-done.12.a1, bf16[256,512]{1,0:T(8,128)(2,1)S(1)} %attention.1.c0, ...), custom_call_target="tpu_custom_call" | custom-call | flops 1024 | bytes 1024 | tf_op jit(solution)/shard_map/down_and_output/pallas_call | solution.py:378
  118.3 5.0 %collective-permute-done.16.v3 = bf16[2048,128]{1,0:T(8,128)(2,1)S(1)} collective-permute-done((bf16[2048,128]{1,0:T(8,128)(2,1)S(1)}, bf16[2048,128]{1,0:T(8,128)(2,1)S(1)}, u32[]{:S(2)}, u32[]{:S(2)}) %collective-permute-start.16) | collective-permute-done | bytes 524320 | tf_op jit(solution)/shard_map/ppermute | solution.py:463
  123.2 3.3 %down_and_output.5 = (f32[512,128]{1,0:T(8,128)S(1)}, f32[512,128]{1,0:T(8,128)S(1)}, bf16[1024,128]{1,0:T(8,128)(2,1)S(1)}) custom-call(s32[8]{0:T(128)S(1)} %pad_add_fusion.place_ref, bf16[256,2048]{1,0:T(8,128)(2,1)S(1)} %gelu.1.a0, bf16[256,2048]{1,0:T(8,128)(2,1)S(1)} %collective-permute-done.12.a1, bf16[256,512]{1,0:T(8,128)(2,1)S(1)} %attention.1.c0, ...), custom_call_target="tpu_custom_call" | custom-call | flops 1024 | bytes 1024 | tf_op jit(solution)/shard_map/down_and_output/pallas_call | solution.py:378
  128.4 2.6 %collective-permute-start.15 = (bf16[512,128]{1,0:T(8,128)(2,1)S(1)}, bf16[512,128]{1,0:T(8,128)(2,1)S(1)}, u32[]{:S(2)}, u32[]{:S(2)}) collective-permute-start(bf16[512,128]{1,0:T(8,128)(2,1)S(1)} %get-tuple-element.102), channel_id=1, source_target_pairs={{0,2},{1,3},{2,0},{3,1},{4,6},{5,7},{6,4},{7,5},{8,10},{9,11},{10,... | collective-permute-start | bytes 393224 | tf_op jit(solution)/shard_map/ppermute | solution.py:463
  131.1 4.0 %down_and_output.6 = (f32[512,128]{1,0:T(8,128)S(1)}, f32[512,128]{1,0:T(8,128)S(1)}, bf16[1024,128]{1,0:T(8,128)(2,1)S(1)}) custom-call(s32[8]{0:T(128)S(1)} %pad_add_fusion.place_ref, bf16[256,2048]{1,0:T(8,128)(2,1)S(1)} %gelu.1.a0, bf16[256,2048]{1,0:T(8,128)(2,1)S(1)} %collective-permute-done.12.a1, bf16[256,512]{1,0:T(8,128)(2,1)S(1)} %attention.1.c0, ...), custom_call_target="tpu_custom_call" | custom-call | flops 1024 | bytes 1024 | tf_op jit(solution)/shard_map/down_and_output/pallas_call | solution.py:378
  138.0 3.4 %collective-permute-start.18 = (bf16[512,128]{1,0:T(8,128)(2,1)S(1)}, bf16[512,128]{1,0:T(8,128)(2,1)S(1)}, u32[]{:S(2)}, u32[]{:S(2)}) collective-permute-start(bf16[512,128]{1,0:T(8,128)(2,1)S(1)} %get-tuple-element.113), channel_id=1, source_target_pairs={{0,2},{1,3},{2,0},{3,1},{4,6},{5,7},{6,4},{7,5},{8,10},{9,11},{10,... | collective-permute-start | bytes 393224 | tf_op jit(solution)/shard_map/ppermute | solution.py:463
  141.4 3.9 %down_and_output.7 = (f32[512,128]{1,0:T(8,128)S(1)}, f32[512,128]{1,0:T(8,128)S(1)}, bf16[1024,128]{1,0:T(8,128)(2,1)S(1)}) custom-call(s32[8]{0:T(128)S(1)} %pad_add_fusion.place_ref, bf16[256,2048]{1,0:T(8,128)(2,1)S(1)} %gelu.1.a0, bf16[256,2048]{1,0:T(8,128)(2,1)S(1)} %collective-permute-done.12.a1, bf16[256,512]{1,0:T(8,128)(2,1)S(1)} %attention.1.c0, ...), custom_call_target="tpu_custom_call" | custom-call | flops 1024 | bytes 1024 | tf_op jit(solution)/shard_map/down_and_output/pallas_call | solution.py:378
  149.1 4.8 %collective-permute-done.21.refs_5_ = bf16[512,128]{1,0:T(8,128)(2,1)S(1)} collective-permute-done((bf16[512,128]{1,0:T(8,128)(2,1)S(1)}, bf16[512,128]{1,0:T(8,128)(2,1)S(1)}, u32[]{:S(2)}, u32[]{:S(2)}) %collective-permute-start.21) | collective-permute-done | bytes 131104 | tf_op jit(solution)/shard_map/ppermute | solution.py:463
  154.3 2.8 %collective-permute-start.24 = (bf16[512,128]{1,0:T(8,128)(2,1)S(1)}, bf16[512,128]{1,0:T(8,128)(2,1)S(1)}, u32[]{:S(2)}, u32[]{:S(2)}) collective-permute-start(bf16[512,128]{1,0:T(8,128)(2,1)S(1)} %get-tuple-element.140), channel_id=1, source_target_pairs={{0,2},{1,3},{2,0},{3,1},{4,6},{5,7},{6,4},{7,5},{8,10},{9,11},{10,... | collective-permute-start | bytes 393224 | tf_op jit(solution)/shard_map/ppermute | solution.py:463
  157.1 4.1 %collective-permute-done.24.refs_7_ = bf16[512,128]{1,0:T(8,128)(2,1)S(1)} collective-permute-done((bf16[512,128]{1,0:T(8,128)(2,1)S(1)}, bf16[512,128]{1,0:T(8,128)(2,1)S(1)}, u32[]{:S(2)}, u32[]{:S(2)}) %collective-permute-start.24) | collective-permute-done | bytes 131104 | tf_op jit(solution)/shard_map/ppermute | solution.py:463
  (93 shorter events, 36.6 us)
Async XLA Ops:
  0.7 48.8 %collective-permute-start.4 = (bf16[512,2048]{1,0:T(8,128)(2,1)}, bf16[512,2048]{1,0:T(8,128)(2,1)S(1)}, u32[]{:S(2)}, u32[]{:S(2)}) collective-permute-start(bf16[512,2048]{1,0:T(8,128)(2,1)} %w0.5), channel_id=1, source_target_pairs={{0,8},{4,12},{8,0},{12,4},{16,24},{20,28},{24,16},{28,20},{1,9},{5... | collective-permute-start | bytes 6291464 | tf_op jit(solution)/shard_map/ppermute | solution.py:463
  3.7 45.8 %collective-permute-start.5 = (bf16[512,2048]{1,0:T(8,128)(2,1)}, bf16[512,2048]{1,0:T(8,128)(2,1)}, u32[]{:S(2)}, u32[]{:S(2)}) collective-permute-start(bf16[512,2048]{1,0:T(8,128)(2,1)} %w0.5), channel_id=1, source_target_pairs={{0,4},{4,0},{8,12},{12,8},{16,20},{20,16},{24,28},{28,24},{1,5},{5... | collective-permute-start | bytes 6291464 | tf_op jit(solution)/shard_map/ppermute | solution.py:463
  3.7 26.9 %collective-permute-start = (bf16[256,1024]{1,0:T(8,128)(2,1)}, bf16[256,1024]{1,0:T(8,128)(2,1)}, u32[]{:S(2)}, u32[]{:S(2)}) collective-permute-start(bf16[256,1024]{1,0:T(8,128)(2,1)} %hidden_ref.1), channel_id=1, source_target_pairs={{0,2},{1,3},{2,0},{3,1},{4,6},{5,7},{6,4},{7,5},{8,10},{9,11},{10,... | collective-permute-start | bytes 1572872 | tf_op jit(solution)/shard_map/ppermute | solution.py:463
  6.3 25.0 %collective-permute-start.2 = (bf16[256,1024]{1,0:T(8,128)(2,1)}, bf16[256,1024]{1,0:T(8,128)(2,1)}, u32[]{:S(2)}, u32[]{:S(2)}) collective-permute-start(bf16[256,1024]{1,0:T(8,128)(2,1)} %hidden_ref.1), channel_id=1, source_target_pairs={{0,1},{1,0},{2,3},{3,2},{4,5},{5,4},{6,7},{7,6},{8,9},{9,8},{10,11... | collective-permute-start | bytes 1572872 | tf_op jit(solution)/shard_map/ppermute | solution.py:463
  7.8 48.8 %collective-permute-start.3 = (bf16[2048,512]{1,0:T(8,128)(2,1)}, bf16[2048,512]{1,0:T(8,128)(2,1)}, u32[]{:S(2)}, u32[]{:S(2)}) collective-permute-start(bf16[2048,512]{1,0:T(8,128)(2,1)} %param.20), channel_id=1, source_target_pairs={{0,16},{4,20},{8,24},{12,28},{16,0},{20,4},{24,8},{28,12},{1,17},{... | collective-permute-start | bytes 6291464 | tf_op jit(solution)/shard_map/ppermute | solution.py:463
  30.6 13.8 %collective-permute-start.1 = (bf16[256,1024]{1,0:T(8,128)(2,1)}, bf16[256,1024]{1,0:T(8,128)(2,1)}, u32[]{:S(2)}, u32[]{:S(2)}) collective-permute-start(bf16[256,1024]{1,0:T(8,128)(2,1)} %collective-permute-done.refs_1_), channel_id=1, source_target_pairs={{0,1},{1,0},{2,3},{3,2},{4,5},{5,4},{6,7},{7,6},{8,9},{9,8},{10,11... | collective-permute-start | bytes 1572872 | tf_op jit(solution)/shard_map/ppermute | solution.py:463
  49.5 17.9 %collective-permute-start.6 = (bf16[512,2048]{1,0:T(8,128)(2,1)S(1)}, bf16[512,2048]{1,0:T(8,128)(2,1)S(1)}, u32[]{:S(2)}, u32[]{:S(2)}) collective-permute-start(bf16[512,2048]{1,0:T(8,128)(2,1)S(1)} %collective-permute-done.4.w1), channel_id=1, source_target_pairs={{0,4},{4,0},{8,12},{12,8},{16,20},{20,16},{24,28},{28,24},{1,5},{5... | collective-permute-start | bytes 6291464 | tf_op jit(solution)/shard_map/ppermute | solution.py:463
  49.6 61.0 %collective-permute-start.13 = (bf16[2048,512]{1,0:T(8,128)(2,1)S(1)}, bf16[2048,512]{1,0:T(8,128)(2,1)S(1)}, u32[]{:S(2)}, u32[]{:S(2)}) collective-permute-start(bf16[2048,512]{1,0:T(8,128)(2,1)S(1)} %copy-done.13), channel_id=1, source_target_pairs={{0,8},{4,12},{8,0},{12,4},{16,24},{20,28},{24,16},{28,20},{1,9},{5... | collective-permute-start | bytes 6291464 | tf_op jit(solution)/shard_map/ppermute | solution.py:463
  51.4 26.6 %collective-permute-start.7 = (bf16[256,2048]{1,0:T(8,128)(2,1)S(1)}, bf16[256,2048]{1,0:T(8,128)(2,1)S(1)}, u32[]{:S(2)}, u32[]{:S(2)}) collective-permute-start(bf16[256,2048]{1,0:T(8,128)(2,1)S(1)} %get-tuple-element.85), channel_id=1, source_target_pairs={{0,16},{4,20},{8,24},{12,28},{16,0},{20,4},{24,8},{28,12},{1,17},{... | collective-permute-start | bytes 3145736 | tf_op jit(solution)/shard_map/ppermute | solution.py:463
  81.7 24.2 %collective-permute-start.8 = (bf16[256,1280]{1,0:T(8,128)(2,1)S(1)}, bf16[256,1280]{1,0:T(8,128)(2,1)S(1)}, u32[]{:S(2)}, u32[]{:S(2)}) collective-permute-start(bf16[256,1280]{1,0:T(8,128)(2,1)S(1)} %up_half.3), channel_id=1, source_target_pairs={{0,16},{4,20},{8,24},{12,28},{16,0},{20,4},{24,8},{28,12},{1,17},{... | collective-permute-start | bytes 1966088 | tf_op jit(solution)/shard_map/ppermute | solution.py:463
  83.2 25.6 %collective-permute-start.11 = (bf16[2048,128]{1,0:T(8,128)(2,1)S(1)}, bf16[2048,128]{1,0:T(8,128)(2,1)S(1)}, u32[]{:S(2)}, u32[]{:S(2)}) collective-permute-start(bf16[2048,128]{1,0:T(8,128)(2,1)S(1)} %get-tuple-element.97.v2), channel_id=1, source_target_pairs={{0,8},{4,12},{8,0},{12,4},{16,24},{20,28},{24,16},{28,20},{1,9},{5... | collective-permute-start | bytes 1572872 | tf_op jit(solution)/shard_map/ppermute | solution.py:463
  87.6 18.2 %collective-permute-start.9 = (bf16[256,768]{1,0:T(8,128)(2,1)S(1)}, bf16[256,768]{1,0:T(8,128)(2,1)S(1)}, u32[]{:S(2)}, u32[]{:S(2)}) collective-permute-start(bf16[256,768]{1,0:T(8,128)(2,1)S(1)} %up_rest.1), channel_id=1, source_target_pairs={{0,16},{4,20},{8,24},{12,28},{16,0},{20,4},{24,8},{28,12},{1,17},{... | collective-permute-start | bytes 1179656 | tf_op jit(solution)/shard_map/ppermute | solution.py:463
  108.9 3.5 %collective-permute-start.12 = (bf16[256,2048]{1,0:T(8,128)(2,1)S(1)}, bf16[256,2048]{1,0:T(8,128)(2,1)S(1)}, u32[]{:S(2)}, u32[]{:S(2)}) collective-permute-start(bf16[256,2048]{1,0:T(8,128)(2,1)S(1)} %gelu.1.a0), channel_id=1, source_target_pairs={{0,4},{4,0},{8,12},{12,8},{16,20},{20,16},{24,28},{28,24},{1,5},{5... | collective-permute-start | bytes 3145736 | tf_op jit(solution)/shard_map/ppermute | solution.py:463
  108.9 14.3 %collective-permute-start.16 = (bf16[2048,128]{1,0:T(8,128)(2,1)S(1)}, bf16[2048,128]{1,0:T(8,128)(2,1)S(1)}, u32[]{:S(2)}, u32[]{:S(2)}) collective-permute-start(bf16[2048,128]{1,0:T(8,128)(2,1)S(1)} %get-tuple-element.107.v2), channel_id=1, source_target_pairs={{0,8},{4,12},{8,0},{12,4},{16,24},{20,28},{24,16},{28,20},{1,9},{5... | collective-permute-start | bytes 1572872 | tf_op jit(solution)/shard_map/ppermute | solution.py:463
  110.7 20.4 %collective-permute-start.19 = (bf16[2048,128]{1,0:T(8,128)(2,1)S(1)}, bf16[2048,128]{1,0:T(8,128)(2,1)S(1)}, u32[]{:S(2)}, u32[]{:S(2)}) collective-permute-start(bf16[2048,128]{1,0:T(8,128)(2,1)S(1)} %get-tuple-element.119.v1), channel_id=1, source_target_pairs={{0,16},{4,20},{8,24},{12,28},{16,0},{20,4},{24,8},{28,12},{1,17},{... | collective-permute-start | bytes 1572872 | tf_op jit(solution)/shard_map/ppermute | solution.py:463
  115.7 25.7 %collective-permute-start.22 = (bf16[2048,128]{1,0:T(8,128)(2,1)S(1)}, bf16[2048,128]{1,0:T(8,128)(2,1)S(1)}, u32[]{:S(2)}, u32[]{:S(2)}) collective-permute-start(bf16[2048,128]{1,0:T(8,128)(2,1)S(1)} %get-tuple-element.134.v1), channel_id=1, source_target_pairs={{0,16},{4,20},{8,24},{12,28},{16,0},{20,4},{24,8},{28,12},{1,17},{... | collective-permute-start | bytes 1572872 | tf_op jit(solution)/shard_map/ppermute | solution.py:463
  116.7 11.7 %collective-permute-start.14 = (bf16[1024,128]{1,0:T(8,128)(2,1)S(1)}, bf16[1024,128]{1,0:T(8,128)(2,1)S(1)}, u32[]{:S(2)}, u32[]{:S(2)}) collective-permute-start(bf16[1024,128]{1,0:T(8,128)(2,1)S(1)} %get-tuple-element.100), channel_id=1, source_target_pairs={{0,1},{1,0},{2,3},{3,2},{4,5},{5,4},{6,7},{7,6},{8,9},{9,8},{10,11... | collective-permute-start | bytes 786440 | tf_op jit(solution)/shard_map/ppermute | solution.py:463
  126.5 11.2 %collective-permute-start.17 = (bf16[1024,128]{1,0:T(8,128)(2,1)S(1)}, bf16[1024,128]{1,0:T(8,128)(2,1)S(1)}, u32[]{:S(2)}, u32[]{:S(2)}) collective-permute-start(bf16[1024,128]{1,0:T(8,128)(2,1)S(1)} %get-tuple-element.110), channel_id=1, source_target_pairs={{0,1},{1,0},{2,3},{3,2},{4,5},{5,4},{6,7},{7,6},{8,9},{9,8},{10,11... | collective-permute-start | bytes 786440 | tf_op jit(solution)/shard_map/ppermute | solution.py:463
  128.4 9.5 %collective-permute-start.15 = (bf16[512,128]{1,0:T(8,128)(2,1)S(1)}, bf16[512,128]{1,0:T(8,128)(2,1)S(1)}, u32[]{:S(2)}, u32[]{:S(2)}) collective-permute-start(bf16[512,128]{1,0:T(8,128)(2,1)S(1)} %get-tuple-element.102), channel_id=1, source_target_pairs={{0,2},{1,3},{2,0},{3,1},{4,6},{5,7},{6,4},{7,5},{8,10},{9,11},{10,... | collective-permute-start | bytes 393224 | tf_op jit(solution)/shard_map/ppermute | solution.py:463
  135.2 11.9 %collective-permute-start.20 = (bf16[1024,128]{1,0:T(8,128)(2,1)S(1)}, bf16[1024,128]{1,0:T(8,128)(2,1)S(1)}, u32[]{:S(2)}, u32[]{:S(2)}) collective-permute-start(bf16[1024,128]{1,0:T(8,128)(2,1)S(1)} %get-tuple-element.122), channel_id=1, source_target_pairs={{0,1},{1,0},{2,3},{3,2},{4,5},{5,4},{6,7},{7,6},{8,9},{9,8},{10,11... | collective-permute-start | bytes 786440 | tf_op jit(solution)/shard_map/ppermute | solution.py:463
  138.0 9.1 %collective-permute-start.18 = (bf16[512,128]{1,0:T(8,128)(2,1)S(1)}, bf16[512,128]{1,0:T(8,128)(2,1)S(1)}, u32[]{:S(2)}, u32[]{:S(2)}) collective-permute-start(bf16[512,128]{1,0:T(8,128)(2,1)S(1)} %get-tuple-element.113), channel_id=1, source_target_pairs={{0,2},{1,3},{2,0},{3,1},{4,6},{5,7},{6,4},{7,5},{8,10},{9,11},{10,... | collective-permute-start | bytes 393224 | tf_op jit(solution)/shard_map/ppermute | solution.py:463
  145.3 8.9 %collective-permute-start.23 = (bf16[1024,128]{1,0:T(8,128)(2,1)S(1)}, bf16[1024,128]{1,0:T(8,128)(2,1)S(1)}, u32[]{:S(2)}, u32[]{:S(2)}) collective-permute-start(bf16[1024,128]{1,0:T(8,128)(2,1)S(1)} %get-tuple-element.137), channel_id=1, source_target_pairs={{0,1},{1,0},{2,3},{3,2},{4,5},{5,4},{6,7},{7,6},{8,9},{9,8},{10,11... | collective-permute-start | bytes 786440 | tf_op jit(solution)/shard_map/ppermute | solution.py:463
  147.1 6.8 %collective-permute-start.21 = (bf16[512,128]{1,0:T(8,128)(2,1)S(1)}, bf16[512,128]{1,0:T(8,128)(2,1)S(1)}, u32[]{:S(2)}, u32[]{:S(2)}) collective-permute-start(bf16[512,128]{1,0:T(8,128)(2,1)S(1)} %get-tuple-element.125), channel_id=1, source_target_pairs={{0,2},{1,3},{2,0},{3,1},{4,6},{5,7},{6,4},{7,5},{8,10},{9,11},{10,... | collective-permute-start | bytes 393224 | tf_op jit(solution)/shard_map/ppermute | solution.py:463
  154.3 6.9 %collective-permute-start.24 = (bf16[512,128]{1,0:T(8,128)(2,1)S(1)}, bf16[512,128]{1,0:T(8,128)(2,1)S(1)}, u32[]{:S(2)}, u32[]{:S(2)}) collective-permute-start(bf16[512,128]{1,0:T(8,128)(2,1)S(1)} %get-tuple-element.140), channel_id=1, source_target_pairs={{0,2},{1,3},{2,0},{3,1},{4,6},{5,7},{6,4},{7,5},{8,10},{9,11},{10,... | collective-permute-start | bytes 393224 | tf_op jit(solution)/shard_map/ppermute | solution.py:463
  (19 other events, 258.9 us)
